TPU v7x, 32 devices: a whole 2x2x4 slice. The times are simulated.
32 devices in a mesh: dp: 4 (over z), seq: 4 (over y, x), mp: 2 (over core).
Axes of the slice: x: 2, y: 2, z: 4, core: 2. Of those that a mesh axis runs over, the one named last changes fastest.
Arguments:
- inputs: bfloat16 [32, 2048, 1024], P('dp', ('seq', 'mp')), may hold values from -6 to 6
- gain_one: bfloat16 [1024], replicated, may hold values from 0.5 to 1.5
- w_query: bfloat16 [1024, 1024], P(None, 'mp'), may hold values from -0.1875 to 0.1875
- w_tied: bfloat16 [1024, 256], P(None, 'mp'), may hold values from -0.1875 to 0.1875
- w_rope: bfloat16 [1024, 32], replicated, may hold values from -0.1875 to 0.1875
- w_out: bfloat16 [1024, 1024], P('mp'), may hold values from -2 to 2
- gain_two: bfloat16 [1024], replicated, may hold values from 0.5 to 1.5
- w_gate: bfloat16 [1024, 2816], P(None, 'mp'), may hold values from -0.1875 to 0.1875
- w_up: bfloat16 [1024, 2816], P(None, 'mp'), may hold values from -0.1875 to 0.1875
- w_down: bfloat16 [2816, 1024], P('mp'), may hold values from -0.109375 to 0.109375
- doc_starts: int32 [32, 8], P('dp'), may hold values from 0 to 2048, as said below
- out_grad: bfloat16 [32, 2048, 1024], P('dp', ('seq', 'mp')), may hold values from -6 to 6
Outputs:
- outputs: bfloat16 [32, 2048, 1024], P('dp', ('seq', 'mp'))
- grad_inputs: float32 [32, 2048, 1024], P('dp', ('seq', 'mp'))
- grad_gain_one: float32 [1024], P(('dp', 'seq', 'mp'))
- grad_w_query: float32 [1024, 1024], P(('dp', 'seq'), 'mp')
- grad_w_tied: float32 [1024, 256], P(('dp', 'seq'), 'mp')
- grad_w_rope: float32 [1024, 32], P(('dp', 'seq', 'mp'))
- grad_w_out: float32 [1024, 1024], P('mp', ('dp', 'seq'))
- grad_gain_two: float32 [1024], P(('dp', 'seq', 'mp'))
- grad_w_gate: float32 [1024, 2816], P(('dp', 'seq'), 'mp')
- grad_w_up: float32 [1024, 2816], P(('dp', 'seq'), 'mp')
- grad_w_down: float32 [2816, 1024], P('mp', ('dp', 'seq'))
Inputs may be any that keep to these rules, and one draw needn't show every extreme that they name: `doc_starts`: row b lists where the documents of packed sequence b begin: the first entry is 0, entries never fall, and an entry equal to 2048 marks no document.
All inputs are finite; a program needn't handle non-finite values.
Results may differ from a plain program's by a relative error of at most 0.018.
Values may be sent and summed in bfloat16 or wider, within the bound.
A program may use at most 384 MiB of HBM per device.

v0:
```python
import jax
import jax.numpy as jnp
from jax import lax
from jax.sharding import PartitionSpec as P

HD = 64
RD = 32


epsilon = 1e-05
rope_base = 10000.0
masked_value = -1e30


def rope_tables(offset, count, rope_width):
    position = (offset + jnp.arange(count, dtype=jnp.int32)).astype(jnp.float32)
    frequency = rope_base ** (-jnp.arange(rope_width // 2, dtype=jnp.float32) * 2.0 / rope_width)
    angles = position[:, None] * frequency[None, :]
    return (jnp.cos(angles), jnp.sin(angles))


def rotate(values, cosine, sine_table):
    half_width = values.shape[-1] // 2
    first_half = values[..., :half_width]
    second_half = values[..., half_width:]
    return jnp.concatenate(
        [
            first_half * cosine - second_half * sine_table,
            second_half * cosine + first_half * sine_table,
        ],
        axis=-1,
    )


def rotate_back(grads, cosine, sine_table):
    half_width = grads.shape[-1] // 2
    first_half = grads[..., :half_width]
    second_half = grads[..., half_width:]
    return jnp.concatenate(
        [
            first_half * cosine + second_half * sine_table,
            second_half * cosine - first_half * sine_table,
        ],
        axis=-1,
    )


def contract_rows(left, right):
    return lax.dot_general(
        left, right, (((0,), (0,)), ((), ())), preferred_element_type=jnp.float32
    )


def times_transposed(left, right):
    return lax.dot_general(
        left, right, (((1,), (1,)), ((), ())), preferred_element_type=jnp.float32
    )


def norm_back(grad_normed, values, inverse, gain):
    scaled = grad_normed * gain
    grad_gain = jnp.sum(grad_normed * values * inverse, axis=(0, 1))
    grad_values = inverse * scaled - values * inverse**3 * jnp.mean(
        scaled * values, axis=-1, keepdims=True
    )
    return (grad_values, grad_gain)


def attend(operands):
    queries, key_full, values, allowed = operands
    scores = jnp.einsum(
        "qghd,kgd->ghqk", queries, key_full, preferred_element_type=jnp.float32
    ) * HD ** (-0.5)
    masked = jnp.where(allowed[None, None], scores, masked_value)
    row_max = jnp.max(masked, axis=-1, keepdims=True)
    weights = jnp.exp(masked - row_max)
    row_total = jnp.sum(weights, axis=-1, keepdims=True)
    attention_probs = (weights / row_total).astype(jnp.bfloat16)
    combined = jnp.einsum(
        "ghqk,kgd->qghd", attention_probs, values, preferred_element_type=jnp.float32
    )
    return (combined.astype(jnp.bfloat16), row_max + jnp.log(row_total))


def attend_back(operands):
    queries, key_full, values, allowed, log_total, grad_heads = operands
    score_scale = HD ** (-0.5)
    plain_width = HD - RD
    scores = (
        jnp.einsum("qghd,kgd->ghqk", queries, key_full, preferred_element_type=jnp.float32)
        * score_scale
    )
    masked = jnp.where(allowed[None, None], scores, masked_value)
    probs_float = jnp.exp(masked - log_total)
    grad_probs = jnp.einsum(
        "qghd,kgd->ghqk", grad_heads, values, preferred_element_type=jnp.float32
    )
    row_delta = jnp.sum(probs_float * grad_probs, axis=-1, keepdims=True)
    grad_scores = (probs_float * (grad_probs - row_delta)).astype(jnp.bfloat16)
    grad_queries = (
        jnp.einsum("ghqk,kgd->qghd", grad_scores, key_full, preferred_element_type=jnp.float32)
        * score_scale
    )
    grad_keys = (
        jnp.einsum("ghqk,qghd->kgd", grad_scores, queries, preferred_element_type=jnp.float32)
        * score_scale
    )
    grad_values = jnp.einsum(
        "ghqk,qghd->kgd",
        probs_float.astype(jnp.bfloat16),
        grad_heads,
        preferred_element_type=jnp.float32,
    )
    grad_tied = grad_values + jnp.concatenate(
        [grad_keys[..., :plain_width], jnp.zeros_like(grad_keys[..., plain_width:])], axis=-1
    )
    grad_rope = jnp.sum(grad_keys[..., plain_width:], axis=1)
    return (grad_queries, grad_tied, grad_rope)


def on_device(
    inputs,
    gain_one,
    w_query,
    w_tied,
    w_rope,
    w_out,
    gain_two,
    w_gate,
    w_up,
    w_down,
    doc_starts,
    out_grad,
):
    seq_count, own_count, model_width = inputs.shape
    plain_width = HD - RD
    group_local = w_tied.shape[1] // HD
    head_local = w_query.shape[1] // HD
    seq_index = lax.axis_index("seq")
    mp_index = lax.axis_index("mp")
    gain_one_float = gain_one.astype(jnp.float32)
    gain_two_float = gain_two.astype(jnp.float32)
    inputs_float = inputs.astype(jnp.float32)
    inverse_one = lax.rsqrt(jnp.mean(inputs_float * inputs_float, axis=-1, keepdims=True) + epsilon)
    normed_one = (inputs_float * inverse_one * gain_one_float).astype(jnp.bfloat16)
    gathered_one = lax.all_gather(normed_one, "mp", axis=1, tiled=True)
    context = gathered_one.shape[1]
    token_count = seq_count * context
    flat_one = gathered_one.reshape(token_count, model_width)
    offset = seq_index * context
    cosine, sine_table = rope_tables(offset, context, RD)
    query_lin = jnp.dot(flat_one, w_query, preferred_element_type=jnp.float32).reshape(
        seq_count, context, head_local, HD
    )
    queries = jnp.concatenate(
        [
            query_lin[..., :plain_width],
            rotate(
                query_lin[..., plain_width:], cosine[None, :, None, :], sine_table[None, :, None, :]
            ),
        ],
        axis=-1,
    ).astype(jnp.bfloat16)
    queries = queries.reshape(seq_count, context, group_local, head_local // group_local, HD)
    tied_state = (
        jnp.dot(flat_one, w_tied, preferred_element_type=jnp.float32)
        .astype(jnp.bfloat16)
        .reshape(seq_count, context, group_local * HD)
    )
    rope_lin = jnp.dot(flat_one, w_rope, preferred_element_type=jnp.float32).reshape(
        seq_count, context, RD
    )
    rope_keys = rotate(rope_lin, cosine[None], sine_table[None]).astype(jnp.bfloat16)
    tied_all, rope_all = (
        lax.all_gather(tied_state, "seq", axis=1, tiled=True),
        lax.all_gather(rope_keys, "seq", axis=1, tiled=True),
    )
    length = tied_all.shape[1]
    values_all = tied_all.reshape(seq_count, length, group_local, HD)
    key_full = jnp.concatenate(
        [
            values_all[..., :plain_width],
            jnp.broadcast_to(rope_all[:, :, None, :], (seq_count, length, group_local, RD)),
        ],
        axis=-1,
    )
    key_position = jnp.arange(length, dtype=jnp.int32)
    key_segment = jnp.sum(
        (doc_starts[:, None, :] <= key_position[None, :, None]).astype(jnp.int32), axis=-1
    )
    query_segment = lax.dynamic_slice_in_dim(key_segment, offset, context, 1)
    query_position = offset + jnp.arange(context, dtype=jnp.int32)
    allowed = (query_segment[:, :, None] == key_segment[:, None, :]) & (
        query_position[:, None] >= key_position[None, :]
    )[None]
    head_outputs, log_total = lax.map(attend, (queries, key_full, values_all, allowed))
    flat_heads = head_outputs.reshape(token_count, head_local * HD)
    attended_part = jnp.dot(flat_heads, w_out, preferred_element_type=jnp.float32).reshape(
        seq_count, context, model_width
    )
    attended = lax.psum_scatter(
        attended_part.astype(jnp.bfloat16), "mp", scatter_dimension=1, tiled=True
    ).astype(jnp.float32)
    hidden = inputs_float + attended
    inverse_two = lax.rsqrt(jnp.mean(hidden * hidden, axis=-1, keepdims=True) + epsilon)
    normed_two = (hidden * inverse_two * gain_two_float).astype(jnp.bfloat16)
    gathered_two = lax.all_gather(normed_two, "mp", axis=1, tiled=True)
    flat_two = gathered_two.reshape(token_count, model_width)
    gate_values = jnp.dot(flat_two, w_gate, preferred_element_type=jnp.float32)
    up_values = jnp.dot(flat_two, w_up, preferred_element_type=jnp.float32)
    sigmoid_gate = jax.nn.sigmoid(gate_values)
    silu_gate = gate_values * sigmoid_gate
    active = (silu_gate * up_values).astype(jnp.bfloat16)
    result_part = jnp.dot(active, w_down, preferred_element_type=jnp.float32).reshape(
        seq_count, context, model_width
    )
    result = lax.psum_scatter(
        result_part.astype(jnp.bfloat16), "mp", scatter_dimension=1, tiled=True
    ).astype(jnp.float32)
    outputs = (hidden + result).astype(jnp.bfloat16)
    grad_out_all = lax.all_gather(out_grad, "mp", axis=1, tiled=True)
    flat_grad = grad_out_all.reshape(token_count, model_width)
    grad_active = times_transposed(flat_grad, w_down)
    grad_w_down = contract_rows(active, flat_grad)
    grad_gate = (
        grad_active * up_values * sigmoid_gate * (1.0 + gate_values * (1.0 - sigmoid_gate))
    ).astype(jnp.bfloat16)
    grad_up = (grad_active * silu_gate).astype(jnp.bfloat16)
    grad_w_gate = contract_rows(flat_two, grad_gate)
    grad_w_up = contract_rows(flat_two, grad_up)
    grad_two_part = (times_transposed(grad_gate, w_gate) + times_transposed(grad_up, w_up)).reshape(
        seq_count, context, model_width
    )
    grad_normed_two = lax.psum_scatter(
        grad_two_part.astype(jnp.bfloat16), "mp", scatter_dimension=1, tiled=True
    ).astype(jnp.float32)
    grad_hidden_norm, grad_gain_two = norm_back(
        grad_normed_two, hidden, inverse_two, gain_two_float
    )
    grad_hidden = out_grad.astype(jnp.float32) + grad_hidden_norm
    grad_attended_all = lax.all_gather(grad_hidden.astype(jnp.bfloat16), "mp", axis=1, tiled=True)
    flat_attended = grad_attended_all.reshape(token_count, model_width)
    grad_w_out = contract_rows(flat_heads, flat_attended)
    grad_heads = times_transposed(flat_attended, w_out).astype(jnp.bfloat16).reshape(queries.shape)
    grad_queries, grad_tied, grad_rope = lax.map(
        attend_back, (queries, key_full, values_all, allowed, log_total, grad_heads)
    )
    grad_queries = grad_queries.reshape(seq_count, context, head_local, HD)
    grad_query_lin = (
        jnp.concatenate(
            [
                grad_queries[..., :plain_width],
                rotate_back(
                    grad_queries[..., plain_width:],
                    cosine[None, :, None, :],
                    sine_table[None, :, None, :],
                ),
            ],
            axis=-1,
        )
        .astype(jnp.bfloat16)
        .reshape(token_count, head_local * HD)
    )
    tied_own, rope_context = (
        lax.psum_scatter(
            grad_tied.reshape(seq_count, length, group_local * HD).astype(jnp.bfloat16),
            "seq",
            scatter_dimension=1,
            tiled=True,
        ).astype(jnp.float32),
        lax.psum_scatter(
            grad_rope.astype(jnp.bfloat16), "seq", scatter_dimension=1, tiled=True
        ).astype(jnp.float32),
    )
    grad_tied_flat = tied_own.astype(jnp.bfloat16).reshape(token_count, group_local * HD)
    grad_one_part = (
        times_transposed(grad_query_lin, w_query) + times_transposed(grad_tied_flat, w_tied)
    ).reshape(seq_count, context, model_width)
    grad_normed_one, rope_own = (
        lax.psum_scatter(
            grad_one_part.astype(jnp.bfloat16), "mp", scatter_dimension=1, tiled=True
        ).astype(jnp.float32),
        lax.psum_scatter(
            rope_context.astype(jnp.bfloat16), "mp", scatter_dimension=1, tiled=True
        ).astype(jnp.float32),
    )
    own_offset = offset + mp_index * own_count
    cosine_own, sine_own = rope_tables(own_offset, own_count, RD)
    grad_rope_flat = (
        rotate_back(rope_own, cosine_own[None], sine_own[None])
        .astype(jnp.bfloat16)
        .reshape(seq_count * own_count, RD)
    )
    grad_normed_one = grad_normed_one + times_transposed(grad_rope_flat, w_rope).reshape(
        seq_count, own_count, model_width
    )
    grad_w_rope = contract_rows(
        normed_one.reshape(seq_count * own_count, model_width), grad_rope_flat
    )
    grad_w_query = contract_rows(flat_one, grad_query_lin)
    grad_w_tied = contract_rows(flat_one, grad_tied_flat)
    grad_inputs_norm, grad_gain_one = norm_back(
        grad_normed_one, inputs_float, inverse_one, gain_one_float
    )
    grad_inputs = grad_hidden + grad_inputs_norm
    small_sums = (
        lax.psum_scatter(grad_gain_one, ("dp", "seq", "mp"), scatter_dimension=0, tiled=True),
        lax.psum_scatter(grad_w_rope, ("dp", "seq", "mp"), scatter_dimension=0, tiled=True),
        lax.psum_scatter(grad_gain_two, ("dp", "seq", "mp"), scatter_dimension=0, tiled=True),
    )
    weight_terms = (grad_w_query, grad_w_tied, grad_w_out, grad_w_gate, grad_w_up, grad_w_down)
    weight_sums = (
        lax.psum_scatter(weight_terms[0], ("dp", "seq"), scatter_dimension=0, tiled=True),
        lax.psum_scatter(weight_terms[1], ("dp", "seq"), scatter_dimension=0, tiled=True),
        lax.psum_scatter(weight_terms[2], ("dp", "seq"), scatter_dimension=1, tiled=True),
        lax.psum_scatter(weight_terms[3], ("dp", "seq"), scatter_dimension=0, tiled=True),
        lax.psum_scatter(weight_terms[4], ("dp", "seq"), scatter_dimension=0, tiled=True),
        lax.psum_scatter(weight_terms[5], ("dp", "seq"), scatter_dimension=1, tiled=True),
    )
    return (
        outputs,
        grad_inputs,
        small_sums[0],
        weight_sums[0],
        weight_sums[1],
        small_sums[1],
        weight_sums[2],
        small_sums[2],
        weight_sums[3],
        weight_sums[4],
        weight_sums[5],
    )


def solution(mesh):
    in_specs = (
        P("dp", ("seq", "mp"), None),
        P(),
        P(None, "mp"),
        P(None, "mp"),
        P(),
        P("mp", None),
        P(),
        P(None, "mp"),
        P(None, "mp"),
        P("mp", None),
        P("dp", None),
        P("dp", ("seq", "mp"), None),
    )
    out_specs = (
        P("dp", ("seq", "mp"), None),
        P("dp", ("seq", "mp"), None),
        P(("dp", "seq", "mp")),
        P(("dp", "seq"), "mp"),
        P(("dp", "seq"), "mp"),
        P(("dp", "seq", "mp"), None),
        P("mp", ("dp", "seq")),
        P(("dp", "seq", "mp")),
        P(("dp", "seq"), "mp"),
        P(("dp", "seq"), "mp"),
        P("mp", ("dp", "seq")),
    )
    return jax.shard_map(
        on_device, mesh=mesh, in_specs=in_specs, out_specs=out_specs, check_vma=False
    )
```

profile of v0, /device:TPU:0, one launch (start us, length us, event | category | flops | bytes accessed | tf_op | source)
XLA Modules:
  0.0 2569.5 jit_solution(11917534684176559158)
XLA Ops:
  16.7 22.7 all-gather.7.cloned.1.call-done
  74.9 25.2 all-gather.9.cloned.1.call-done
  109.8 19.2 all-gather.11.cloned.1.call-done
  134.6 376.9 %while.26 = (s32[]{:T(128)}, bf16[8,512,2,4,64]{1,4,3,2,0:T(8,128)(2,1)}, f32[8,2,4,512,1]{3,2,1,4,0:T(4,128)}, bf16[8,2048,2,64]{1,3,2,0:T(8,128)(2,1)}, pred[8...) while((s32[]{:T(128)}, ...), condition=%wide.region_5.6_spmd, body=%wide.region_2.5_spmd.sunk | while | flops 2248404992 | bytes 108136552 | solution.py:196
  259.3 15.9 fusion.160
  306.4 15.9 fusion.160
  353.5 15.9 fusion.160
  400.6 15.9 fusion.160
  447.7 15.9 fusion.160
  494.8 15.9 fusion.160
  522.6 16.3 reduce-scatter.15.cloned.1.call-done
  548.7 20.6 all-gather.13.cloned.1.call-done
  569.3 19.9 fusion.93
  589.2 16.2 fusion.92
  605.4 40.1 %multiply_convert_fusion = (bf16[4096,1408]{1,0:T(8,128)(2,1)}, bf16[4096,1408]{1,0:T(8,128)(2,1)}, bf16[4096,1408]{1,0:T(8,128)(2,1)}) fusion(f32[4096,1408]{1,0:T(8,128)} %fusion.92, f32[4096,1408]{1,0:T(8,128)} %fusion.93, bf16[4096,1024]{1,0:T(8,128)(2,1)} %bitcast.316, bf16[1408,1024]{1,0:T(8,128)(2,1)S(1)} %copy-done), kind=kOutput, calls=%fused_computation.71 | convolution fusion | flops 11897667584 | bytes 92012544 | tf_op jit(solution)/shard_map/dot_general | solution.py:55
  645.5 19.1 fusion.94
  664.7 21.6 add_convert_fusion.1
  686.3 18.2 reduce-scatter.19.cloned.1.call-done
  719.1 21.2 all-gather.17.cloned.1.call-done
  776.9 884.4 %while.27 = (s32[]{:T(128)}, f32[8,512,2,4,64]{1,4,3,2,0:T(8,128)}, bf16[8,2048,2,64]{1,3,2,0:T(8,128)(2,1)}, bf16[8,2048,32]{1,2,0:T(8,128)(2,1)}, bf16[8,2048,...) while((s32[]{:T(128)}, f32[8,512,2,4,64]{1,4,3,2,0:T(8,128)}, ...), condition=%wide.region_14.15_spmd, body=%wide.region_11.14_spmd.sunk | while | flops 5495648256 | bytes 274190592 | solution.py:245
  779.6 17.2 fusion.169
  796.8 23.7 fusion.170
  820.4 28.5 %fusion.171 = bf16[2,4,512,2048]{2,3,1,0:T(8,128)(2,1)} fusion(f32[2,2048,512,4]{2,1,3,0:T(8,128)} %get-tuple-element.326, f32[2,2048,512,4]{2,1,3,0:T(8,128)} %fusion.169, f32[2,4,512]{2,1,0:T(4,128)S(1)} %get-tuple-element.327, f32[2,4,512]{2,1,0:T(4,128)S(1)} %dynamic-slice_bitcast_fusion.7, pred[512,2048]{0,1:T(8,128)(4,1)} %copy-done.1), kind=kLoop, calls=%fused_computation.26.clone.1 | loop fusion | flops 50331648 | bytes 84967424 | tf_op jit(solution)/shard_map/while/body/eval_jaxpr/convert_element_type | solution.py:99
  861.0 16.1 fusion.174
  890.1 17.2 fusion.169
  907.3 23.7 fusion.170
  930.9 28.5 %fusion.171 = bf16[2,4,512,2048]{2,3,1,0:T(8,128)(2,1)} fusion(f32[2,2048,512,4]{2,1,3,0:T(8,128)} %get-tuple-element.326, f32[2,2048,512,4]{2,1,3,0:T(8,128)} %fusion.169, f32[2,4,512]{2,1,0:T(4,128)S(1)} %get-tuple-element.327, f32[2,4,512]{2,1,0:T(4,128)S(1)} %dynamic-slice_bitcast_fusion.7, pred[512,2048]{0,1:T(8,128)(4,1)} %copy-done.1), kind=kLoop, calls=%fused_computation.26.clone.1 | loop fusion | flops 50331648 | bytes 84967424 | tf_op jit(solution)/shard_map/while/body/eval_jaxpr/convert_element_type | solution.py:99
  971.5 16.1 fusion.174
  1000.6 17.2 fusion.169
  1017.8 23.7 fusion.170
  1041.5 28.5 %fusion.171 = bf16[2,4,512,2048]{2,3,1,0:T(8,128)(2,1)} fusion(f32[2,2048,512,4]{2,1,3,0:T(8,128)} %get-tuple-element.326, f32[2,2048,512,4]{2,1,3,0:T(8,128)} %fusion.169, f32[2,4,512]{2,1,0:T(4,128)S(1)} %get-tuple-element.327, f32[2,4,512]{2,1,0:T(4,128)S(1)} %dynamic-slice_bitcast_fusion.7, pred[512,2048]{0,1:T(8,128)(4,1)} %copy-done.1), kind=kLoop, calls=%fused_computation.26.clone.1 | loop fusion | flops 50331648 | bytes 84967424 | tf_op jit(solution)/shard_map/while/body/eval_jaxpr/convert_element_type | solution.py:99
  1082.0 16.1 fusion.174
  1111.1 17.2 fusion.169
  1128.2 23.7 fusion.170
  1151.9 28.5 %fusion.171 = bf16[2,4,512,2048]{2,3,1,0:T(8,128)(2,1)} fusion(f32[2,2048,512,4]{2,1,3,0:T(8,128)} %get-tuple-element.326, f32[2,2048,512,4]{2,1,3,0:T(8,128)} %fusion.169, f32[2,4,512]{2,1,0:T(4,128)S(1)} %get-tuple-element.327, f32[2,4,512]{2,1,0:T(4,128)S(1)} %dynamic-slice_bitcast_fusion.7, pred[512,2048]{0,1:T(8,128)(4,1)} %copy-done.1), kind=kLoop, calls=%fused_computation.26.clone.1 | loop fusion | flops 50331648 | bytes 84967424 | tf_op jit(solution)/shard_map/while/body/eval_jaxpr/convert_element_type | solution.py:99
  1192.5 16.1 fusion.174
  1221.5 17.2 fusion.169
  1238.7 23.7 fusion.170
  1262.4 28.5 %fusion.171 = bf16[2,4,512,2048]{2,3,1,0:T(8,128)(2,1)} fusion(f32[2,2048,512,4]{2,1,3,0:T(8,128)} %get-tuple-element.326, f32[2,2048,512,4]{2,1,3,0:T(8,128)} %fusion.169, f32[2,4,512]{2,1,0:T(4,128)S(1)} %get-tuple-element.327, f32[2,4,512]{2,1,0:T(4,128)S(1)} %dynamic-slice_bitcast_fusion.7, pred[512,2048]{0,1:T(8,128)(4,1)} %copy-done.1), kind=kLoop, calls=%fused_computation.26.clone.1 | loop fusion | flops 50331648 | bytes 84967424 | tf_op jit(solution)/shard_map/while/body/eval_jaxpr/convert_element_type | solution.py:99
  1303.0 16.1 fusion.174
  1332.0 17.2 fusion.169
  1349.2 23.7 fusion.170
  1372.9 28.5 %fusion.171 = bf16[2,4,512,2048]{2,3,1,0:T(8,128)(2,1)} fusion(f32[2,2048,512,4]{2,1,3,0:T(8,128)} %get-tuple-element.326, f32[2,2048,512,4]{2,1,3,0:T(8,128)} %fusion.169, f32[2,4,512]{2,1,0:T(4,128)S(1)} %get-tuple-element.327, f32[2,4,512]{2,1,0:T(4,128)S(1)} %dynamic-slice_bitcast_fusion.7, pred[512,2048]{0,1:T(8,128)(4,1)} %copy-done.1), kind=kLoop, calls=%fused_computation.26.clone.1 | loop fusion | flops 50331648 | bytes 84967424 | tf_op jit(solution)/shard_map/while/body/eval_jaxpr/convert_element_type | solution.py:99
  1413.4 16.1 fusion.174
  1442.5 17.2 fusion.169
  1459.7 23.7 fusion.170
  1483.4 28.5 %fusion.171 = bf16[2,4,512,2048]{2,3,1,0:T(8,128)(2,1)} fusion(f32[2,2048,512,4]{2,1,3,0:T(8,128)} %get-tuple-element.326, f32[2,2048,512,4]{2,1,3,0:T(8,128)} %fusion.169, f32[2,4,512]{2,1,0:T(4,128)S(1)} %get-tuple-element.327, f32[2,4,512]{2,1,0:T(4,128)S(1)} %dynamic-slice_bitcast_fusion.7, pred[512,2048]{0,1:T(8,128)(4,1)} %copy-done.1), kind=kLoop, calls=%fused_computation.26.clone.1 | loop fusion | flops 50331648 | bytes 84967424 | tf_op jit(solution)/shard_map/while/body/eval_jaxpr/convert_element_type | solution.py:99
  1523.9 16.1 fusion.174
  1553.0 17.2 fusion.169
  1570.2 23.7 fusion.170
  1593.8 28.5 %fusion.171 = bf16[2,4,512,2048]{2,3,1,0:T(8,128)(2,1)} fusion(f32[2,2048,512,4]{2,1,3,0:T(8,128)} %get-tuple-element.326, f32[2,2048,512,4]{2,1,3,0:T(8,128)} %fusion.169, f32[2,4,512]{2,1,0:T(4,128)S(1)} %get-tuple-element.327, f32[2,4,512]{2,1,0:T(4,128)S(1)} %dynamic-slice_bitcast_fusion.7, pred[512,2048]{0,1:T(8,128)(4,1)} %copy-done.1), kind=kLoop, calls=%fused_computation.26.clone.1 | loop fusion | flops 50331648 | bytes 84967424 | tf_op jit(solution)/shard_map/while/body/eval_jaxpr/convert_element_type | solution.py:99
  1634.4 16.1 fusion.174
  1690.5 55.8 %reduce-scatter.21.cloned.1.call-done = bf16[8,512,128]{2,1,0:T(8,128)(2,1)} async-done(((bf16[8,2048,128]{2,1,0:T(8,128)(2,1)}), bf16[8,512,128]{2,1,0:T(8,128)(2,1)}) %reduce-scatter.21.cloned.1.call-update) | async-done | bytes 1048592 | tf_op jit(solution)/shard_map/reduce_scatter | solution.py:265
  1758.1 18.3 convolution_convert_fusion
  1776.5 19.6 fusion.100
  1796.2 20.0 fusion.98
  1816.3 19.6 fusion.99
  1886.6 42.6 %all-reduce.2 = (f32[1024]{0:T(1024)S(1)}, f32[1024]{0:T(1024)S(1)}) all-reduce(f32[1024]{0:T(1024)S(1)} %get-tuple-element.150, f32[1024]{0:T(1024)S(1)} %copy-done.33), channel_id=9, replica_groups=mesh['dp'=4,'seq'=4,'mp'=2] {'dp','seq','mp'}, use_global_device_ids=true, to_apply=%region_21.22.clone | all-reduce | flops 2048 | bytes 16384
  1946.1 112.4 %reduce-scatter.37.cloned.1.call-done = f32[64,1408]{1,0:T(8,128)} async-done(((f32[1024,1408]{1,0:T(8,128)}), f32[64,1408]{1,0:T(8,128)}) %reduce-scatter.37.cloned.1.call-update) | async-done | bytes 360464 | tf_op jit(solution)/shard_map/reduce_scatter | solution.py:316
  2058.5 129.9 %reduce-scatter.39.cloned.1.call-done = f32[64,1408]{1,0:T(8,128)} async-done(((f32[1024,1408]{1,0:T(8,128)}), f32[64,1408]{1,0:T(8,128)}) %reduce-scatter.39.cloned.1.call-update) | async-done | bytes 360464 | tf_op jit(solution)/shard_map/reduce_scatter | solution.py:317
  2188.4 137.6 %reduce-scatter.33.cloned.1.call-done = f32[32,32]{1,0:T(8,128)} async-done(((f32[1024,32]{1,0:T(8,128)}), f32[32,32]{1,0:T(8,128)}) %reduce-scatter.33.cloned.1.call-update) | async-done | bytes 4112 | tf_op jit(solution)/shard_map/reduce_scatter | solution.py:308
  2326.0 79.2 %reduce-scatter.35.cloned.1.call-done = f32[512,64]{0,1:T(8,128)} async-done(((f32[512,1024]{0,1:T(8,128)}), f32[512,64]{0,1:T(8,128)}) %reduce-scatter.35.cloned.1.call-update) | async-done | bytes 131088 | tf_op jit(solution)/shard_map/reduce_scatter | solution.py:315
  2405.2 80.9 %reduce-scatter.29.cloned.1.call-done = f32[64,512]{1,0:T(8,128)} async-done(((f32[1024,512]{1,0:T(8,128)}), f32[64,512]{1,0:T(8,128)}) %reduce-scatter.29.cloned.1.call-update) | async-done | bytes 131088 | tf_op jit(solution)/shard_map/reduce_scatter | solution.py:313
  2486.1 76.3 %reduce-scatter.31.cloned.1.call-done = f32[64,128]{1,0:T(8,128)} async-done(((f32[1024,128]{1,0:T(8,128)}), f32[64,128]{1,0:T(8,128)}) %reduce-scatter.31.cloned.1.call-update) | async-done | bytes 32784 | tf_op jit(solution)/shard_map/reduce_scatter | solution.py:314
  (301 shorter events, 722.0 us)
Async XLA Ops:
  7.2 598.2 %copy-start = (bf16[1408,1024]{1,0:T(8,128)(2,1)S(1)}, bf16[1408,1024]{1,0:T(8,128)(2,1)}, u32[]{:S(2)}) copy-start(bf16[1408,1024]{1,0:T(8,128)(2,1)} %param.25) | copy-start | bytes 8650756
  7.2 32.1 %all-gather.7.cloned.1.call-start = ((), (), s32[]{:S(2)}) async-start(), calls=%async_computation.14 | async-start | bytes 12582912 | tf_op jit(solution)/shard_map/all_gather | solution.py:146
  8.1 31.2 %copy-start.14 = (bf16[1024,128]{1,0:T(8,128)(2,1)S(1)}, bf16[1024,128]{1,0:T(8,128)(2,1)}, u32[]{:S(2)}) copy-start(bf16[1024,128]{1,0:T(8,128)(2,1)} %param.19) | copy-start | bytes 786436
  16.6 83.5 %all-gather.9.cloned.1.call-start = ((), (), s32[]{:S(2)}) async-start(), calls=%async_computation.15 | async-start | bytes 5242880 | tf_op jit(solution)/shard_map/all_gather | solution.py:175
  39.3 9.1 copy-start.34
  46.0 11.1 copy-start.28
  46.1 83.0 %all-gather.11.cloned.1.call-start = ((), (), s32[]{:S(2)}) async-start(), calls=%async_computation.16 | async-start | bytes 1310720 | tf_op jit(solution)/shard_map/all_gather | solution.py:176
  48.4 14.6 copy-start.35
  48.9 23.0 copy-start.10
  48.9 23.0 copy-start.12
  63.9 475.0 %reduce-scatter.15.cloned.1.call-start = ((), (), s32[]{:S(2)}) async-start(), calls=%async_computation.17 | async-start | bytes 12582912 | tf_op jit(solution)/shard_map/reduce_scatter | solution.py:201
  522.0 47.4 %all-gather.13.cloned.1.call-start = ((), (), s32[]{:S(2)}) async-start(), calls=%async_computation.18 | async-start | bytes 12582912 | tf_op jit(solution)/shard_map/all_gather | solution.py:207
  522.6 25.4 copy-start.19
  548.1 57.3 %all-gather.15.cloned.1.call-start = ((), (), s32[]{:S(2)}) async-start(), calls=%async_computation.20 | async-start | bytes 12582912 | tf_op jit(solution)/shard_map/all_gather | solution.py:221
  548.6 155.8 %reduce-scatter.19.cloned.1.call-start = ((), (), s32[]{:S(2)}) async-start(), calls=%async_computation.21 | async-start | bytes 12582912 | tf_op jit(solution)/shard_map/reduce_scatter | solution.py:234
  569.3 19.9 copy-start.38
  569.3 19.9 copy-start.39
  686.2 18.3 copy-start.17
  686.2 18.3 copy-start.20
  686.3 26.1 %copy-start.24 = (f32[8,256]{1,0:T(8,128)S(1)}, f32[8,256]{1,0:T(8,128)}, u32[]{:S(2)}) copy-start(f32[8,256]{1,0:T(8,128)} %get-tuple-element.207) | copy-start | bytes 24580
  686.3 54.0 %all-gather.17.cloned.1.call-start = ((), (), s32[]{:S(2)}) async-start(), calls=%async_computation.22 | async-start | bytes 12582912 | tf_op jit(solution)/shard_map/all_gather | solution.py:241
  704.5 7.9 copy-start.3
  704.5 7.9 copy-start.6
  704.5 8.3 copy-start.7
  719.0 971.4 %reduce-scatter.25.cloned.1.call-start = ((), (), s32[]{:S(2)}) async-start(), calls=%async_computation.25 | async-start | bytes 1310720 | tf_op jit(solution)/shard_map/reduce_scatter | solution.py:271
  764.2 12.7 copy-start.40
  779.6 17.2 copy-start.1
  877.1 9.9 copy-start.4
  890.1 17.2 copy-start.1
  987.6 9.9 copy-start.4
  1000.6 17.2 copy-start.1
  1098.1 9.9 copy-start.4
  1111.0 17.2 copy-start.1
  1208.6 9.9 copy-start.4
  1221.5 17.2 copy-start.1
  1319.1 9.9 copy-start.4
  1332.0 17.2 copy-start.1
  1429.5 9.9 copy-start.4
  1442.5 17.2 copy-start.1
  1540.0 9.9 copy-start.4
  1553.0 17.2 copy-start.1
  1650.5 9.9 copy-start.4
  1661.3 84.9 %reduce-scatter.21.cloned.1.call-start = ((), (), s32[]{:S(2)}) async-start(), calls=%async_computation.23 | async-start | bytes 5242880 | tf_op jit(solution)/shard_map/reduce_scatter | solution.py:265
  1661.4 9.3 copy-start.11
  1661.4 9.3 copy-start.13
  1667.9 177.5 %reduce-scatter.27.cloned.1.call-start = ((), (), s32[]{:S(2)}) async-start(), calls=%async_computation.26 | async-start | bytes 393216 | tf_op jit(solution)/shard_map/reduce_scatter | solution.py:283
  1680.9 65.3 %copy-start.15 = (bf16[1024,128]{1,0:T(8,128)(2,1)S(1)}, bf16[1024,128]{1,0:T(8,128)(2,1)}, u32[]{:S(2)}) copy-start(bf16[1024,128]{1,0:T(8,128)(2,1)} %param.19) | copy-start | bytes 786436
  1690.4 188.6 %reduce-scatter.23.cloned.1.call-start = ((), (), s32[]{:S(2)}) async-start(), calls=%async_computation.24 | async-start | bytes 12582912 | tf_op jit(solution)/shard_map/reduce_scatter | solution.py:280
  1758.1 172.3 %reduce-scatter.17.cloned.1.call-start = ((), (), s32[]{:S(2)}) async-start(), calls=%async_computation.19 | async-start | bytes 12582912 | tf_op jit(solution)/shard_map/reduce_scatter | solution.py:217
  1776.5 169.6 %reduce-scatter.41.cloned.1.call-start = ((), (), s32[]{:S(2)}) async-start(), calls=%async_computation.33 | async-start | bytes 6127616 | tf_op jit(solution)/shard_map/reduce_scatter | solution.py:318
  1796.1 262.4 %reduce-scatter.37.cloned.1.call-start = ((), (), s32[]{:S(2)}) async-start(), calls=%async_computation.31 | async-start | bytes 6127616 | tf_op jit(solution)/shard_map/reduce_scatter | solution.py:316
  1816.2 20.0 copy-start.36
  1816.2 372.1 %reduce-scatter.39.cloned.1.call-start = ((), (), s32[]{:S(2)}) async-start(), calls=%async_computation.32 | async-start | bytes 6127616 | tf_op jit(solution)/shard_map/reduce_scatter | solution.py:317
  1835.9 490.0 %reduce-scatter.33.cloned.1.call-start = ((), (), s32[]{:S(2)}) async-start(), calls=%async_computation.29 | async-start | bytes 540672 | tf_op jit(solution)/shard_map/reduce_scatter | solution.py:308
  1850.7 554.5 %reduce-scatter.35.cloned.1.call-start = ((), (), s32[]{:S(2)}) async-start(), calls=%async_computation.30 | async-start | bytes 2228224 | tf_op jit(solution)/shard_map/reduce_scatter | solution.py:315
  1861.3 624.8 %reduce-scatter.29.cloned.1.call-start = ((), (), s32[]{:S(2)}) async-start(), calls=%async_computation.27 | async-start | bytes 2228224 | tf_op jit(solution)/shard_map/reduce_scatter | solution.py:313
  1872.1 7.0 copy-start.31
  1872.1 690.4 %reduce-scatter.31.cloned.1.call-start = ((), (), s32[]{:S(2)}) async-start(), calls=%async_computation.28 | async-start | bytes 557056 | tf_op jit(solution)/shard_map/reduce_scatter | solution.py:314
  1879.0 7.6 copy-start.33
  1879.0 51.4 %copy-start.18 = (f32[8,256]{1,0:T(8,128)S(1)}, f32[8,256]{1,0:T(8,128)}, u32[]{:S(2)}) copy-start(f32[8,256]{1,0:T(8,128)} %copy-done.16) | copy-start | bytes 24580
  1879.0 51.4 %copy-start.21 = (f32[1024]{0:T(1024)S(1)}, f32[1024]{0:T(1024)}, u32[]{:S(2)}) copy-start(f32[1024]{0:T(1024)} %copy-done.19) | copy-start | bytes 12292
  1879.0 51.4 %copy-start.25 = (f32[8,256]{1,0:T(8,128)S(1)}, f32[8,256]{1,0:T(8,128)}, u32[]{:S(2)}) copy-start(f32[8,256]{1,0:T(8,128)} %get-tuple-element.207) | copy-start | bytes 24580
  1879.0 51.4 %copy-start.27 = (f32[8,256]{1,0:T(8,128)S(1)}, f32[8,256]{1,0:T(8,128)}, u32[]{:S(2)}) copy-start(f32[8,256]{1,0:T(8,128)} %copy-done.26) | copy-start | bytes 24580
  1879.0 51.4 %copy-start.32 = (f32[8,256]{1,0:T(8,128)S(1)}, f32[8,256]{1,0:T(8,128)}, u32[]{:S(2)}) copy-start(f32[8,256]{1,0:T(8,128)} %get-tuple-element.205) | copy-start | bytes 24580
  (11 other events, 41.5 us)
Sparse Core Ops, SparseCore 0:
  16.7 22.5 all-gather.6
  46.2 53.8 all-gather.8
  102.5 26.4 all-gather.10
  522.1 16.8 reduce-scatter.14
  548.2 21.1 all-gather.12
  570.8 21.0 all-gather.14
  686.4 18.0 reduce-scatter.18
  719.1 21.1 all-gather.16
  1661.5 28.8 reduce-scatter.24
  1693.5 52.6 reduce-scatter.20
  1748.4 7.6 reduce-scatter.26
  1759.0 17.9 reduce-scatter.22
  1779.3 18.0 reduce-scatter.16
  1800.2 128.0 reduce-scatter.40
  1931.1 127.3 reduce-scatter.36
  2061.4 126.9 reduce-scatter.38
  2191.1 134.8 reduce-scatter.32
  2328.7 76.4 reduce-scatter.34
  2408.0 78.0 reduce-scatter.28
  2488.8 73.6 reduce-scatter.30
where the time goes:
time: 2580 us; the launch traced here: 2570 us
  matrix products  1170 us (45%)
  waiting for transfers between devices  817 us (32%)
  other arithmetic  416 us (16%)
  local copies, waits for them, and re-layouts  106 us (4%)
  blocking collectives  42.6 us (2%)
    convert_element_type x8, other arithmetic, attend_back(): grad_scores = (probs_float * (grad_probs - row_delta)).astype(jnp.bfloat16)  228 us
    dot_general x8, matrix products, attend_back(): jnp.einsum('qghd,kgd->ghqk', grad_heads, values, preferred_element_type=j...  189 us
    reduce_scatter x1, waiting for transfers between devices, on_device(): lax.psum_scatter(grad_w_rope, ('dp', 'seq', 'mp'), scatter_dimension=0, t...  138 us
    dot_general x8, matrix products, attend_back(): jnp.einsum('qghd,kgd->ghqk', queries, key_full, preferred_element_type=jn...  138 us
    reduce_scatter x1, waiting for transfers between devices, on_device(): lax.psum_scatter(weight_terms[4], ('dp', 'seq'), scatter_dimension=0, til...  130 us
    dot_general x8, matrix products, attend_back(): jnp.einsum('ghqk,qghd->kgd', probs_float.astype(jnp.bfloat16), grad_heads...  129 us
    dot_general x8, matrix products, attend(): jnp.einsum('ghqk,kgd->qghd', attention_probs, values, preferred_element_t...  127 us
    dot_general x7, matrix products, times_transposed(): lax.dot_general(left, right, (((1,), (1,)), ((), ())), preferred_element_...  119 us
  transfers between devices with their start and end apart: 20, of which 15 were waited for; matrix products, arithmetic and copies ran while one was open for 10% of the time, Pallas kernels for 0%

commit v1 on v0

--- a/solution.py
+++ b/solution.py
@@ -1,6 +1,10 @@
+import functools
+
 import jax
 import jax.numpy as jnp
 from jax import lax
+from jax.experimental import pallas as pl
+from jax.experimental.pallas import tpu as pltpu
 from jax.sharding import PartitionSpec as P
 
 HD = 64
@@ -332,6 +336,687 @@
     )
 
 
+BF = jnp.bfloat16
+F32 = jnp.float32
+NN = (((1,), (0,)), ((), ()))
+NT = (((1,), (1,)), ((), ()))
+TN = (((0,), (0,)), ((), ()))
+BIG = 2.0**100
+MIB = 1 << 20
+LANE = 128
+
+
+def mxu(left, right, dims):
+    return lax.dot_general(left, right, dims, preferred_element_type=F32)
+
+
+def params(limit=56):
+    return pltpu.CompilerParams(vmem_limit_bytes=limit * MIB)
+
+
+def swap_cores(value):
+    return lax.ppermute(value, "mp", [(0, 1), (1, 0)])
+
+
+def by_core(own, other, axis):
+    first = lax.axis_index("mp") == 0
+    return jnp.concatenate(
+        [jnp.where(first, own, other), jnp.where(first, other, own)], axis=axis
+    )
+
+
+def rotate_rows(values, cosine, sine_table):
+    half = values.shape[0] // 2
+    a, b = values[:half], values[half:]
+    return jnp.concatenate([a * cosine - b * sine_table, b * cosine + a * sine_table], axis=0)
+
+
+def project_kernel(heads, x_ref, gain_ref, w_ref, cos_ref, sin_ref, q_ref, kv_ref, nt_ref):
+    x = x_ref[0].astype(F32)
+    inverse = lax.rsqrt(jnp.mean(x * x, axis=-1, keepdims=True) + epsilon)
+    normed = (x * inverse * gain_ref[...]).astype(BF)
+    nt_ref[...] = normed.T
+    cosine, sine_table = cos_ref[...], sin_ref[...]
+    lin = mxu(w_ref[...], normed, NT)
+    plain = HD - RD
+    pieces = []
+    for h in range(heads):
+        at = h * HD
+        pieces.append(lin[at : at + plain])
+        pieces.append(rotate_rows(lin[at + plain : at + HD], cosine, sine_table))
+    queries = jnp.concatenate(pieces, axis=0)
+    q_ref[...] = (queries.astype(BF) * HD ** (-0.5)).astype(BF)
+    tied_end = w_ref.shape[0] - RD
+    kv_ref[0, : tied_end - heads * HD] = lin[heads * HD : tied_end].astype(BF)
+    kv_ref[0, tied_end - heads * HD :] = rotate_rows(lin[tied_end:], cosine, sine_table).astype(BF)
+
+
+def project(x, gain, weights, cosine, sine_table, heads):
+    count, own, width = x.shape
+    rows = weights.shape[0]
+    kv_rows = rows - heads * HD
+    whole = lambda b: (0, 0)
+    return pl.pallas_call(
+        functools.partial(project_kernel, heads),
+        grid=(count,),
+        in_specs=[
+            pl.BlockSpec((1, own, width), lambda b: (b, 0, 0)),
+            pl.BlockSpec((1, width), whole),
+            pl.BlockSpec((rows, width), whole),
+            pl.BlockSpec(cosine.shape, whole),
+            pl.BlockSpec(cosine.shape, whole),
+        ],
+        out_specs=[
+            pl.BlockSpec((heads * HD, own), lambda b: (0, b)),
+            pl.BlockSpec((1, kv_rows, own), lambda b: (b, 0, 0)),
+            pl.BlockSpec((width, own), lambda b: (0, b)),
+        ],
+        out_shape=[
+            jax.ShapeDtypeStruct((heads * HD, count * own), BF),
+            jax.ShapeDtypeStruct((count, kv_rows, own), BF),
+            jax.ShapeDtypeStruct((width, count * own), BF),
+        ],
+        compiler_params=params(),
+        name="project",
+    )(x, gain, weights, cosine, sine_table)
+
+
+def segment_counts(starts, first, width):
+    position = first + lax.broadcasted_iota(jnp.int32, (1, width), 1)
+    count = jnp.zeros((1, width), jnp.int32)
+    for start in starts:
+        count = count + (start <= position).astype(jnp.int32)
+    return count
+
+
+def query_rows(starts, first, width):
+    row = lax.broadcasted_iota(jnp.int32, (16, width), 0)
+    match = segment_counts(starts, first, width) == row + 1
+    return jnp.where(match, 1.0, 0.0).astype(BF)
+
+
+def key_rows(starts, first, width):
+    row = lax.broadcasted_iota(jnp.int32, (16, width), 0)
+    match = (segment_counts(starts, first, width) == row + 1) | (row >= len(starts))
+    return jnp.where(match, 0.0, -BIG).astype(BF)
+
+
+def first_rows(count, width):
+    row = lax.broadcasted_iota(jnp.int32, (16, width), 0)
+    return jnp.where(row < count, 1.0, 0.0).astype(BF)
+
+
+def three_parts(row, width):
+    high = row.astype(BF)
+    rest = row - high.astype(F32)
+    middle = rest.astype(BF)
+    low = (rest - middle.astype(F32)).astype(BF)
+    at = lax.broadcasted_iota(jnp.int32, (16, width), 0)
+    parts = jnp.where(at == 0, high.astype(F32), 0.0)
+    parts = jnp.where(at == 1, middle.astype(F32), parts)
+    return jnp.where(at == 2, low.astype(F32), parts).astype(BF)
+
+
+def start_chunk(starts, first, chunk):
+    begin = jnp.int32(0)
+    for start in starts:
+        begin = jnp.where(start <= first, jnp.maximum(begin, start), begin)
+    return begin // chunk
+
+
+def my_chunk():
+    return lax.axis_index("seq") * lax.axis_size("mp") + lax.axis_index("mp")
+
+
+def stack_heads(value, at, heads):
+    return jnp.concatenate([value[at + h * HD : at + (h + 1) * HD] for h in range(heads)], axis=1)
+
+
+def attend_kernel(groups, heads, docs_ref, q_ref, kv_ref, out_ref, lse_ref, qa, ka, va, acc, top):
+    b = pl.program_id(0)
+    own = q_ref.shape[1]
+    ndoc = docs_ref.shape[1]
+    starts = [docs_ref[b, k] for k in range(ndoc)]
+    me = my_chunk()
+    begin = start_chunk(starts, me * own, own)
+    wide = heads * own
+    tied = groups * HD
+    plain = HD - RD
+    q_doc = query_rows(starts, me * own, own)
+    q_doc = jnp.concatenate([q_doc] * heads, axis=1)
+    q_all = q_ref[...]
+    for g in range(groups):
+        qa[g, :HD] = stack_heads(q_all, g * heads * HD, heads)
+        qa[g, HD : HD + 16] = q_doc
+        qa[g, HD + 16 :] = jnp.zeros((LANE - HD - 16, wide), BF)
+    ones = first_rows(1, own)
+    zeros = jnp.zeros((LANE - HD - 16, own), BF)
+
+    def scores(j, g):
+        doc = key_rows(starts, j * own, own)
+        block = jnp.concatenate(
+            [
+                kv_ref[j, 0, g * HD : g * HD + plain],
+                kv_ref[j, 0, tied : tied + RD],
+                doc,
+                zeros,
+            ],
+            axis=0,
+        )
+        return mxu(block.T, qa[g], NN)
+
+    def weighted(j, g, weights):
+        values = jnp.concatenate([kv_ref[j, 0, g * HD : (g + 1) * HD], ones], axis=0)
+        return mxu(values, weights.astype(BF), NN)
+
+    key_at = lax.broadcasted_iota(jnp.int32, (own, own), 0)
+    query_at = lax.broadcasted_iota(jnp.int32, (own, own), 1)
+    causal = jnp.concatenate([key_at <= query_at] * heads, axis=1)
+    for g in range(groups):
+        logits = jnp.where(causal, scores(me, g), masked_value)
+        peak = jnp.max(logits, axis=0, keepdims=True)
+        acc[g] = weighted(me, g, jnp.exp(logits - peak))
+        top[g] = peak
+
+    def step(i, carry):
+        j = me - 1 - i
+        for g in range(groups):
+            logits = scores(j, g)
+            peak = jnp.maximum(top[g], jnp.max(logits, axis=0, keepdims=True))
+            shrink = jnp.exp(top[g] - peak)
+            acc[g] = acc[g] * shrink + weighted(j, g, jnp.exp(logits - peak))
+            top[g] = peak
+        return carry
+
+    lax.fori_loop(0, me - begin, step, 0)
+    for g in range(groups):
+        total = acc[g, HD : HD + 1]
+        result = acc[g, :HD] / total
+        lse_ref[0, g : g + 1] = top[g] + jnp.log(total)
+        for h in range(heads):
+            at = (g * heads + h) * HD
+            out_ref[at : at + HD] = result[:, h * own : (h + 1) * own].astype(BF)
+
+
+def attend_forward(docs, q, kv, groups, heads):
+    chunks, count, kv_rows, own = kv.shape
+    wide = heads * own
+    return pl.pallas_call(
+        functools.partial(attend_kernel, groups, heads),
+        grid=(count,),
+        in_specs=[
+            pl.BlockSpec(memory_space=pltpu.SMEM),
+            pl.BlockSpec((q.shape[0], own), lambda b: (0, b)),
+            pl.BlockSpec((chunks, 1, kv_rows, own), lambda b: (0, b, 0, 0)),
+        ],
+        out_specs=[
+            pl.BlockSpec((q.shape[0], own), lambda b: (0, b)),
+            pl.BlockSpec((1, groups, wide), lambda b: (b, 0, 0)),
+        ],
+        out_shape=[
+            jax.ShapeDtypeStruct(q.shape, BF),
+            jax.ShapeDtypeStruct((count, groups, wide), F32),
+        ],
+        scratch_shapes=[
+            pltpu.VMEM((groups, LANE, wide), BF),
+            pltpu.VMEM((8, LANE), BF),
+            pltpu.VMEM((8, LANE), BF),
+            pltpu.VMEM((groups, HD + 16, wide), F32),
+            pltpu.VMEM((groups, 1, wide), F32),
+        ],
+        compiler_params=params(),
+        name="attend",
+    )(docs, q, kv)
+
+
+def attend_back_kernel(
+    groups, heads, docs_ref, q_ref, do_ref, lse_ref, delta_ref, kv_ref, rot_ref,
+    dq_ref, dkv_ref, qs, qa, ds_, da, dq,
+):
+    b = pl.program_id(0)
+    own = q_ref.shape[1]
+    ndoc = docs_ref.shape[1]
+    starts = [docs_ref[b, k] for k in range(ndoc)]
+    me = my_chunk()
+    begin = start_chunk(starts, me * own, own)
+    wide = heads * own
+    tied = groups * HD
+    plain = HD - RD
+    q_doc = query_rows(starts, me * own, own)
+    q_doc = jnp.concatenate([q_doc] * heads, axis=1)
+    q_all, do_all = q_ref[...], do_ref[...]
+    pad_q = jnp.zeros((LANE - HD - 32, wide), BF)
+    pad_d = jnp.zeros((LANE - HD - 16, wide), BF)
+    for g in range(groups):
+        q_rows = stack_heads(q_all, g * heads * HD, heads)
+        do_rows = stack_heads(do_all, g * heads * HD, heads)
+        qs[g] = q_rows
+        ds_[g] = do_rows
+        lse_rows = three_parts(-lse_ref[0, g : g + 1], wide)
+        delta_row = jnp.concatenate(
+            [delta_ref[0, g * heads + h : g * heads + h + 1] for h in range(heads)], axis=1
+        )
+        delta_rows = three_parts(-delta_row, wide)
+        qa[g] = jnp.concatenate([q_rows, q_doc, lse_rows, pad_q], axis=0).T
+        da[g] = jnp.concatenate([do_rows, delta_rows, pad_d], axis=0).T
+    ones = first_rows(3, own)
+    pad_k = jnp.zeros((LANE - HD - 32, own), BF)
+    pad_v = jnp.zeros((LANE - HD - 16, own), BF)
+
+    def clear(j, carry):
+        dkv_ref[j, 0] = jnp.zeros(dkv_ref.shape[2:], BF)
+        return carry
+
+    lax.fori_loop(0, begin, clear, 0)
+    lax.fori_loop(me + 1, dkv_ref.shape[0], clear, 0)
+
+    def block(j, diagonal):
+        doc = key_rows(starts, j * own, own)
+        rope_rows = kv_ref[j, 0, tied : tied + RD]
+        rope_sum = jnp.zeros((RD, own), F32)
+        for g in range(groups):
+            values = kv_ref[j, 0, g * HD : (g + 1) * HD]
+            keys = jnp.concatenate([values[:plain], rope_rows], axis=0)
+            logits = mxu(qa[g], jnp.concatenate([keys, doc, ones, pad_k], axis=0), NN)
+            weights = jnp.exp(logits)
+            if diagonal:
+                query_at = lax.broadcasted_iota(jnp.int32, (own, own), 0)
+                key_at = lax.broadcasted_iota(jnp.int32, (own, own), 1)
+                causal = jnp.concatenate([key_at <= query_at] * heads, axis=0)
+                weights = jnp.where(causal, weights, 0.0)
+            slopes = mxu(da[g], jnp.concatenate([values, ones, pad_v], axis=0), NN)
+            grads = (weights * slopes).astype(BF)
+            grad_values = mxu(ds_[g], weights.astype(BF), NN)
+            grad_keys = mxu(qs[g], grads, NN)
+            grad_queries = mxu(grads, keys.T, NN)
+            if diagonal:
+                dq[g] = grad_queries
+            else:
+                dq[g] += grad_queries
+            dkv_ref[j, 0, g * HD : g * HD + plain] = (
+                grad_values[:plain] + grad_keys[:plain]
+            ).astype(BF)
+            dkv_ref[j, 0, g * HD + plain : (g + 1) * HD] = grad_values[plain:].astype(BF)
+            rope_sum = rope_sum + grad_keys[plain:]
+        dkv_ref[j, 0, tied : tied + RD] = rope_sum.astype(BF)
+
+    block(me, True)
+
+    def step(j, carry):
+        block(j, False)
+        return carry
+
+    lax.fori_loop(begin, me, step, 0)
+    straight, ahead, behind = rot_ref[0], rot_ref[1], rot_ref[2]
+    half = RD // 2
+    for g in range(groups):
+        for pair in range(heads // 2):
+            at = 2 * pair * own
+            both = jnp.concatenate([dq[g, at : at + own], dq[g, at + own : at + 2 * own]], axis=1)
+            both = both * HD ** (-0.5)
+            turned = (
+                both * straight
+                + pltpu.roll(both, LANE - half, 1) * ahead
+                + pltpu.roll(both, half, 1) * behind
+            )
+            to = (g * heads + 2 * pair) * HD
+            dq_ref[:, to : to + 2 * HD] = turned.astype(BF)
+
+
+def attend_backward(docs, q, do, lse, delta, kv, turns, groups, heads):
+    chunks, count, kv_rows, own = kv.shape
+    wide = heads * own
+    width = q.shape[0]
+    return pl.pallas_call(
+        functools.partial(attend_back_kernel, groups, heads),
+        grid=(count,),
+        in_specs=[
+            pl.BlockSpec(memory_space=pltpu.SMEM),
+            pl.BlockSpec((width, own), lambda b: (0, b)),
+            pl.BlockSpec((width, own), lambda b: (0, b)),
+            pl.BlockSpec((1, groups, wide), lambda b: (b, 0, 0)),
+            pl.BlockSpec((1, groups * heads, own), lambda b: (b, 0, 0)),
+            pl.BlockSpec((chunks, 1, kv_rows, own), lambda b: (0, b, 0, 0)),
+            pl.BlockSpec(turns.shape, lambda b: (0, 0, 0)),
+        ],
+        out_specs=[
+            pl.BlockSpec((own, width), lambda b: (b, 0)),
+            pl.BlockSpec((chunks, 1, kv_rows, own), lambda b: (0, b, 0, 0)),
+        ],
+        out_shape=[
+            jax.ShapeDtypeStruct((count * own, width), BF),
+            jax.ShapeDtypeStruct(kv.shape, BF),
+        ],
+        scratch_shapes=[
+            pltpu.VMEM((groups, HD, wide), BF),
+            pltpu.VMEM((groups, wide, LANE), BF),
+            pltpu.VMEM((groups, HD, wide), BF),
+            pltpu.VMEM((groups, wide, LANE), BF),
+            pltpu.VMEM((groups, wide, HD), F32),
+        ],
+        compiler_params=params(),
+        name="attend_back",
+    )(docs, q, do, lse, delta, kv, turns)
+
+
+def load_weights(refs, targets, sems):
+    copies = []
+    slot = 0
+    for (source, side, axis), target in zip(refs, targets, strict=True):
+        blocks = source.shape[axis] // LANE
+        for t in range(blocks):
+            to = pl.ds((2 * t + side) * LANE, LANE)
+            of = pl.ds(t * LANE, LANE)
+            src = source.at[:, of] if axis == 1 else source.at[of]
+            dst = target.at[:, to] if axis == 1 else target.at[to]
+            copies.append(pltpu.make_async_copy(src, dst, sems.at[slot]))
+            slot += 1
+    return copies
+
+
+def feed_kernel(
+    x_ref, og_ref, o_ref, gain_ref, wo_ref, wgo_ref, wgp_ref, wuo_ref, wup_ref, wdo_ref, wdp_ref,
+    out_ref, nt_ref, ogt_ref, act_ref, gg_ref, gu_ref, gh_ref, gat_ref, do_ref, delta_ref, gg2_ref,
+    wo, wg, wu, wd, sems,
+):
+    b = pl.program_id(0)
+
+    @pl.when(b == 0)
+    def _():
+        copies = [pltpu.make_async_copy(wo_ref, wo, sems.at[sems.shape[0] - 1])]
+        copies += load_weights(
+            [
+                (wgo_ref, 0, 1), (wgp_ref, 1, 1), (wuo_ref, 0, 1), (wup_ref, 1, 1),
+                (wdo_ref, 0, 0), (wdp_ref, 1, 0),
+            ],
+            [wg, wg, wu, wu, wd, wd],
+            sems,
+        )
+        for copy in copies:
+            copy.start()
+        for copy in copies:
+            copy.wait()
+        gg2_ref[...] = jnp.zeros(gg2_ref.shape, F32)
+
+    og = og_ref[0]
+    heads_out = o_ref[...]
+    gain = gain_ref[...]
+    hidden = x_ref[0].astype(F32) + mxu(heads_out, wo[...], TN)
+    inverse = lax.rsqrt(jnp.mean(hidden * hidden, axis=-1, keepdims=True) + epsilon)
+    normed = (hidden * inverse * gain).astype(BF)
+    nt_ref[...] = normed.T
+    ogt_ref[...] = og.T
+    units = wg.shape[1]
+    tile = 2 * LANE
+    for t in range(units // tile):
+        at = slice(t * tile, (t + 1) * tile)
+        gate = mxu(normed, wg[:, at], NN)
+        up = mxu(normed, wu[:, at], NN)
+        grad = mxu(og, wd[at], NT)
+        sigmoid = 1.0 / (1.0 + jnp.exp(-gate))
+        silu = gate * sigmoid
+        act_ref[:, at] = (silu * up).astype(BF)
+        gu_ref[:, at] = (grad * silu).astype(BF)
+        gg_ref[:, at] = (grad * up * (sigmoid + silu * (1.0 - sigmoid))).astype(BF)
+    result = mxu(act_ref[...], wd[...], NN)
+    out_ref[0] = (hidden + result).astype(BF)
+    grad_normed = mxu(gg_ref[...], wg[...], NT) + mxu(gu_ref[...], wu[...], NT)
+    scaled = grad_normed * gain
+    gg2_ref[...] += jnp.sum(grad_normed * (hidden * inverse), axis=0, keepdims=True)
+    mean = jnp.mean(scaled * hidden, axis=-1, keepdims=True)
+    grad_hidden = og.astype(F32) + inverse * scaled - hidden * (inverse * inverse * inverse * mean)
+    gh_ref[0] = grad_hidden
+    grad_attended = grad_hidden.astype(BF)
+    gat_ref[...] = grad_attended.T
+    grad_heads = mxu(wo[...], grad_attended, NT).astype(BF)
+    do_ref[...] = grad_heads
+    product = grad_heads.astype(F32) * heads_out.astype(F32)
+    for h in range(product.shape[0] // HD):
+        delta_ref[0, h : h + 1] = jnp.sum(product[h * HD : (h + 1) * HD], axis=0, keepdims=True)
+
+
+def feed(x, og, heads_out, gain, wo, wg, wu, wd):
+    count, own, width = x.shape
+    hd = heads_out.shape[0]
+    half = wg[0].shape[1]
+    units = 2 * half
+    tokens = count * own
+    seq = pl.BlockSpec((1, own, width), lambda b: (b, 0, 0))
+    column = lambda rows: pl.BlockSpec((rows, own), lambda b: (0, b))
+    row = pl.BlockSpec((own, units), lambda b: (b, 0))
+    hbm = pl.BlockSpec(memory_space=pl.ANY)
+    return pl.pallas_call(
+        feed_kernel,
+        grid=(count,),
+        in_specs=[seq, seq, column(hd), pl.BlockSpec((1, width), lambda b: (0, 0))] + [hbm] * 7,
+        out_specs=[
+            seq, column(width), column(width), row, row, row, seq, column(width), column(hd),
+            pl.BlockSpec((1, hd // HD, own), lambda b: (b, 0, 0)),
+            pl.BlockSpec((1, width), lambda b: (0, 0)),
+        ],
+        out_shape=[
+            jax.ShapeDtypeStruct(x.shape, BF),
+            jax.ShapeDtypeStruct((width, tokens), BF),
+            jax.ShapeDtypeStruct((width, tokens), BF),
+            jax.ShapeDtypeStruct((tokens, units), BF),
+            jax.ShapeDtypeStruct((tokens, units), BF),
+            jax.ShapeDtypeStruct((tokens, units), BF),
+            jax.ShapeDtypeStruct(x.shape, F32),
+            jax.ShapeDtypeStruct((width, tokens), BF),
+            jax.ShapeDtypeStruct((hd, tokens), BF),
+            jax.ShapeDtypeStruct((count, hd // HD, own), F32),
+            jax.ShapeDtypeStruct((1, width), F32),
+        ],
+        scratch_shapes=[
+            pltpu.VMEM((hd, width), BF),
+            pltpu.VMEM((width, units), BF),
+            pltpu.VMEM((width, units), BF),
+            pltpu.VMEM((units, width), BF),
+            pltpu.SemaphoreType.DMA((6 * (half // LANE) + 1,)),
+        ],
+        compiler_params=params(),
+        name="feed",
+    )(x, og, heads_out, gain, wo, *wg, *wu, *wd)
+
+
+def unit_grads_kernel(left_ref, right_ref, own_ref, other_ref):
+    product = mxu(left_ref[...], right_ref[...], NN).astype(BF)
+    own_ref[...] = product[:, :LANE]
+    other_ref[...] = product[:, LANE:]
+
+
+def unit_grads(left, right):
+    width, tokens = left.shape
+    units = right.shape[1]
+    tile = 2 * LANE
+    part = pl.BlockSpec((width, LANE), lambda t: (0, t))
+    return pl.pallas_call(
+        unit_grads_kernel,
+        grid=(units // tile,),
+        in_specs=[
+            pl.BlockSpec((width, tokens), lambda t: (0, 0)),
+            pl.BlockSpec((tokens, tile), lambda t: (0, t)),
+        ],
+        out_specs=[part, part],
+        out_shape=[jax.ShapeDtypeStruct((width, units // 2), BF)] * 2,
+        compiler_params=params(),
+        name="unit_grads",
+    )(left, right)
+
+
+def plain_grads_kernel(dims, left_ref, right_ref, out_ref):
+    out_ref[...] = mxu(left_ref[...], right_ref[...], dims).astype(BF)
+
+
+def plain_grads(left, right, dims):
+    rows, tokens = left.shape
+    columns = right.shape[1] if dims == NN else right.shape[0]
+    tile = 2 * LANE
+    if dims == NN:
+        spec = pl.BlockSpec((tokens, tile), lambda t: (0, t))
+    else:
+        spec = pl.BlockSpec((tile, tokens), lambda t: (t, 0))
+    return pl.pallas_call(
+        functools.partial(plain_grads_kernel, dims),
+        grid=(columns // tile,),
+        in_specs=[pl.BlockSpec((rows, tokens), lambda t: (0, 0)), spec],
+        out_specs=pl.BlockSpec((rows, tile), lambda t: (0, t)),
+        out_shape=jax.ShapeDtypeStruct((rows, columns), BF),
+        compiler_params=params(),
+        name="plain_grads",
+    )(left, right)
+
+
+def finish_kernel(
+    x_ref, gh_ref, dq_ref, dkv_ref, nt_ref, gain_ref, w_ref, cos_ref, sin_ref,
+    gi_ref, gg1_ref, dw_ref,
+):
+    b = pl.program_id(0)
+
+    @pl.when(b == 0)
+    def _():
+        gg1_ref[...] = jnp.zeros(gg1_ref.shape, F32)
+        dw_ref[...] = jnp.zeros(dw_ref.shape, F32)
+
+    rows = w_ref.shape[0]
+    kv_rows = dkv_ref.shape[1]
+    tied = kv_rows - RD
+    summed = dkv_ref[0].astype(F32)
+    turned = rotate_rows(summed[tied:], cos_ref[...], -sin_ref[...])
+    dkv = jnp.concatenate([summed[:tied], turned], axis=0).astype(BF)
+    grad_normed = mxu(dq_ref[...], w_ref[: rows - kv_rows], NN)
+    grad_normed = grad_normed + mxu(dkv, w_ref[rows - kv_rows :], TN)
+    dw_ref[...] += mxu(nt_ref[...], dkv, NT)
+    x = x_ref[0].astype(F32)
+    inverse = lax.rsqrt(jnp.mean(x * x, axis=-1, keepdims=True) + epsilon)
+    scaled = grad_normed * gain_ref[...]
+    gg1_ref[...] += jnp.sum(grad_normed * (x * inverse), axis=0, keepdims=True)
+    mean = jnp.mean(scaled * x, axis=-1, keepdims=True)
+    gi_ref[0] = gh_ref[0] + inverse * scaled - x * (inverse * inverse * inverse * mean)
+
+
+def finish(x, grad_hidden, dq, dkv, nt, gain, weights, cosine, sine_table):
+    count, own, width = x.shape
+    kv_rows = dkv.shape[1]
+    seq = pl.BlockSpec((1, own, width), lambda b: (b, 0, 0))
+    whole = lambda b: (0, 0)
+    return pl.pallas_call(
+        finish_kernel,
+        grid=(count,),
+        in_specs=[
+            seq, seq,
+            pl.BlockSpec((own, dq.shape[1]), lambda b: (b, 0)),
+            pl.BlockSpec((1, kv_rows, own), lambda b: (b, 0, 0)),
+            pl.BlockSpec((width, own), lambda b: (0, b)),
+            pl.BlockSpec((1, width), whole),
+            pl.BlockSpec(weights.shape, whole),
+            pl.BlockSpec(cosine.shape, whole),
+            pl.BlockSpec(cosine.shape, whole),
+        ],
+        out_specs=[
+            seq, pl.BlockSpec((1, width), whole), pl.BlockSpec((width, kv_rows), whole),
+        ],
+        out_shape=[
+            jax.ShapeDtypeStruct(x.shape, F32),
+            jax.ShapeDtypeStruct((1, width), F32),
+            jax.ShapeDtypeStruct((width, kv_rows), F32),
+        ],
+        compiler_params=params(),
+        name="finish",
+    )(x, grad_hidden, dq, dkv, nt, gain, weights, cosine, sine_table)
+
+
+def turn_tables(cosine, sine_table):
+    plain = HD - RD
+    one = jnp.ones((cosine.shape[0], plain), F32)
+    none = jnp.zeros_like(one)
+    quiet = jnp.zeros_like(sine_table)
+    straight = jnp.concatenate([one, cosine, cosine], axis=1)
+    ahead = jnp.concatenate([none, sine_table, quiet], axis=1)
+    behind = jnp.concatenate([none, quiet, -sine_table], axis=1)
+    return jnp.stack([jnp.concatenate([t, t], axis=1) for t in (straight, ahead, behind)])
+
+
+def on_device_fast(
+    inputs, gain_one, w_query, w_tied, w_rope, w_out, gain_two, w_gate, w_up, w_down,
+    doc_starts, out_grad,
+):
+    count, own, width = inputs.shape
+    cores = lax.axis_size("mp")
+    groups = cores * w_tied.shape[1] // HD
+    all_heads = cores * w_query.shape[1] // HD
+    heads = all_heads // groups
+    mp_index = lax.axis_index("mp")
+    query_t, tied_t = w_query.T, w_tied.T
+    tied_both = by_core(tied_t, swap_cores(tied_t), 0)
+    query_both = by_core(query_t, swap_cores(query_t), 0)
+    weights_one = jnp.concatenate([query_both, tied_both, w_rope.T], axis=0)
+    out_other = swap_cores(w_out)
+    gate_other, up_other, down_other = swap_cores(w_gate), swap_cores(w_up), swap_cores(w_down)
+    gain_one_float = gain_one.astype(F32)[None]
+    gain_two_float = gain_two.astype(F32)[None]
+    cosine, sine_table = rope_tables(my_chunk() * own, own, RD)
+    cosine_t, sine_t = cosine.T, sine_table.T
+    q, kv, normed_t = project(inputs, gain_one_float, weights_one, cosine_t, sine_t, all_heads)
+    kv_all = lax.all_gather(kv, ("seq", "mp"), axis=0, tiled=False)
+    heads_out, lse = attend_forward(doc_starts, q, kv_all, groups, heads)
+    out_both = by_core(w_out, out_other, 0)
+    (
+        outputs, normed_two_t, out_grad_t, active, grad_gate, grad_up, grad_hidden, grad_attended_t,
+        grad_heads, delta, grad_gain_two,
+    ) = feed(
+        inputs, out_grad, heads_out, gain_two_float, out_both, (w_gate, gate_other),
+        (w_up, up_other), (w_down, down_other),
+    )
+    unit_own, unit_other = [], []
+    for left, right in (
+        (normed_two_t, grad_gate), (normed_two_t, grad_up), (out_grad_t, active),
+    ):
+        own_part, other_part = unit_grads(left, right)
+        unit_own.append(own_part)
+        unit_other.append(swap_cores(other_part))
+    unit_sum = jnp.concatenate([a + c for a, c in zip(unit_own, unit_other)], axis=1)
+    unit_scattered = lax.psum_scatter(unit_sum, ("dp", "seq"), scatter_dimension=0, tiled=True)
+
+    dq, dkv = attend_backward(
+        doc_starts, q, grad_heads, lse, delta, kv_all, turn_tables(cosine, sine_table), groups, heads
+    )
+    dkv_own = lax.psum_scatter(dkv, ("seq", "mp"), scatter_dimension=0, tiled=False)
+    grad_out = plain_grads(grad_attended_t, heads_out, NT)
+    grad_query = plain_grads(normed_t, dq, NN)
+    grad_inputs, grad_gain_one, grad_kv = finish(
+        inputs, grad_hidden, dq, dkv_own, normed_t, gain_one_float, weights_one, cosine_t, sine_t
+    )
+    tied = groups * HD
+    grad_tied = grad_kv[:, :tied].astype(BF)
+    late_own, late_other = [], []
+    for value in (grad_query, grad_tied, grad_out):
+        half = value.shape[1] // cores
+        late_own.append(lax.dynamic_slice_in_dim(value, mp_index * half, half, 1))
+        late_other.append(lax.dynamic_slice_in_dim(value, (1 - mp_index) * half, half, 1))
+    late = jnp.concatenate(late_own, axis=1) + swap_cores(jnp.concatenate(late_other, axis=1))
+    late_sum = lax.psum_scatter(late, ("dp", "seq"), scatter_dimension=0, tiled=True)
+    small = jnp.concatenate([grad_kv[:, tied:], grad_gain_one.T, grad_gain_two.T], axis=1)
+    small_sum = lax.psum_scatter(small, ("dp", "seq", "mp"), scatter_dimension=0, tiled=True)
+    unit_scattered = unit_scattered.astype(F32)
+    late_sum = late_sum.astype(F32)
+    half_units = w_gate.shape[1]
+    query_half, tied_half = w_query.shape[1], w_tied.shape[1]
+    return (
+        outputs,
+        grad_inputs,
+        small_sum[:, RD],
+        late_sum[:, :query_half],
+        late_sum[:, query_half : query_half + tied_half],
+        small_sum[:, :RD],
+        late_sum[:, query_half + tied_half :].T,
+        small_sum[:, RD + 1],
+        unit_scattered[:, :half_units],
+        unit_scattered[:, half_units : 2 * half_units],
+        unit_scattered[:, 2 * half_units :].T,
+    )
+
+
 def solution(mesh):
     in_specs = (
         P("dp", ("seq", "mp"), None),
@@ -360,6 +1045,11 @@
         P(("dp", "seq"), "mp"),
         P("mp", ("dp", "seq")),
     )
+
+    def local(inputs, *rest):
+        step = on_device_fast if inputs.shape[1] % (2 * LANE) == 0 else on_device
+        return step(inputs, *rest)
+
     return jax.shard_map(
-        on_device, mesh=mesh, in_specs=in_specs, out_specs=out_specs, check_vma=False
-    )
+        local, mesh=mesh, in_specs=in_specs, out_specs=out_specs, check_vma=False
+    )

time: 2580 us -> 940 us (0.36)
  matrix products: 1170 us -> 0 us
  other arithmetic: 416 us -> 29.8 us
  Pallas kernels: 0 us -> 260 us
  waiting for transfers between devices: 817 us -> 579 us
  local copies, waits for them, and re-layouts: 106 us -> 20.5 us
  blocking collectives: 42.6 us -> 0 us
  starting transfers between devices: 1.38 us -> 39.7 us
    dot_general x77 -> x0, matrix products: 1170 us -> none  [the longest x8 189 us: attend_back(): jnp.einsum('qghd,kgd->ghqk', grad_heads, values, preferred_element_type=j...]
    reduce_scatter x14 -> x3, waiting for transfers between devices: 708 us -> 421 us  [the longest x1 168 us: on_device_fast(): lax.psum_scatter(unit_sum, ('dp', 'seq'), scatter_dimension=0, tiled=True)]
    pallas_call x0 -> x10, Pallas kernels: none -> 260 us  [the longest x1 102 us: feed(): pl.pallas_call(feed_kernel, grid=(count,), in_specs=[seq, seq, column(hd)...]
    convert_element_type x15 -> x2, other arithmetic: 243 us -> 2.05 us  [the longest x1 1.12 us: on_device_fast(): unit_scattered = unit_scattered.astype(F32)]
    reduce_sum x20 -> x0, other arithmetic: 131 us -> none  [the longest x8 115 us: attend(): row_total = jnp.sum(weights, axis=-1, keepdims=True)]
    unnamed x20 -> x6, waiting for transfers between devices: 0.83 us -> 99.7 us
    all_gather x6 -> x1, waiting for transfers between devices: 109 us -> 42.9 us  [on_device_fast(): kv_all = lax.all_gather(kv, ('seq', 'mp'), axis=0, tiled=False)]
    unnamed x1 -> x0, blocking collectives: 42.6 us -> none
  transfers between devices with their start and end apart: 20 -> 15, of which waited for: 15 -> 7; matrix products, arithmetic and copies ran while one was open for 10% -> 4% of each run, Pallas kernels for 0% -> 9%
where the time goes in v1:
time: 940 us; the launch traced here: 943 us
  waiting for transfers between devices  579 us (62%)
  Pallas kernels  260 us (28%)
  starting transfers between devices  39.7 us (4%)
  other arithmetic  29.8 us (3%)
  local copies, waits for them, and re-layouts  20.5 us (2%)
  between operations  14 us (1%)
    reduce_scatter x1, waiting for transfers between devices, on_device_fast(): lax.psum_scatter(unit_sum, ('dp', 'seq'), scatter_dimension=0, tiled=True)  168 us
    reduce_scatter x1, waiting for transfers between devices, on_device_fast(): lax.psum_scatter(late, ('dp', 'seq'), scatter_dimension=0, tiled=True)  129 us
    reduce_scatter x1, waiting for transfers between devices, on_device_fast(): lax.psum_scatter(dkv, ('seq', 'mp'), scatter_dimension=0, tiled=False)  124 us
    pallas_call x1, Pallas kernels, feed(): pl.pallas_call(feed_kernel, grid=(count,), in_specs=[seq, seq, column(hd)...  102 us
    unnamed x6, waiting for transfers between devices  99.7 us
    pallas_call x3, Pallas kernels, unit_grads(): pl.pallas_call(unit_grads_kernel, grid=(units // tile,), in_specs=[pl.Blo...  54.4 us
    all_gather x1, waiting for transfers between devices, on_device_fast(): kv_all = lax.all_gather(kv, ('seq', 'mp'), axis=0, tiled=False)  42.9 us
    ppermute x10, starting transfers between devices, swap_cores(): return lax.ppermute(value, 'mp', [(0, 1), (1, 0)])  39.4 us
  transfers between devices with their start and end apart: 15, of which 7 were waited for; matrix products, arithmetic and copies ran while one was open for 4% of the time, Pallas kernels for 9%

profile of v1, /device:TPU:0, one launch (start us, length us, event | category | flops | bytes accessed | tf_op | source)
XLA Modules:
  0.0 942.9 jit_solution(7544242698980109191)
XLA Ops:
  7.2 1.5 copy.37
  8.7 0.5 collective-permute-start
  9.2 1.1 copy.38
  10.3 0.1 collective-permute-start.1
  10.5 1.3 broadcast_in_dim.28
  11.7 0.8 multiply_sine_fusion.1
  12.5 0.4 select_dynamic-update-slice_fusion.1
  12.9 0.4 select_dynamic-update-slice_fusion
  13.5 0.3 copy-done.7
  13.8 1.5 copy-done
  15.3 12.7 %project.1 = (bf16[1024,2048]{1,0:T(8,128)(2,1)}, bf16[8,288,256]{2,1,0:T(8,128)(2,1)}, bf16[1024,2048]{1,0:T(8,128)(2,1)}) custom-call(bf16[8,256,1024]{2,1,0:T(8,128)(2,1)} %x_ref.5, f32[1,1024]{1,0:T(1,128)} %bitcast.34, bf16[1312,1024]{1,0:T(8,128)(2,1)} %copy-done, f32[16,256]{1,0:T(8,128)} %get-tuple-element.114.cos_ref, ...), custom_call_target="tpu_custom_call" | custom-call | tf_op jit(solution)/shard_map/project/pallas_call | solution.py:399
  28.0 0.5 collective-permute-start.3
  28.6 0.1 collective-permute-start.4
  28.6 0.4 collective-permute-start.5
  29.1 0.1 collective-permute-start.2
  29.2 0.6 broadcast_in_dim.29
  29.8 0.5 multiply_cosine_fusion
  30.3 0.9 concatenate.36
  31.2 0.2 concatenate.37
  31.5 0.2 concatenate.35
  31.7 1.7 pad_maximum_fusion.3.rot_ref
  33.4 10.1 %collective-permute-done.2 = bf16[512,1024]{1,0:T(8,128)(2,1)} collective-permute-done((bf16[512,1024]{1,0:T(8,128)(2,1)}, bf16[512,1024]{1,0:T(8,128)(2,1)}, u32[]{:S(2)}, u32[]{:S(2)}) %collective-permute-start.2) | collective-permute-done | bytes 1048608 | tf_op jit(solution)/shard_map/ppermute | solution.py:358
  43.6 1.7 broadcast_select_fusion.1
  45.2 1.5 pad_maximum_fusion.2.wo_ref
  46.8 42.9 %all-gather.3.cloned.1.call-done = bf16[64,288,256]{2,1,0:T(8,128)(2,1)} async-done(((bf16[8,288,256]{2,1,0:T(8,128)(2,1)}), bf16[64,288,256]{2,1,0:T(8,128)(2,1)}) %all-gather.3.cloned.1.call-update) | async-done | bytes 9437200 | tf_op jit(solution)/shard_map/all_gather | solution.py:961
  89.7 17.7 %attend.1 = (bf16[1024,2048]{1,0:T(8,128)(2,1)}, f32[8,4,1024]{2,1,0:T(4,128)}) custom-call(s32[8,8]{1,0:T(8,128)} %docs_ref.3, bf16[1024,2048]{1,0:T(8,128)(2,1)} %get-tuple-element.38.q_ref, bf16[8,8,288,256]{3,2,1,0:T(8,128)(2,1)} %bitcast.25), custom_call_target="tpu_custom_call" | custom-call | tf_op jit(solution)/shard_map/attend/pallas_call | solution.py:544
  107.4 101.7 %feed.1 = (bf16[8,256,1024]{2,1,0:T(8,128)(2,1)}, bf16[1024,2048]{1,0:T(8,128)(2,1)}, bf16[1024,2048]{1,0:T(8,128)(2,1)}, bf16[2048,2816]{1,0:T(8,128)(2,1)}, bf...) custom-call(bf16[8,256,1024]{2,1,0:T(8,128)(2,1)} %x_ref.5, ...), custom_call_target="tpu_custom_call" | custom-call | tf_op jit(solution)/shard_map/feed/pallas_call | solution.py:788
  209.1 38.6 %attend_back.1 = (bf16[2048,1024]{1,0:T(8,128)(2,1)}, bf16[8,8,288,256]{3,2,1,0:T(8,128)(2,1)}) custom-call(s32[8,8]{1,0:T(8,128)} %docs_ref.3, bf16[1024,2048]{1,0:T(8,128)(2,1)} %get-tuple-element.38.q_ref, bf16[1024,2048]{1,0:T(8,128)(2,1)} %get-tuple-element.43.do_ref, f32[8,4,1024]{2,1,0:T(4,128)} %get-tuple-element.44.lse_ref, ...), custom_call_target="tpu_custom_call" | custom-call | tf_op jit(solution)/shard_map/attend_back/pallas_call | solution.py:670
  247.8 18.1 %unit_grads.3 = (bf16[1024,1408]{1,0:T(8,128)(2,1)}, bf16[1024,1408]{1,0:T(8,128)(2,1)}) custom-call(bf16[1024,2048]{1,0:T(8,128)(2,1)} %get-tuple-element.54.left_ref, bf16[2048,2816]{1,0:T(8,128)(2,1)} %get-tuple-element.55.right_ref), custom_call_target="tpu_custom_call" | custom-call | tf_op jit(solution)/shard_map/unit_grads/pallas_call | solution.py:833
  265.9 37.1 %collective-permute-start.7 = (bf16[1024,1408]{1,0:T(8,128)(2,1)}, bf16[1024,1408]{1,0:T(8,128)(2,1)S(1)}, u32[]{:S(2)}, u32[]{:S(2)}) collective-permute-start(bf16[1024,1408]{1,0:T(8,128)(2,1)} %get-tuple-element.57), channel_id=1, source_target_pairs={{0,1},{1,0},{2,3},{3,2},{4,5},{5,4},{6,7},{7,6},{8,9},{9,8},{10,11... | collective-permute-start | bytes 8650760 | tf_op jit(solution)/shard_map/ppermute | solution.py:358
  303.0 18.1 %unit_grads.4 = (bf16[1024,1408]{1,0:T(8,128)(2,1)}, bf16[1024,1408]{1,0:T(8,128)(2,1)}) custom-call(bf16[1024,2048]{1,0:T(8,128)(2,1)} %get-tuple-element.54.left_ref, bf16[2048,2816]{1,0:T(8,128)(2,1)} %get-tuple-element.58.right_ref), custom_call_target="tpu_custom_call" | custom-call | tf_op jit(solution)/shard_map/unit_grads/pallas_call | solution.py:833
  321.1 18.2 %unit_grads.5 = (bf16[1024,1408]{1,0:T(8,128)(2,1)}, bf16[1024,1408]{1,0:T(8,128)(2,1)}) custom-call(bf16[1024,2048]{1,0:T(8,128)(2,1)} %get-tuple-element.61.left_ref, bf16[2048,2816]{1,0:T(8,128)(2,1)} %get-tuple-element.62.right_ref), custom_call_target="tpu_custom_call" | custom-call | tf_op jit(solution)/shard_map/unit_grads/pallas_call | solution.py:833
  339.3 0.5 collective-permute-start.9
  339.8 1.6 copy-done.5
  341.4 2.7 add.55
  344.1 4.2 add.56
  348.3 2.4 add.57
  350.7 123.8 %reduce-scatter.7.cloned.1.call-done = bf16[1,8,288,256]{3,2,1,0:T(8,128)(2,1)} async-done(((bf16[8,8,288,256]{3,2,1,0:T(8,128)(2,1)}), bf16[1,8,288,256]{3,2,1,0:T(8,128)(2,1)}) %reduce-scatter.7.cloned.1.call-update) | async-done | bytes 1179664 | tf_op jit(solution)/shard_map/reduce_scatter | solution.py:984
  474.5 17.9 %finish.1 = (f32[8,256,1024]{2,1,0:T(8,128)}, f32[1,1024]{1,0:T(1,128)}, f32[1024,288]{1,0:T(8,128)}) custom-call(bf16[8,256,1024]{2,1,0:T(8,128)(2,1)} %x_ref.5, f32[8,256,1024]{2,1,0:T(8,128)} %get-tuple-element.42.gh_ref, bf16[2048,1024]{1,0:T(8,128)(2,1)} %get-tuple-element.46.dq_ref.right_ref, bf16[8,288,256]{2,1,0:T(8,128)(2,1)} %bitcast.29, ...), custom_call_target="tpu_custom_call" | custom-call | tf_op jit(solution)/shard_map/finish/pallas_call | solution.py:903
  492.3 1.1 slice.34
  493.4 0.2 copy.40
  493.6 0.7 pad_maximum_fusion.4
  494.3 1.1 copy.42
  495.4 6.4 pad_maximum_fusion
  501.9 8.6 plain_grads.2
  510.6 8.8 plain_grads.3
  519.4 1.9 constant_dynamic-slice_fusion.3
  521.3 1.3 slice.58
  522.7 0.2 pad_maximum_fusion.1
  522.9 0.1 collective-permute-start.6
  523.0 4.5 collective-permute-done.6
  527.5 2.1 maximum_add_fusion
  529.6 99.7 %reduce-scatter.13.cloned.1.call-done = f32[32,34]{1,0:T(8,128)} async-done(((f32[1024,34]{1,0:T(8,128)}), f32[32,34]{1,0:T(8,128)}) %reduce-scatter.13.cloned.1.call-update) | async-done | bytes 4368
  629.3 0.9 fusion.2
  630.2 0.6 copy.44
  630.7 0.6 copy.46
  631.3 168.4 %reduce-scatter.11.cloned.1.call-done = bf16[64,4224]{1,0:T(8,128)(2,1)} async-done(((bf16[1024,4224]{1,0:T(8,128)(2,1)}), bf16[64,4224]{1,0:T(8,128)(2,1)}) %reduce-scatter.11.cloned.1.call-update) | async-done | bytes 540688 | tf_op jit(solution)/shard_map/reduce_scatter | solution.py:979
  799.7 1.1 convert_element_type.18
  800.8 2.0 fusion.1
  802.9 129.1 %reduce-scatter.9.cloned.1.call-done = bf16[64,1152]{1,0:T(8,128)(2,1)} async-done(((bf16[1024,1152]{1,0:T(8,128)(2,1)}), bf16[64,1152]{1,0:T(8,128)(2,1)}) %reduce-scatter.9.cloned.1.call-update) | async-done | bytes 147472 | tf_op jit(solution)/shard_map/reduce_scatter | solution.py:998
  932.0 0.9 convert_element_type.17
  932.9 0.7 slice_bitcast_fusion.1
  933.6 1.5 slice.47
  935.1 1.3 slice.48
  (45 shorter events, 0.6 us)
Async XLA Ops:
  7.2 82.5 %all-gather.3.cloned.1.call-start = ((), (), s32[]{:S(2)}) async-start(), calls=%async_computation.7 | async-start | bytes 10616832 | tf_op jit(solution)/shard_map/all_gather | solution.py:961
  8.7 3.8 collective-permute-start
  10.3 3.0 collective-permute-start.1
  12.9 0.8 copy-start.7
  13.8 1.5 copy-start
  15.3 12.7 %copy-start.6 = (bf16[1024,1408]{1,0:T(8,128)(2,1)S(1)}, bf16[1024,1408]{1,0:T(8,128)(2,1)}, u32[]{:S(2)}) copy-start(bf16[1024,1408]{1,0:T(8,128)(2,1)} %wgo_ref.1) | copy-start | bytes 8650756
  15.3 13.8 %copy-start.9 = (bf16[1024]{0:T(1024)(128)(2,1)S(1)}, bf16[1024]{0:T(1024)(128)(2,1)}, u32[]{:S(2)}) copy-start(bf16[1024]{0:T(1024)(128)(2,1)} %param.18) | copy-start | bytes 6148
  28.0 446.5 %reduce-scatter.7.cloned.1.call-start = ((), (), s32[]{:S(2)}) async-start(), calls=%async_computation.4 | async-start | bytes 10616832 | tf_op jit(solution)/shard_map/reduce_scatter | solution.py:984
  28.0 79.3 %collective-permute-start.3 = (bf16[1024,1408]{1,0:T(8,128)(2,1)S(1)}, bf16[1024,1408]{1,0:T(8,128)(2,1)}, u32[]{:S(2)}, u32[]{:S(2)}) collective-permute-start(bf16[1024,1408]{1,0:T(8,128)(2,1)S(1)} %copy-done.6), channel_id=1, source_target_pairs={{0,1},{1,0},{2,3},{3,2},{4,5},{5,4},{6,7},{7,6},{8,9},{9,8},{10,11... | collective-permute-start | bytes 8650760 | tf_op jit(solution)/shard_map/ppermute | solution.py:358
  28.6 78.8 %collective-permute-start.4 = (bf16[1024,1408]{1,0:T(8,128)(2,1)}, bf16[1024,1408]{1,0:T(8,128)(2,1)}, u32[]{:S(2)}, u32[]{:S(2)}) collective-permute-start(bf16[1024,1408]{1,0:T(8,128)(2,1)} %wuo_ref.1), channel_id=1, source_target_pairs={{0,1},{1,0},{2,3},{3,2},{4,5},{5,4},{6,7},{7,6},{8,9},{9,8},{10,11... | collective-permute-start | bytes 8650760 | tf_op jit(solution)/shard_map/ppermute | solution.py:358
  28.6 78.7 %collective-permute-start.5 = (bf16[1408,1024]{1,0:T(8,128)(2,1)}, bf16[1408,1024]{1,0:T(8,128)(2,1)}, u32[]{:S(2)}, u32[]{:S(2)}) collective-permute-start(bf16[1408,1024]{1,0:T(8,128)(2,1)} %wdo_ref.1), channel_id=1, source_target_pairs={{0,1},{1,0},{2,3},{3,2},{4,5},{5,4},{6,7},{7,6},{8,9},{9,8},{10,11... | collective-permute-start | bytes 8650760 | tf_op jit(solution)/shard_map/ppermute | solution.py:358
  29.1 14.5 %collective-permute-start.2 = (bf16[512,1024]{1,0:T(8,128)(2,1)}, bf16[512,1024]{1,0:T(8,128)(2,1)}, u32[]{:S(2)}, u32[]{:S(2)}) collective-permute-start(bf16[512,1024]{1,0:T(8,128)(2,1)} %param.17), channel_id=1, source_target_pairs={{0,1},{1,0},{2,3},{3,2},{4,5},{5,4},{6,7},{7,6},{8,9},{9,8},{10,11... | collective-permute-start | bytes 3145736 | tf_op jit(solution)/shard_map/ppermute | solution.py:358
  247.7 381.5 %reduce-scatter.13.cloned.1.call-start = ((), (), s32[]{:S(2)}) async-start(), calls=%async_computation.8 | async-start | bytes 540672
  265.9 73.9 %collective-permute-start.7 = (bf16[1024,1408]{1,0:T(8,128)(2,1)}, bf16[1024,1408]{1,0:T(8,128)(2,1)S(1)}, u32[]{:S(2)}, u32[]{:S(2)}) collective-permute-start(bf16[1024,1408]{1,0:T(8,128)(2,1)} %get-tuple-element.57), channel_id=1, source_target_pairs={{0,1},{1,0},{2,3},{3,2},{4,5},{5,4},{6,7},{7,6},{8,9},{9,8},{10,11... | collective-permute-start | bytes 8650760 | tf_op jit(solution)/shard_map/ppermute | solution.py:358
  321.1 22.9 %collective-permute-start.8 = (bf16[1024,1408]{1,0:T(8,128)(2,1)}, bf16[1024,1408]{1,0:T(8,128)(2,1)}, u32[]{:S(2)}, u32[]{:S(2)}) collective-permute-start(bf16[1024,1408]{1,0:T(8,128)(2,1)} %get-tuple-element.60), channel_id=1, source_target_pairs={{0,1},{1,0},{2,3},{3,2},{4,5},{5,4},{6,7},{7,6},{8,9},{9,8},{10,11... | collective-permute-start | bytes 8650760 | tf_op jit(solution)/shard_map/ppermute | solution.py:358
  321.1 20.3 %copy-start.2 = (bf16[1024,1408]{1,0:T(8,128)(2,1)S(1)}, bf16[1024,1408]{1,0:T(8,128)(2,1)}, u32[]{:S(2)}) copy-start(bf16[1024,1408]{1,0:T(8,128)(2,1)} %get-tuple-element.56) | copy-start | bytes 8650756
  339.3 9.0 collective-permute-start.9
  339.8 1.6 copy-start.5
  341.4 2.7 copy-start.3
  344.1 4.2 copy-start.4
  474.5 19.1 %copy-start.8 = (f32[1,1024]{1,0:T(1,128)S(1)}, f32[1,1024]{1,0:T(1,128)}, u32[]{:S(2)}) copy-start(f32[1,1024]{1,0:T(1,128)} %get-tuple-element.52) | copy-start | bytes 12292
  495.4 304.4 %reduce-scatter.11.cloned.1.call-start = ((), (), s32[]{:S(2)}) async-start(), calls=%async_computation.6 | async-start | bytes 9191424 | tf_op jit(solution)/shard_map/reduce_scatter | solution.py:979
  501.9 430.1 %reduce-scatter.9.cloned.1.call-start = ((), (), s32[]{:S(2)}) async-start(), calls=%async_computation.5 | async-start | bytes 2506752 | tf_op jit(solution)/shard_map/reduce_scatter | solution.py:998
  510.6 8.8 copy-start.1
  522.9 4.6 collective-permute-start.6
Sparse Core Ops, SparseCore 0:
  28.1 61.5 all-gather.2
  247.9 226.5 reduce-scatter.6
  495.5 133.7 reduce-scatter.12
  635.8 163.9 reduce-scatter.10
  804.5 127.4 reduce-scatter.8

commit v2 on v1

--- a/solution.py
+++ b/solution.py
@@ -354,8 +354,22 @@
     return pltpu.CompilerParams(vmem_limit_bytes=limit * MIB)
 
 
+def cost(flops, moved=0):
+    return pl.CostEstimate(flops=int(flops), bytes_accessed=int(moved), transcendentals=0)
+
+
 def swap_cores(value):
     return lax.ppermute(value, "mp", [(0, 1), (1, 0)])
+
+
+def shift(value, axis, by):
+    size = lax.axis_size(axis)
+    return lax.ppermute(value, axis, [(i, (i + by) % size) for i in range(size)])
+
+
+def gather_keys(kv):
+    near = [kv] + [shift(kv, "seq", k) for k in range(1, lax.axis_size("seq"))]
+    return near + [swap_cores(value) for value in near]
 
 
 def by_core(own, other, axis):
@@ -371,33 +385,23 @@
     return jnp.concatenate([a * cosine - b * sine_table, b * cosine + a * sine_table], axis=0)
 
 
-def project_kernel(heads, x_ref, gain_ref, w_ref, cos_ref, sin_ref, q_ref, kv_ref, nt_ref):
+def keys_kernel(x_ref, gain_ref, w_ref, cos_ref, sin_ref, kv_ref, nt_ref):
     x = x_ref[0].astype(F32)
     inverse = lax.rsqrt(jnp.mean(x * x, axis=-1, keepdims=True) + epsilon)
     normed = (x * inverse * gain_ref[...]).astype(BF)
     nt_ref[...] = normed.T
-    cosine, sine_table = cos_ref[...], sin_ref[...]
     lin = mxu(w_ref[...], normed, NT)
-    plain = HD - RD
-    pieces = []
-    for h in range(heads):
-        at = h * HD
-        pieces.append(lin[at : at + plain])
-        pieces.append(rotate_rows(lin[at + plain : at + HD], cosine, sine_table))
-    queries = jnp.concatenate(pieces, axis=0)
-    q_ref[...] = (queries.astype(BF) * HD ** (-0.5)).astype(BF)
-    tied_end = w_ref.shape[0] - RD
-    kv_ref[0, : tied_end - heads * HD] = lin[heads * HD : tied_end].astype(BF)
-    kv_ref[0, tied_end - heads * HD :] = rotate_rows(lin[tied_end:], cosine, sine_table).astype(BF)
-
-
-def project(x, gain, weights, cosine, sine_table, heads):
+    tied = w_ref.shape[0] - RD
+    kv_ref[0, :tied] = lin[:tied].astype(BF)
+    kv_ref[0, tied:] = rotate_rows(lin[tied:], cos_ref[...], sin_ref[...]).astype(BF)
+
+
+def project_keys(x, gain, weights, cosine, sine_table):
     count, own, width = x.shape
     rows = weights.shape[0]
-    kv_rows = rows - heads * HD
     whole = lambda b: (0, 0)
     return pl.pallas_call(
-        functools.partial(project_kernel, heads),
+        keys_kernel,
         grid=(count,),
         in_specs=[
             pl.BlockSpec((1, own, width), lambda b: (b, 0, 0)),
@@ -407,18 +411,50 @@
             pl.BlockSpec(cosine.shape, whole),
         ],
         out_specs=[
-            pl.BlockSpec((heads * HD, own), lambda b: (0, b)),
-            pl.BlockSpec((1, kv_rows, own), lambda b: (b, 0, 0)),
+            pl.BlockSpec((1, rows, own), lambda b: (b, 0, 0)),
             pl.BlockSpec((width, own), lambda b: (0, b)),
         ],
         out_shape=[
-            jax.ShapeDtypeStruct((heads * HD, count * own), BF),
-            jax.ShapeDtypeStruct((count, kv_rows, own), BF),
+            jax.ShapeDtypeStruct((count, rows, own), BF),
             jax.ShapeDtypeStruct((width, count * own), BF),
         ],
         compiler_params=params(),
-        name="project",
+        cost_estimate=cost(2 * x.size * rows, 4 * x.size),
+        name="project_keys",
     )(x, gain, weights, cosine, sine_table)
+
+
+def queries_kernel(nt_ref, w_ref, cos_ref, sin_ref, q_ref):
+    lin = mxu(w_ref[...], nt_ref[...], NN)
+    cosine, sine_table = cos_ref[...], sin_ref[...]
+    plain = HD - RD
+    pieces = []
+    for at in range(0, lin.shape[0], HD):
+        pieces.append(lin[at : at + plain])
+        pieces.append(rotate_rows(lin[at + plain : at + HD], cosine, sine_table))
+    queries = jnp.concatenate(pieces, axis=0)
+    q_ref[...] = (queries.astype(BF) * HD ** (-0.5)).astype(BF)
+
+
+def project_queries(normed_t, weights, cosine, sine_table):
+    width, tokens = normed_t.shape
+    rows, own = weights.shape[0], cosine.shape[1]
+    whole = lambda b: (0, 0)
+    return pl.pallas_call(
+        queries_kernel,
+        grid=(tokens // own,),
+        in_specs=[
+            pl.BlockSpec((width, own), lambda b: (0, b)),
+            pl.BlockSpec((rows, width), whole),
+            pl.BlockSpec(cosine.shape, whole),
+            pl.BlockSpec(cosine.shape, whole),
+        ],
+        out_specs=pl.BlockSpec((rows, own), lambda b: (0, b)),
+        out_shape=jax.ShapeDtypeStruct((rows, tokens), BF),
+        compiler_params=params(),
+        cost_estimate=cost(2 * normed_t.size * rows, 4 * normed_t.size),
+        name="project_queries",
+    )(normed_t, weights, cosine, sine_table)
 
 
 def segment_counts(starts, first, width):
@@ -468,17 +504,32 @@
     return lax.axis_index("seq") * lax.axis_size("mp") + lax.axis_index("mp")
 
 
+def place_keys(refs, kv, begin, me):
+    steps = len(refs) // 2
+    seq, core = lax.axis_index("seq"), lax.axis_index("mp")
+    for at, ref in enumerate(refs):
+        of = core if at < steps else 1 - core
+        j = lax.rem(seq - at % steps + steps, steps) * 2 + of
+
+        @pl.when((j >= begin) & (j <= me))
+        def _():
+            kv[j] = ref[0]
+
+
 def stack_heads(value, at, heads):
     return jnp.concatenate([value[at + h * HD : at + (h + 1) * HD] for h in range(heads)], axis=1)
 
 
-def attend_kernel(groups, heads, docs_ref, q_ref, kv_ref, out_ref, lse_ref, qa, ka, va, acc, top):
-    b = pl.program_id(0)
+def attend_kernel(groups, heads, first, chunks, docs_ref, q_ref, *refs):
+    kv_refs = refs[:chunks]
+    out_ref, lse_ref, kv_ref, qa, acc, top = refs[-6:]
+    b = pl.program_id(0) + first
     own = q_ref.shape[1]
     ndoc = docs_ref.shape[1]
     starts = [docs_ref[b, k] for k in range(ndoc)]
     me = my_chunk()
     begin = start_chunk(starts, me * own, own)
+    place_keys(kv_refs, kv_ref, begin, me)
     wide = heads * own
     tied = groups * HD
     plain = HD - RD
@@ -496,8 +547,8 @@
         doc = key_rows(starts, j * own, own)
         block = jnp.concatenate(
             [
-                kv_ref[j, 0, g * HD : g * HD + plain],
-                kv_ref[j, 0, tied : tied + RD],
+                kv_ref[j, g * HD : g * HD + plain],
+                kv_ref[j, tied : tied + RD],
                 doc,
                 zeros,
             ],
@@ -506,7 +557,7 @@
         return mxu(block.T, qa[g], NN)
 
     def weighted(j, g, weights):
-        values = jnp.concatenate([kv_ref[j, 0, g * HD : (g + 1) * HD], ones], axis=0)
+        values = jnp.concatenate([kv_ref[j, g * HD : (g + 1) * HD], ones], axis=0)
         return mxu(values, weights.astype(BF), NN)
 
     key_at = lax.broadcasted_iota(jnp.int32, (own, own), 0)
@@ -538,47 +589,53 @@
             out_ref[at : at + HD] = result[:, h * own : (h + 1) * own].astype(BF)
 
 
-def attend_forward(docs, q, kv, groups, heads):
-    chunks, count, kv_rows, own = kv.shape
+def attend_forward(docs, q, kv, groups, heads, first, into):
+    size, kv_rows, own = kv[0].shape
+    count, chunks = docs.shape[0], len(kv)
     wide = heads * own
+    hbm = pl.BlockSpec(memory_space=pl.ANY)
     return pl.pallas_call(
-        functools.partial(attend_kernel, groups, heads),
-        grid=(count,),
+        functools.partial(attend_kernel, groups, heads, first, chunks),
+        grid=(size,),
         in_specs=[
             pl.BlockSpec(memory_space=pltpu.SMEM),
-            pl.BlockSpec((q.shape[0], own), lambda b: (0, b)),
-            pl.BlockSpec((chunks, 1, kv_rows, own), lambda b: (0, b, 0, 0)),
-        ],
+            pl.BlockSpec((q.shape[0], own), lambda b: (0, b + first)),
+        ]
+        + [pl.BlockSpec((1, kv_rows, own), lambda b: (b, 0, 0))] * chunks
+        + [hbm] * len(into),
         out_specs=[
-            pl.BlockSpec((q.shape[0], own), lambda b: (0, b)),
-            pl.BlockSpec((1, groups, wide), lambda b: (b, 0, 0)),
+            pl.BlockSpec((q.shape[0], own), lambda b: (0, b + first)),
+            pl.BlockSpec((1, groups, wide), lambda b: (b + first, 0, 0)),
         ],
         out_shape=[
             jax.ShapeDtypeStruct(q.shape, BF),
             jax.ShapeDtypeStruct((count, groups, wide), F32),
         ],
         scratch_shapes=[
+            pltpu.VMEM((chunks, kv_rows, own), BF),
             pltpu.VMEM((groups, LANE, wide), BF),
-            pltpu.VMEM((8, LANE), BF),
-            pltpu.VMEM((8, LANE), BF),
             pltpu.VMEM((groups, HD + 16, wide), F32),
             pltpu.VMEM((groups, 1, wide), F32),
         ],
+        input_output_aliases={2 + chunks + i: i for i in range(len(into))},
         compiler_params=params(),
+        cost_estimate=cost(10**10 * size),
         name="attend",
-    )(docs, q, kv)
+    )(docs, q, *kv, *into)
 
 
 def attend_back_kernel(
-    groups, heads, docs_ref, q_ref, do_ref, lse_ref, delta_ref, kv_ref, rot_ref,
-    dq_ref, dkv_ref, qs, qa, ds_, da, dq,
+    groups, heads, first, chunks, docs_ref, q_ref, do_ref, lse_ref, delta_ref, rot_ref, *refs
 ):
-    b = pl.program_id(0)
+    kv_refs = refs[:chunks]
+    dq_ref, keep_ref, give_ref, kv_ref, stage, qs, qa, ds_, da, dq = refs[-10:]
+    b = pl.program_id(0) + first
     own = q_ref.shape[1]
     ndoc = docs_ref.shape[1]
     starts = [docs_ref[b, k] for k in range(ndoc)]
     me = my_chunk()
     begin = start_chunk(starts, me * own, own)
+    place_keys(kv_refs, kv_ref, begin, me)
     wide = heads * own
     tied = groups * HD
     plain = HD - RD
@@ -587,6 +644,17 @@
     q_all, do_all = q_ref[...], do_ref[...]
     pad_q = jnp.zeros((LANE - HD - 32, wide), BF)
     pad_d = jnp.zeros((LANE - HD - 16, wide), BF)
+    row_at = lax.broadcasted_iota(jnp.int32, (own, own), 0)
+    column_at = lax.broadcasted_iota(jnp.int32, (own, own), 1)
+    identity = jnp.where(row_at == column_at, 1.0, 0.0).astype(BF)
+
+    def turn(rows, ref):
+        for h in range(0, heads, 2):
+            pair = [rows[:, (h + i) * own : (h + i + 1) * own] for i in range(2)]
+            turned = mxu(identity, jnp.concatenate(pair, axis=0), NT).astype(BF)
+            ref[h * own : (h + 1) * own] = turned[:, :LANE]
+            ref[(h + 1) * own : (h + 2) * own] = turned[:, LANE:]
+
     for g in range(groups):
         q_rows = stack_heads(q_all, g * heads * HD, heads)
         do_rows = stack_heads(do_all, g * heads * HD, heads)
@@ -597,25 +665,39 @@
             [delta_ref[0, g * heads + h : g * heads + h + 1] for h in range(heads)], axis=1
         )
         delta_rows = three_parts(-delta_row, wide)
-        qa[g] = jnp.concatenate([q_rows, q_doc, lse_rows, pad_q], axis=0).T
-        da[g] = jnp.concatenate([do_rows, delta_rows, pad_d], axis=0).T
+        turn(jnp.concatenate([q_rows, q_doc, lse_rows, pad_q], axis=0), qa.at[g])
+        turn(jnp.concatenate([do_rows, delta_rows, pad_d], axis=0), da.at[g])
     ones = first_rows(3, own)
     pad_k = jnp.zeros((LANE - HD - 32, own), BF)
     pad_v = jnp.zeros((LANE - HD - 16, own), BF)
 
+    seq, core = lax.axis_index("seq"), lax.axis_index("mp")
+    steps = chunks // 2
+
+    def deliver(j, value):
+        k = lax.rem(j // 2 - seq + steps, steps)
+
+        @pl.when(lax.rem(j, 2) == core)
+        def _():
+            keep_ref[k, 0] = value()
+
+        @pl.when(lax.rem(j, 2) != core)
+        def _():
+            give_ref[k, 0] = value()
+
     def clear(j, carry):
-        dkv_ref[j, 0] = jnp.zeros(dkv_ref.shape[2:], BF)
+        deliver(j, lambda: jnp.zeros(keep_ref.shape[2:], BF))
         return carry
 
     lax.fori_loop(0, begin, clear, 0)
-    lax.fori_loop(me + 1, dkv_ref.shape[0], clear, 0)
+    lax.fori_loop(me + 1, chunks, clear, 0)
 
     def block(j, diagonal):
         doc = key_rows(starts, j * own, own)
-        rope_rows = kv_ref[j, 0, tied : tied + RD]
+        rope_rows = kv_ref[j, tied : tied + RD]
         rope_sum = jnp.zeros((RD, own), F32)
         for g in range(groups):
-            values = kv_ref[j, 0, g * HD : (g + 1) * HD]
+            values = kv_ref[j, g * HD : (g + 1) * HD]
             keys = jnp.concatenate([values[:plain], rope_rows], axis=0)
             logits = mxu(qa[g], jnp.concatenate([keys, doc, ones, pad_k], axis=0), NN)
             weights = jnp.exp(logits)
@@ -633,12 +715,13 @@
                 dq[g] = grad_queries
             else:
                 dq[g] += grad_queries
-            dkv_ref[j, 0, g * HD : g * HD + plain] = (
+            stage[g * HD : g * HD + plain] = (
                 grad_values[:plain] + grad_keys[:plain]
             ).astype(BF)
-            dkv_ref[j, 0, g * HD + plain : (g + 1) * HD] = grad_values[plain:].astype(BF)
+            stage[g * HD + plain : (g + 1) * HD] = grad_values[plain:].astype(BF)
             rope_sum = rope_sum + grad_keys[plain:]
-        dkv_ref[j, 0, tied : tied + RD] = rope_sum.astype(BF)
+        stage[tied : tied + RD] = rope_sum.astype(BF)
+        deliver(j, lambda: stage[...])
 
     block(me, True)
 
@@ -663,40 +746,61 @@
             dq_ref[:, to : to + 2 * HD] = turned.astype(BF)
 
 
-def attend_backward(docs, q, do, lse, delta, kv, turns, groups, heads):
-    chunks, count, kv_rows, own = kv.shape
+def attend_backward(docs, q, do, lse, delta, turns, kv, groups, heads, first, into):
+    size, kv_rows, own = kv[0].shape
+    count, chunks = docs.shape[0], len(kv)
     wide = heads * own
     width = q.shape[0]
+    column = pl.BlockSpec((width, own), lambda b: (0, b + first))
+    hbm = pl.BlockSpec(memory_space=pl.ANY)
     return pl.pallas_call(
-        functools.partial(attend_back_kernel, groups, heads),
-        grid=(count,),
+        functools.partial(attend_back_kernel, groups, heads, first, chunks),
+        grid=(size,),
         in_specs=[
             pl.BlockSpec(memory_space=pltpu.SMEM),
-            pl.BlockSpec((width, own), lambda b: (0, b)),
-            pl.BlockSpec((width, own), lambda b: (0, b)),
-            pl.BlockSpec((1, groups, wide), lambda b: (b, 0, 0)),
-            pl.BlockSpec((1, groups * heads, own), lambda b: (b, 0, 0)),
-            pl.BlockSpec((chunks, 1, kv_rows, own), lambda b: (0, b, 0, 0)),
+            column,
+            column,
+            pl.BlockSpec((1, groups, wide), lambda b: (b + first, 0, 0)),
+            pl.BlockSpec((1, groups * heads, own), lambda b: (b + first, 0, 0)),
             pl.BlockSpec(turns.shape, lambda b: (0, 0, 0)),
-        ],
+        ]
+        + [pl.BlockSpec((1, kv_rows, own), lambda b: (b, 0, 0))] * chunks
+        + [hbm] * len(into),
         out_specs=[
-            pl.BlockSpec((own, width), lambda b: (b, 0)),
-            pl.BlockSpec((chunks, 1, kv_rows, own), lambda b: (0, b, 0, 0)),
+            pl.BlockSpec((own, width), lambda b: (b + first, 0)),
+            pl.BlockSpec((chunks // 2, 1, kv_rows, own), lambda b: (0, b, 0, 0)),
+            pl.BlockSpec((chunks // 2, 1, kv_rows, own), lambda b: (0, b, 0, 0)),
         ],
         out_shape=[
             jax.ShapeDtypeStruct((count * own, width), BF),
-            jax.ShapeDtypeStruct(kv.shape, BF),
+            jax.ShapeDtypeStruct((chunks // 2, size, kv_rows, own), BF),
+            jax.ShapeDtypeStruct((chunks // 2, size, kv_rows, own), BF),
         ],
         scratch_shapes=[
+            pltpu.VMEM((chunks, kv_rows, own), BF),
+            pltpu.VMEM((kv_rows, own), BF),
             pltpu.VMEM((groups, HD, wide), BF),
             pltpu.VMEM((groups, wide, LANE), BF),
             pltpu.VMEM((groups, HD, wide), BF),
             pltpu.VMEM((groups, wide, LANE), BF),
             pltpu.VMEM((groups, wide, HD), F32),
         ],
+        input_output_aliases={6 + chunks + i: i for i in range(len(into))},
         compiler_params=params(),
+        cost_estimate=cost(15 * 10**9 * size),
         name="attend_back",
-    )(docs, q, do, lse, delta, kv, turns)
+    )(docs, q, do, lse, delta, turns, *kv, *into)
+
+
+def join_cores(keep, give):
+    received = swap_cores(give)
+    return [
+        (keep[k].astype(F32) + received[k].astype(F32)).astype(BF) for k in range(keep.shape[0])
+    ]
+
+
+def send_keys(summed):
+    return [summed[0]] + [shift(summed[k], "seq", k) for k in range(1, len(summed))]
 
 
 def load_weights(refs, targets, sems):
@@ -714,8 +818,43 @@
     return copies
 
 
+def slopes_kernel(og_ref, wdo_ref, wdp_ref, out_ref, wd, sems):
+    @pl.when(pl.program_id(0) == 0)
+    def _():
+        copies = load_weights([(wdo_ref, 0, 0), (wdp_ref, 1, 0)], [wd, wd], sems)
+        for copy in copies:
+            copy.start()
+        for copy in copies:
+            copy.wait()
+
+    og = og_ref[0]
+    for at in range(0, wd.shape[0], 2 * LANE):
+        to = slice(at, at + 2 * LANE)
+        out_ref[:, to] = mxu(og, wd[to], NT).astype(BF)
+
+
+def unit_slopes(og, wd):
+    count, own, width = og.shape
+    half = wd[0].shape[0]
+    hbm = pl.BlockSpec(memory_space=pl.ANY)
+    return pl.pallas_call(
+        slopes_kernel,
+        grid=(count,),
+        in_specs=[pl.BlockSpec((1, own, width), lambda b: (b, 0, 0)), hbm, hbm],
+        out_specs=pl.BlockSpec((own, 2 * half), lambda b: (b, 0)),
+        out_shape=jax.ShapeDtypeStruct((count * own, 2 * half), BF),
+        scratch_shapes=[
+            pltpu.VMEM((2 * half, width), BF),
+            pltpu.SemaphoreType.DMA((2 * (half // LANE),)),
+        ],
+        compiler_params=params(),
+        cost_estimate=cost(4 * og.size * half),
+        name="unit_slopes",
+    )(og, *wd)
+
+
 def feed_kernel(
-    x_ref, og_ref, o_ref, gain_ref, wo_ref, wgo_ref, wgp_ref, wuo_ref, wup_ref, wdo_ref, wdp_ref,
+    x_ref, og_ref, ga_ref, o_ref, gain_ref, wo_ref, wgo_ref, wgp_ref, wuo_ref, wup_ref, wdo_ref, wdp_ref,
     out_ref, nt_ref, ogt_ref, act_ref, gg_ref, gu_ref, gh_ref, gat_ref, do_ref, delta_ref, gg2_ref,
     wo, wg, wu, wd, sems,
 ):
@@ -752,7 +891,7 @@
         at = slice(t * tile, (t + 1) * tile)
         gate = mxu(normed, wg[:, at], NN)
         up = mxu(normed, wu[:, at], NN)
-        grad = mxu(og, wd[at], NT)
+        grad = ga_ref[:, at].astype(F32)
         sigmoid = 1.0 / (1.0 + jnp.exp(-gate))
         silu = gate * sigmoid
         act_ref[:, at] = (silu * up).astype(BF)
@@ -775,7 +914,7 @@
         delta_ref[0, h : h + 1] = jnp.sum(product[h * HD : (h + 1) * HD], axis=0, keepdims=True)
 
 
-def feed(x, og, heads_out, gain, wo, wg, wu, wd):
+def feed(x, og, slopes, heads_out, gain, wo, wg, wu, wd):
     count, own, width = x.shape
     hd = heads_out.shape[0]
     half = wg[0].shape[1]
@@ -788,7 +927,7 @@
     return pl.pallas_call(
         feed_kernel,
         grid=(count,),
-        in_specs=[seq, seq, column(hd), pl.BlockSpec((1, width), lambda b: (0, 0))] + [hbm] * 7,
+        in_specs=[seq, seq, row, column(hd), pl.BlockSpec((1, width), lambda b: (0, 0))] + [hbm] * 7,
         out_specs=[
             seq, column(width), column(width), row, row, row, seq, column(width), column(hd),
             pl.BlockSpec((1, hd // HD, own), lambda b: (b, 0, 0)),
@@ -815,23 +954,39 @@
             pltpu.SemaphoreType.DMA((6 * (half // LANE) + 1,)),
         ],
         compiler_params=params(),
+        cost_estimate=cost(2 * tokens * width * (5 * units + 2 * hd)),
         name="feed",
-    )(x, og, heads_out, gain, wo, *wg, *wu, *wd)
-
-
-def unit_grads_kernel(left_ref, right_ref, own_ref, other_ref):
-    product = mxu(left_ref[...], right_ref[...], NN).astype(BF)
+    )(x, og, slopes, heads_out, gain, wo, *wg, *wu, *wd)
+
+
+def regroup_rows(value, split):
+    if split is None:
+        return value
+    count_d, count_s = split
+    own = value.shape[0] // (count_d * count_s)
+    return jnp.concatenate(
+        [
+            value[(d * count_s + s) * own : (d * count_s + s + 1) * own]
+            for s in range(count_s)
+            for d in range(count_d)
+        ],
+        axis=0,
+    )
+
+
+def unit_grads_kernel(split, left_ref, right_ref, own_ref, other_ref):
+    product = regroup_rows(mxu(left_ref[...], right_ref[...], NN), split).astype(BF)
     own_ref[...] = product[:, :LANE]
     other_ref[...] = product[:, LANE:]
 
 
-def unit_grads(left, right):
+def unit_grads(left, right, split):
     width, tokens = left.shape
     units = right.shape[1]
     tile = 2 * LANE
     part = pl.BlockSpec((width, LANE), lambda t: (0, t))
     return pl.pallas_call(
-        unit_grads_kernel,
+        functools.partial(unit_grads_kernel, split),
         grid=(units // tile,),
         in_specs=[
             pl.BlockSpec((width, tokens), lambda t: (0, 0)),
@@ -840,90 +995,294 @@
         out_specs=[part, part],
         out_shape=[jax.ShapeDtypeStruct((width, units // 2), BF)] * 2,
         compiler_params=params(),
+        cost_estimate=cost(2 * left.size * units),
         name="unit_grads",
     )(left, right)
 
 
-def plain_grads_kernel(dims, left_ref, right_ref, out_ref):
-    out_ref[...] = mxu(left_ref[...], right_ref[...], dims).astype(BF)
-
-
-def plain_grads(left, right, dims):
+def head_grads_kernel(dims, split, core_ref, left_ref, right_ref, out_ref):
+    product = regroup_rows(mxu(left_ref[...], right_ref[...], dims), split)
+    out_ref[0] = product.astype(BF)
+
+
+def head_grads(left, right, dims, split):
     rows, tokens = left.shape
     columns = right.shape[1] if dims == NN else right.shape[0]
     tile = 2 * LANE
+    tiles = columns // tile
+    part = tiles // 2
+    at = lambda t, core: (t + core[0] * part) % tiles
     if dims == NN:
-        spec = pl.BlockSpec((tokens, tile), lambda t: (0, t))
+        spec = pl.BlockSpec((tokens, tile), lambda t, core: (0, at(t, core)))
     else:
-        spec = pl.BlockSpec((tile, tokens), lambda t: (t, 0))
+        spec = pl.BlockSpec((tile, tokens), lambda t, core: (at(t, core), 0))
     return pl.pallas_call(
-        functools.partial(plain_grads_kernel, dims),
-        grid=(columns // tile,),
-        in_specs=[pl.BlockSpec((rows, tokens), lambda t: (0, 0)), spec],
-        out_specs=pl.BlockSpec((rows, tile), lambda t: (0, t)),
-        out_shape=jax.ShapeDtypeStruct((rows, columns), BF),
+        functools.partial(head_grads_kernel, dims, split),
+        grid_spec=pltpu.PrefetchScalarGridSpec(
+            num_scalar_prefetch=1,
+            grid=(tiles,),
+            in_specs=[pl.BlockSpec((rows, tokens), lambda t, core: (0, 0)), spec],
+            out_specs=pl.BlockSpec((1, rows, tile), lambda t, core: (t // part, 0, t % part)),
+        ),
+        out_shape=jax.ShapeDtypeStruct((2, rows, columns // 2), BF),
         compiler_params=params(),
-        name="plain_grads",
-    )(left, right)
-
-
-def finish_kernel(
-    x_ref, gh_ref, dq_ref, dkv_ref, nt_ref, gain_ref, w_ref, cos_ref, sin_ref,
-    gi_ref, gg1_ref, dw_ref,
+        cost_estimate=cost(2 * left.size * columns),
+        name="head_grads",
+    )(lax.axis_index("mp").astype(jnp.int32)[None], left, right)
+
+
+def tail_kernel(
+    order, x_ref, gh_ref, dq_ref, nt_ref, gain_ref, wq_ref, wkv_ref, cos_ref, sin_ref, gg2_ref,
+    query_ref, early_ref, near_refs, *refs,
 ):
-    b = pl.program_id(0)
-
-    @pl.when(b == 0)
+    count_d, count_s = lax.axis_size("dp"), lax.axis_size("seq")
+    me_d, me_s, core = lax.axis_index("dp"), lax.axis_index("seq"), lax.axis_index("mp")
+    late = len(order) - 1
+    far_refs, refs = refs[:late], refs[late:]
+    gi_ref, query_out, small_out, early_out = refs[:4]
+    (
+        key_in, query_in, query_sum, query_seq, query_part, query_dp, early_in, dw, gg1,
+        small_other, small_in, small_sum, small_seq, small_part, small_dp, sends, receives,
+    ) = refs[4:]
+    rows = query_out.shape[0]
+    step = pl.program_id(0)
+    other_core = {"mp": 1 - core}
+    seq_peers = [{"seq": lax.rem(me_s + k, count_s)} for k in range(1, count_s)]
+    dp_peers = [{"dp": lax.rem(me_d + k, count_d)} for k in range(1, count_d)]
+    peers = [other_core] + seq_peers + dp_peers
+    slots = iter(range(sends.shape[0]))
+
+    def link(source, target, peer):
+        slot = next(slots)
+        return pltpu.make_async_remote_copy(
+            src_ref=source,
+            dst_ref=target,
+            send_sem=sends.at[slot],
+            recv_sem=receives.at[slot],
+            device_id=peer,
+            device_id_type=pl.DeviceIdType.MESH,
+        )
+
+    to_seq = [lax.rem(me_s + k, count_s) for k in range(1, count_s)]
+    to_dp = [lax.rem(me_d + k, count_d) for k in range(1, count_d)]
+    early_copies = [
+        link(early_ref.at[to_dp[k]], early_in.at[k], dp_peers[k]) for k in range(count_d - 1)
+    ]
+    key_copies, at = [], 0
+    for far in far_refs:
+        size = far.shape[1]
+        key_copies.append(
+            [
+                link(far.at[k + 1], key_in.at[k, pl.ds(at, size)], seq_peers[k])
+                for k in range(count_s - 1)
+            ]
+        )
+        at += size
+    query_core = link(query_ref.at[1], query_in, other_core)
+    query_seqs = [
+        link(query_sum.at[to_seq[k]], query_seq.at[k], seq_peers[k]) for k in range(count_s - 1)
+    ]
+    query_dps = [
+        link(query_part.at[to_dp[k]], query_dp.at[k], dp_peers[k]) for k in range(count_d - 1)
+    ]
+    small_core = link(small_other, small_in, other_core)
+    small_seqs = [
+        link(small_sum.at[to_seq[k]], small_seq.at[k], seq_peers[k]) for k in range(count_s - 1)
+    ]
+    small_dps = [
+        link(small_part.at[to_dp[k]], small_dp.at[k], dp_peers[k]) for k in range(count_d - 1)
+    ]
+
+    def start(copies):
+        for copy in copies:
+            copy.start()
+
+    def by_seq(total, target):
+        for s in range(count_s):
+            for d in range(count_d):
+                of = (d * count_s + s) * rows
+                target[s, d * rows : (d + 1) * rows] = total[of : of + rows].astype(BF)
+
+    def gather(own, copies, arrived):
+        total = own.astype(F32)
+        for k, copy in enumerate(copies):
+            copy.wait()
+            total = total + arrived[k].astype(F32)
+        return total
+
+    def by_dp(total, target):
+        for d in range(count_d):
+            target[d] = total[d * rows : (d + 1) * rows].astype(BF)
+
+    @pl.when(step == 0)
     def _():
-        gg1_ref[...] = jnp.zeros(gg1_ref.shape, F32)
-        dw_ref[...] = jnp.zeros(dw_ref.shape, F32)
-
-    rows = w_ref.shape[0]
-    kv_rows = dkv_ref.shape[1]
+        barrier = pltpu.get_barrier_semaphore()
+        for peer in peers:
+            pl.semaphore_signal(barrier, inc=1, device_id=peer, device_id_type=pl.DeviceIdType.MESH)
+        pl.semaphore_wait(barrier, len(peers))
+        start([query_core])
+        for copies in key_copies:
+            start(copies)
+        start(early_copies)
+        dw[...] = jnp.zeros(dw.shape, F32)
+        gg1[...] = jnp.zeros(gg1.shape, F32)
+
+    @pl.when(step == 1)
+    def _():
+        query_core.wait()
+        by_seq(query_ref[0].astype(F32) + query_in[...].astype(F32), query_sum)
+        start(query_seqs)
+
+    tied = wkv_ref.shape[0] - RD
+
+    def finish(summed):
+        turned = rotate_rows(summed[tied:], cos_ref[...], -sin_ref[...])
+        dkv = jnp.concatenate([summed[:tied], turned], axis=0).astype(BF)
+        grad_normed = mxu(dq_ref[...], wq_ref[...], NN) + mxu(dkv, wkv_ref[...], TN)
+        dw[...] += mxu(nt_ref[...], dkv, NT)
+        x = x_ref[0].astype(F32)
+        inverse = lax.rsqrt(jnp.mean(x * x, axis=-1, keepdims=True) + epsilon)
+        scaled = grad_normed * gain_ref[...]
+        gg1[...] += jnp.sum(grad_normed * (x * inverse), axis=0, keepdims=True)
+        mean = jnp.mean(scaled * x, axis=-1, keepdims=True)
+        gi_ref[0] = gh_ref[0] + inverse * scaled - x * (inverse * inverse * inverse * mean)
+
+    begin = order[0][1]
+
+    @pl.when(step < begin)
+    def _():
+        summed = near_refs[0][0].astype(F32)
+        for ref in near_refs[1:]:
+            summed = summed + ref[0].astype(F32)
+        finish(summed)
+
+    base = begin
+    for part, far in enumerate(far_refs):
+        size = far.shape[1]
+
+        @pl.when(step == begin)
+        def _():
+            for copy in key_copies[part]:
+                copy.wait()
+
+        @pl.when((step >= begin) & (step < begin + size))
+        def _():
+            at = step - base
+            summed = far[0, step - begin].astype(F32)
+            for k in range(count_s - 1):
+                summed = summed + key_in[k, at].astype(F32)
+            finish(summed)
+
+        begin += size
+
+    @pl.when(step == begin - 2)
+    def _():
+        total = gather(query_sum[me_s], query_seqs, query_seq)
+        by_dp(total, query_part)
+        start(query_dps)
+
+    @pl.when(step == begin - 1)
+    def _():
+        width = dw.shape[0]
+        pad = jnp.zeros((LANE - RD, width), F32)
+        row = lax.broadcasted_iota(jnp.int32, (LANE, width), 0)
+        gains = jnp.where(row == RD, gg1[...], 0.0)
+        gains = jnp.where(row == RD + 1, gg2_ref[...], gains)
+        weights = dw[...]
+        rope = jnp.concatenate([weights[:, tied:], jnp.zeros((width, LANE - RD), F32)], axis=1)
+        small = rope + gains.T
+        half = tied // 2
+        first, second = weights[:, :half], weights[:, half:tied]
+        mine = jnp.concatenate([jnp.where(core == 0, first, second), small], axis=1)
+        other = jnp.concatenate([jnp.where(core == 0, second, first), small], axis=1)
+        small_other[...] = other.astype(BF)
+        start([small_core])
+        small_core.wait()
+        by_seq(mine + small_in[...].astype(F32), small_sum)
+        start(small_seqs)
+        by_dp(gather(small_sum[me_s], small_seqs, small_seq), small_part)
+        start(small_dps)
+        early_out[...] = gather(early_ref[me_d], early_copies, early_in)
+        query_out[...] = gather(query_part[me_d], query_dps, query_dp)
+        small_out[...] = gather(small_part[me_d], small_dps, small_dp)
+
+
+def tail(
+    order, x, grad_hidden, dq, nt, gain, wq, wkv, cosine, sine_table, grad_gain_two, grad_query,
+    early, near, far,
+):
+    count, own, width = x.shape
+    count_d, count_s = lax.axis_size("dp"), lax.axis_size("seq")
+    rows = width // (count_d * count_s)
+    kv_rows = wkv.shape[0]
     tied = kv_rows - RD
-    summed = dkv_ref[0].astype(F32)
-    turned = rotate_rows(summed[tied:], cos_ref[...], -sin_ref[...])
-    dkv = jnp.concatenate([summed[:tied], turned], axis=0).astype(BF)
-    grad_normed = mxu(dq_ref[...], w_ref[: rows - kv_rows], NN)
-    grad_normed = grad_normed + mxu(dkv, w_ref[rows - kv_rows :], TN)
-    dw_ref[...] += mxu(nt_ref[...], dkv, NT)
-    x = x_ref[0].astype(F32)
-    inverse = lax.rsqrt(jnp.mean(x * x, axis=-1, keepdims=True) + epsilon)
-    scaled = grad_normed * gain_ref[...]
-    gg1_ref[...] += jnp.sum(grad_normed * (x * inverse), axis=0, keepdims=True)
-    mean = jnp.mean(scaled * x, axis=-1, keepdims=True)
-    gi_ref[0] = gh_ref[0] + inverse * scaled - x * (inverse * inverse * inverse * mean)
-
-
-def finish(x, grad_hidden, dq, dkv, nt, gain, weights, cosine, sine_table):
-    count, own, width = x.shape
-    kv_rows = dkv.shape[1]
-    seq = pl.BlockSpec((1, own, width), lambda b: (b, 0, 0))
-    whole = lambda b: (0, 0)
+    wide = grad_query.shape[2]
+    narrow = tied // 2 + LANE
+    sent = sum(part.shape[1] for part in far)
+
+    def place(i):
+        done, at = 0, i
+        for first, size in order:
+            at = jnp.where((i >= done) & (i < done + size), first + i - done, at)
+            done += size
+        return at
+
+    seq = pl.BlockSpec((1, own, width), lambda i: (place(i), 0, 0))
+    whole = lambda array: pl.BlockSpec(array.shape, lambda i: (0,) * array.ndim)
+    last = order[0][1] - 1
+    near_spec = pl.BlockSpec((1, kv_rows, own), lambda i: (jnp.minimum(i, last), 0, 0))
+    fixed = [gain, wq, wkv, cosine, sine_table, grad_gain_two, grad_query, early]
+    outs = [
+        jax.ShapeDtypeStruct(x.shape, F32),
+        jax.ShapeDtypeStruct((rows, wide), F32),
+        jax.ShapeDtypeStruct((rows, narrow), F32),
+        jax.ShapeDtypeStruct((rows, early.shape[2]), F32),
+    ]
+    terms = len(near)
+
+    def kernel(*refs):
+        head, nears, rest = refs[:12], refs[12 : 12 + terms], refs[12 + terms :]
+        tail_kernel(order, *head, nears, *rest)
+
+    slots = 3 * (count_d - 1) + (2 + len(far)) * (count_s - 1) + 2
     return pl.pallas_call(
-        finish_kernel,
+        kernel,
         grid=(count,),
         in_specs=[
             seq, seq,
-            pl.BlockSpec((own, dq.shape[1]), lambda b: (b, 0)),
-            pl.BlockSpec((1, kv_rows, own), lambda b: (b, 0, 0)),
-            pl.BlockSpec((width, own), lambda b: (0, b)),
-            pl.BlockSpec((1, width), whole),
-            pl.BlockSpec(weights.shape, whole),
-            pl.BlockSpec(cosine.shape, whole),
-            pl.BlockSpec(cosine.shape, whole),
-        ],
-        out_specs=[
-            seq, pl.BlockSpec((1, width), whole), pl.BlockSpec((width, kv_rows), whole),
-        ],
-        out_shape=[
-            jax.ShapeDtypeStruct(x.shape, F32),
-            jax.ShapeDtypeStruct((1, width), F32),
-            jax.ShapeDtypeStruct((width, kv_rows), F32),
-        ],
-        compiler_params=params(),
-        name="finish",
-    )(x, grad_hidden, dq, dkv, nt, gain, weights, cosine, sine_table)
+            pl.BlockSpec((own, dq.shape[1]), lambda i: (place(i), 0)),
+            pl.BlockSpec((width, own), lambda i: (0, place(i))),
+        ]
+        + [whole(array) for array in fixed]
+        + [near_spec] * terms
+        + [whole(array) for array in far],
+        out_specs=[seq] + [whole(out) for out in outs[1:]],
+        out_shape=outs,
+        scratch_shapes=[
+            pltpu.VMEM((count_s - 1, sent, kv_rows, own), BF),
+            pltpu.VMEM((width, wide), BF),
+            pltpu.VMEM((count_s, count_d * rows, wide), BF),
+            pltpu.VMEM((count_s - 1, count_d * rows, wide), BF),
+            pltpu.VMEM((count_d, rows, wide), BF),
+            pltpu.VMEM((count_d - 1, rows, wide), BF),
+            pltpu.VMEM((count_d - 1, rows, early.shape[2]), BF),
+            pltpu.VMEM((width, kv_rows), F32),
+            pltpu.VMEM((1, width), F32),
+            pltpu.VMEM((width, narrow), BF),
+            pltpu.VMEM((width, narrow), BF),
+            pltpu.VMEM((count_s, count_d * rows, narrow), BF),
+            pltpu.VMEM((count_s - 1, count_d * rows, narrow), BF),
+            pltpu.VMEM((count_d, rows, narrow), BF),
+            pltpu.VMEM((count_d - 1, rows, narrow), BF),
+            pltpu.SemaphoreType.DMA((slots,)),
+            pltpu.SemaphoreType.DMA((slots,)),
+        ],
+        compiler_params=pltpu.CompilerParams(
+            vmem_limit_bytes=56 * MIB, collective_id=1, has_side_effects=True
+        ),
+        cost_estimate=cost(4 * 10**10),
+        name="tail",
+    )(x, grad_hidden, dq, nt, *fixed, *near, *far)
 
 
 def turn_tables(cosine, sine_table):
@@ -935,6 +1294,21 @@
     ahead = jnp.concatenate([none, sine_table, quiet], axis=1)
     behind = jnp.concatenate([none, quiet, -sine_table], axis=1)
     return jnp.stack([jnp.concatenate([t, t], axis=1) for t in (straight, ahead, behind)])
+
+
+def after(value, *others):
+    return lax.optimization_barrier((value, *others))[0]
+
+
+def spans(count, shares):
+    if count % 4:
+        return [(0, count)]
+    cuts, at = [], 0
+    for share in shares:
+        size = share * count // 4
+        cuts.append((at, size))
+        at += size
+    return cuts
 
 
 def on_device_fast(
@@ -947,73 +1321,94 @@
     all_heads = cores * w_query.shape[1] // HD
     heads = all_heads // groups
     mp_index = lax.axis_index("mp")
-    query_t, tied_t = w_query.T, w_tied.T
+    split = (lax.axis_size("dp"), lax.axis_size("seq"))
+    tied_t = w_tied.T
     tied_both = by_core(tied_t, swap_cores(tied_t), 0)
-    query_both = by_core(query_t, swap_cores(query_t), 0)
-    weights_one = jnp.concatenate([query_both, tied_both, w_rope.T], axis=0)
-    out_other = swap_cores(w_out)
-    gate_other, up_other, down_other = swap_cores(w_gate), swap_cores(w_up), swap_cores(w_down)
+    keys_weights = jnp.concatenate([tied_both, w_rope.T], axis=0)
+    query_t = w_query.T
+    queries_weights = by_core(query_t, swap_cores(query_t), 0)
+    down_other = swap_cores(w_down)
     gain_one_float = gain_one.astype(F32)[None]
     gain_two_float = gain_two.astype(F32)[None]
     cosine, sine_table = rope_tables(my_chunk() * own, own, RD)
     cosine_t, sine_t = cosine.T, sine_table.T
-    q, kv, normed_t = project(inputs, gain_one_float, weights_one, cosine_t, sine_t, all_heads)
-    kv_all = lax.all_gather(kv, ("seq", "mp"), axis=0, tiled=False)
-    heads_out, lse = attend_forward(doc_starts, q, kv_all, groups, heads)
+    kv, normed_t = project_keys(inputs, gain_one_float, keys_weights, cosine_t, sine_t)
+    forward = spans(count, (1, 1, 2))
+    gathered = [gather_keys(kv[at : at + size]) for at, size in forward]
+    q = project_queries(normed_t, queries_weights, cosine_t, sine_t)
+    slopes = unit_slopes(out_grad, (w_down, down_other))
+    out_other = swap_cores(w_out)
+    gate_other, up_other = swap_cores(w_gate), swap_cores(w_up)
+    gathered[0] = list(after(tuple(gathered[0]), slopes))
+    made = ()
+    for (at, _), kv_part in zip(forward, gathered):
+        made = attend_forward(doc_starts, q, kv_part, groups, heads, at, made)
+    heads_out, lse = made
     out_both = by_core(w_out, out_other, 0)
     (
         outputs, normed_two_t, out_grad_t, active, grad_gate, grad_up, grad_hidden, grad_attended_t,
         grad_heads, delta, grad_gain_two,
     ) = feed(
-        inputs, out_grad, heads_out, gain_two_float, out_both, (w_gate, gate_other),
+        inputs, out_grad, slopes, heads_out, gain_two_float, out_both, (w_gate, gate_other),
         (w_up, up_other), (w_down, down_other),
     )
-    unit_own, unit_other = [], []
-    for left, right in (
-        (normed_two_t, grad_gate), (normed_two_t, grad_up), (out_grad_t, active),
-    ):
-        own_part, other_part = unit_grads(left, right)
-        unit_own.append(own_part)
-        unit_other.append(swap_cores(other_part))
-    unit_sum = jnp.concatenate([a + c for a, c in zip(unit_own, unit_other)], axis=1)
-    unit_scattered = lax.psum_scatter(unit_sum, ("dp", "seq"), scatter_dimension=0, tiled=True)
-
-    dq, dkv = attend_backward(
-        doc_starts, q, grad_heads, lse, delta, kv_all, turn_tables(cosine, sine_table), groups, heads
-    )
-    dkv_own = lax.psum_scatter(dkv, ("seq", "mp"), scatter_dimension=0, tiled=False)
-    grad_out = plain_grads(grad_attended_t, heads_out, NT)
-    grad_query = plain_grads(normed_t, dq, NN)
-    grad_inputs, grad_gain_one, grad_kv = finish(
-        inputs, grad_hidden, dq, dkv_own, normed_t, gain_one_float, weights_one, cosine_t, sine_t
-    )
-    tied = groups * HD
-    grad_tied = grad_kv[:, :tied].astype(BF)
-    late_own, late_other = [], []
-    for value in (grad_query, grad_tied, grad_out):
-        half = value.shape[1] // cores
-        late_own.append(lax.dynamic_slice_in_dim(value, mp_index * half, half, 1))
-        late_other.append(lax.dynamic_slice_in_dim(value, (1 - mp_index) * half, half, 1))
-    late = jnp.concatenate(late_own, axis=1) + swap_cores(jnp.concatenate(late_other, axis=1))
-    late_sum = lax.psum_scatter(late, ("dp", "seq"), scatter_dimension=0, tiled=True)
-    small = jnp.concatenate([grad_kv[:, tied:], grad_gain_one.T, grad_gain_two.T], axis=1)
-    small_sum = lax.psum_scatter(small, ("dp", "seq", "mp"), scatter_dimension=0, tiled=True)
-    unit_scattered = unit_scattered.astype(F32)
-    late_sum = late_sum.astype(F32)
-    half_units = w_gate.shape[1]
-    query_half, tied_half = w_query.shape[1], w_tied.shape[1]
+    def unit_part(left, right, parts):
+        own_part, other_part = unit_grads(left, right, parts)
+        return own_part, swap_cores(other_part)
+
+    parts = [
+        unit_part(normed_two_t, grad_gate, split),
+        unit_part(normed_two_t, grad_up, split),
+        unit_part(out_grad_t, active, split),
+    ]
+    out = head_grads(grad_attended_t, heads_out, NT, split)
+    parts.append((out[0], swap_cores(out[1])))
+    first_sum = jnp.concatenate([mine + other for mine, other in parts], axis=1)
+    first_sum, grad_heads = lax.optimization_barrier((first_sum, grad_heads))
+    first_sum = lax.psum_scatter(first_sum, "seq", scatter_dimension=0, tiled=True)
+
+    turns = turn_tables(cosine, sine_table)
+    backward = list(zip(forward, gathered))[::-1]
+    dq, summed = (), []
+    for part, ((at, _), kv_part) in enumerate(backward):
+        first_q = q
+        if part == 1:
+            near = send_keys(summed[0])
+            first_q = after(q, near[0])
+        if part == 2:
+            first_q = after(q, *near)
+        made_dq, keep, give = attend_backward(
+            doc_starts, first_q, grad_heads, lse, delta, turns, kv_part, groups, heads, at, dq
+        )
+        dq = (made_dq,)
+        summed.append(join_cores(keep, give))
+    if len(backward) == 1:
+        near = send_keys(summed[0])
+    early = first_sum.reshape(split[0], -1, first_sum.shape[1])
+    grad_query = head_grads(normed_t, dq[0], NN, None)
+    order = [span for span, _ in backward]
+    grad_inputs, query_sum, small_sum, first_sum = tail(
+        order, inputs, grad_hidden, dq[0], normed_t, gain_one_float, queries_weights, keys_weights,
+        cosine_t, sine_t, grad_gain_two, grad_query, early, near,
+        [jnp.stack(terms) for terms in summed[1:]],
+    )
+    half_tied = groups * HD // cores
+    late_sum, small_sum = small_sum[:, :half_tied], small_sum[:, half_tied:]
+    rows = small_sum.shape[0] // cores
+    small_sum = lax.dynamic_slice_in_dim(small_sum, mp_index * rows, rows, 0)
+    units = w_gate.shape[1]
     return (
         outputs,
         grad_inputs,
         small_sum[:, RD],
-        late_sum[:, :query_half],
-        late_sum[:, query_half : query_half + tied_half],
+        query_sum,
+        late_sum,
         small_sum[:, :RD],
-        late_sum[:, query_half + tied_half :].T,
+        first_sum[:, 3 * units :].T,
         small_sum[:, RD + 1],
-        unit_scattered[:, :half_units],
-        unit_scattered[:, half_units : 2 * half_units],
-        unit_scattered[:, 2 * half_units :].T,
+        first_sum[:, :units],
+        first_sum[:, units : 2 * units],
+        first_sum[:, 2 * units : 3 * units].T,
     )
 
 

time: 940 us -> 587 us (0.62)
  waiting for transfers between devices: 579 us -> 36.6 us
  Pallas kernels: 260 us -> 366 us
  starting transfers between devices: 39.7 us -> 115 us
    reduce_scatter x3 -> x1, waiting for transfers between devices: 421 us -> 0.01 us  [on_device_fast(): lax.psum_scatter(first_sum, 'seq', scatter_dimension=0, tiled=True)]
    pallas_call x10 -> x16, Pallas kernels: 260 us -> 366 us  [the longest x1 95.2 us: tail(): pl.pallas_call(kernel, grid=(count,), in_specs=[seq, seq, pl.BlockSpec((o...]
    unnamed x6 -> x1, waiting for transfers between devices: 99.7 us -> 0.02 us
    ppermute x0 -> x12, starting transfers between devices: none -> 74.1 us  [shift(): lax.ppermute(value, axis, [(i, (i + by) % size) for i in range(size)])]
    all_gather x1 -> x0, waiting for transfers between devices: 42.9 us -> none  [on_device_fast(): kv_all = lax.all_gather(kv, ('seq', 'mp'), axis=0, tiled=False)]
    ppermute x0 -> x12, waiting for transfers between devices: none -> 29.1 us  [shift(): lax.ppermute(value, axis, [(i, (i + by) % size) for i in range(size)])]
    ppermute x10 -> x25, starting transfers between devices: 39.4 us -> 40.9 us  [swap_cores(): return lax.ppermute(value, 'mp', [(0, 1), (1, 0)])]
  transfers between devices with their start and end apart: 15 -> 38, of which waited for: 7 -> 9; matrix products, arithmetic and copies ran while one was open for 4% -> 4% of each run, Pallas kernels for 9% -> 28%
where the time goes in v2:
time: 587 us; the launch traced here: 585 us
  Pallas kernels  366 us (62%)
  starting transfers between devices  115 us (20%)
  waiting for transfers between devices  36.6 us (6%)
  other arithmetic  26.7 us (5%)
  local copies, waits for them, and re-layouts  25.5 us (4%)
  between operations  15.2 us (3%)
    pallas_call x1, Pallas kernels, tail(): pl.pallas_call(kernel, grid=(count,), in_specs=[seq, seq, pl.BlockSpec((o...  95.2 us
    pallas_call x1, Pallas kernels, feed(): pl.pallas_call(feed_kernel, grid=(count,), in_specs=[seq, seq, row, colum...  88.5 us
    ppermute x12, starting transfers between devices, shift(): lax.ppermute(value, axis, [(i, (i + by) % size) for i in range(size)])  74.1 us
    pallas_call x3, Pallas kernels, unit_grads(): pl.pallas_call(functools.partial(unit_grads_kernel, split), grid=(units /...  54.3 us
    pallas_call x3, Pallas kernels, attend_backward(): pl.pallas_call(functools.partial(attend_back_kernel, groups, heads, first...  49.6 us
    ppermute x25, starting transfers between devices, swap_cores(): return lax.ppermute(value, 'mp', [(0, 1), (1, 0)])  40.9 us
    ppermute x12, waiting for transfers between devices, shift(): lax.ppermute(value, axis, [(i, (i + by) % size) for i in range(size)])  29.1 us
    pallas_call x3, Pallas kernels, attend_forward(): pl.pallas_call(functools.partial(attend_kernel, groups, heads, first, chu...  23.3 us
  transfers between devices with their start and end apart: 38, of which 9 were waited for; matrix products, arithmetic and copies ran while one was open for 4% of the time, Pallas kernels for 28%

profile of v2, /device:TPU:0, one launch (start us, length us, event | category | flops | bytes accessed | tf_op | source)
XLA Modules:
  0.0 584.8 jit_solution(11953700771256728115)
XLA Ops:
  7.8 1.1 copy.33
  9.1 1.5 copy.34
  12.4 0.8 multiply_sine_fusion.1
  13.6 1.0 broadcast_select_fusion.5
  14.6 0.9 pad_maximum_fusion.5.w_ref.refs_6_
  15.4 8.1 %project_keys.1 = (bf16[8,288,256]{2,1,0:T(8,128)(2,1)}, bf16[1024,2048]{1,0:T(8,128)(2,1)}) custom-call(bf16[8,256,1024]{2,1,0:T(8,128)(2,1)} %refs_0_.1, f32[1,1024]{1,0:T(1,128)} %bitcast.38, bf16[288,1024]{1,0:T(8,128)(2,1)} %pad_maximum_fusion.5.w_ref.refs_6_, f32[16,256]{1,0:T(8,128)} %get-tuple-element.142.cos_ref.refs_7_, ...), custom_call_target="tpu_custom_call" | custom-call | flops 1207959552 | bytes 8388608 | tf_op jit(solution)/shard_map/project_keys/pallas_call | solution.py:403
  23.5 1.1 fusion.6
  24.7 2.9 collective-permute-start.17
  27.6 1.5 collective-permute-start.18
  29.1 1.1 slice.114.refs_0_
  30.2 1.5 collective-permute-start.19
  31.7 1.5 broadcast_select_fusion.1
  33.2 1.5 pad_maximum_fusion.1.w_ref.refs_5_
  34.7 1.5 pad_maximum_fusion.2.wo_ref
  36.4 1.1 collective-permute-start.10
  37.4 5.2 collective-permute-done.18.refs_2_
  43.3 0.7 copy-done.27
  44.0 10.1 %project_queries.1.q_ref = bf16[1024,2048]{1,0:T(8,128)(2,1)} custom-call(bf16[1024,2048]{1,0:T(8,128)(2,1)} %get-tuple-element.61.nt_ref.left_ref.refs_3_, bf16[1024,1024]{1,0:T(8,128)(2,1)} %pad_maximum_fusion.1.w_ref.refs_5_, f32[16,256]{1,0:T(8,128)} %get-tuple-element.142.cos_ref.refs_7_, f32[16,256]{1,0:T(8,128)} %get-tuple-element.141.sin_ref.refs_8_), custom_call_target="tpu_custom_call" | custom-call | flops 4294967296 | bytes 8388608 | tf_op jit(solution)/shard_map/project_queries/pallas_call | solution.py:443
  54.1 1.9 collective-permute-start.11
  56.1 1.1 collective-permute-start.12
  57.9 19.0 %unit_slopes.1.ga_ref = bf16[2048,2816]{1,0:T(8,128)(2,1)} custom-call(bf16[8,256,1024]{2,1,0:T(8,128)(2,1)} %og_ref.3, bf16[1408,1024]{1,0:T(8,128)(2,1)} %wdo_ref.3, bf16[1408,1024]{1,0:T(8,128)(2,1)} %collective-permute-done.wdp_ref), custom_call_target="tpu_custom_call" | custom-call | flops 11811160064 | tf_op jit(solution)/shard_map/unit_slopes/pallas_call | solution.py:840
  77.0 1.0 collective-permute-start.3
  78.1 2.5 collective-permute-start.5
  81.2 6.4 %attend.3 = (bf16[1024,2048]{1,0:T(8,128)(2,1)}, f32[8,4,1024]{2,1,0:T(4,128)}) custom-call(s32[8,8]{1,0:T(8,128)} %docs_ref.11, bf16[1024,2048]{1,0:T(8,128)(2,1)} %project_queries.1.q_ref, bf16[2,288,256]{2,1,0:T(8,128)(2,1)} %copy-done.7, bf16[2,288,256]{2,1,0:T(8,128)(2,1)} %copy-done.25, bf16[2,288,256]{2,1,0:T(8,128)(2,1)} %copy-done.26, ...), custom_call_target="tpu_custom_call" | custom-call | flops 20000000000 | tf_op jit(solution)/shard_map/attend/pallas_call | solution.py:597
  87.7 4.5 collective-permute-start.25
  92.2 1.9 collective-permute-done.3.refs_1_
  94.1 11.9 %collective-permute-done.4.refs_2_ = bf16[4,288,256]{2,1,0:T(8,128)(2,1)S(1)} collective-permute-done((bf16[4,288,256]{2,1,0:T(8,128)(2,1)S(1)}, bf16[4,288,256]{2,1,0:T(8,128)(2,1)S(1)}, u32[]{:S(2)}, u32[]{:S(2)}) %collective-permute-start.4) | collective-permute-done | bytes 589856 | tf_op jit(solution)/shard_map/ppermute | solution.py:367
  106.5 6.5 %attend.4 = (bf16[1024,2048]{1,0:T(8,128)(2,1)}, f32[8,4,1024]{2,1,0:T(4,128)}) custom-call(s32[8,8]{1,0:T(8,128)} %docs_ref.11, bf16[1024,2048]{1,0:T(8,128)(2,1)} %project_queries.1.q_ref, bf16[2,288,256]{2,1,0:T(8,128)(2,1)} %copy-done.8, bf16[2,288,256]{2,1,0:T(8,128)(2,1)} %copy-done.31, ...), custom_call_target="tpu_custom_call", output_to_operand_aliasing={{0}: (10, {}), {1}: (11, {})} | custom-call | flops 20000000000 | tf_op jit(solution)/shard_map/attend/pallas_call | solution.py:597
  113.1 4.4 collective-permute-start.26
  117.5 10.4 %attend.5 = (bf16[1024,2048]{1,0:T(8,128)(2,1)}, f32[8,4,1024]{2,1,0:T(4,128)}) custom-call(s32[8,8]{1,0:T(8,128)} %docs_ref.11, bf16[1024,2048]{1,0:T(8,128)(2,1)} %project_queries.1.q_ref, bf16[4,288,256]{2,1,0:T(8,128)(2,1)} %copy-done.6, bf16[4,288,256]{2,1,0:T(8,128)(2,1)} %copy-done.20, ...), custom_call_target="tpu_custom_call", output_to_operand_aliasing={{0}: (10, {}), {1}: (11, {})} | custom-call | flops 40000000000 | tf_op jit(solution)/shard_map/attend/pallas_call | solution.py:597
  128.0 88.5 %feed.1 = (bf16[8,256,1024]{2,1,0:T(8,128)(2,1)}, bf16[1024,2048]{1,0:T(8,128)(2,1)}, bf16[1024,2048]{1,0:T(8,128)(2,1)}, bf16[2048,2816]{1,0:T(8,128)(2,1)}, bf...) custom-call(bf16[8,256,1024]{2,1,0:T(8,128)(2,1)} %refs_0_.1, ...), custom_call_target="tpu_custom_call" | custom-call | flops 67645734912 | tf_op jit(solution)/shard_map/feed/pallas_call | solution.py:927
  216.5 18.1 %unit_grads.3 = (bf16[1024,1408]{1,0:T(8,128)(2,1)}, bf16[1024,1408]{1,0:T(8,128)(2,1)}) custom-call(bf16[1024,2048]{1,0:T(8,128)(2,1)} %get-tuple-element.78.left_ref, bf16[2048,2816]{1,0:T(8,128)(2,1)} %get-tuple-element.79.right_ref), custom_call_target="tpu_custom_call" | custom-call | flops 11811160064 | tf_op jit(solution)/shard_map/unit_grads/pallas_call | solution.py:988
  234.6 8.6 %collective-permute-start.27 = (bf16[1024,1408]{1,0:T(8,128)(2,1)}, bf16[1024,1408]{1,0:T(8,128)(2,1)S(1)}, u32[]{:S(2)}, u32[]{:S(2)}) collective-permute-start(bf16[1024,1408]{1,0:T(8,128)(2,1)} %get-tuple-element.81), channel_id=1, source_target_pairs={{0,1},{1,0},{2,3},{3,2},{4,5},{5,4},{6,7},{7,6},{8,9},{9,8},{10,11... | collective-permute-start | bytes 8650760 | tf_op jit(solution)/shard_map/ppermute | solution.py:362
  243.3 18.1 %unit_grads.4 = (bf16[1024,1408]{1,0:T(8,128)(2,1)}, bf16[1024,1408]{1,0:T(8,128)(2,1)}) custom-call(bf16[1024,2048]{1,0:T(8,128)(2,1)} %get-tuple-element.78.left_ref, bf16[2048,2816]{1,0:T(8,128)(2,1)} %get-tuple-element.82.right_ref), custom_call_target="tpu_custom_call" | custom-call | flops 11811160064 | tf_op jit(solution)/shard_map/unit_grads/pallas_call | solution.py:988
  261.3 18.1 %unit_grads.5 = (bf16[1024,1408]{1,0:T(8,128)(2,1)}, bf16[1024,1408]{1,0:T(8,128)(2,1)}) custom-call(bf16[1024,2048]{1,0:T(8,128)(2,1)} %get-tuple-element.85.left_ref, bf16[2048,2816]{1,0:T(8,128)(2,1)} %get-tuple-element.86.right_ref), custom_call_target="tpu_custom_call" | custom-call | flops 11811160064 | tf_op jit(solution)/shard_map/unit_grads/pallas_call | solution.py:988
  279.9 8.9 %head_grads.2 = bf16[2,1024,512]{2,1,0:T(8,128)(2,1)} custom-call(s32[1]{0:T(128)} %bitcast.5.core_ref, bf16[1024,2048]{1,0:T(8,128)(2,1)} %get-tuple-element.89.left_ref, bf16[1024,2048]{1,0:T(8,128)(2,1)} %get-tuple-element.75.o_ref.right_ref), custom_call_target="tpu_custom_call" | custom-call | flops 4294967296 | tf_op jit(solution)/shard_map/head_grads/pallas_call | solution.py:1019
  288.9 1.4 slice_bitcast_fusion
  290.4 2.6 collective-permute-done.30
  293.0 1.4 fusion
  294.4 0.7 add.81
  295.1 1.1 copy-done.1
  296.2 0.7 add.82
  297.0 1.1 copy-done.2
  298.0 2.5 add.83
  300.6 5.5 pad_maximum_fusion
  308.2 0.8 pad_maximum_fusion.6.rot_ref
  308.9 23.0 %attend_back.3 = (bf16[2048,1024]{1,0:T(8,128)(2,1)}, bf16[4,4,288,256]{3,2,1,0:T(8,128)(2,1)}, bf16[4,4,288,256]{3,2,1,0:T(8,128)(2,1)}) custom-call(s32[8,8]{1,0:T(8,128)} %docs_ref.11, bf16[1024,2048]{1,0:T(8,128)(2,1)} %project_queries.1.q_ref, bf16[1024,2048]{1,0:T(8,128)(2,1)} %get-tuple-element.91.do_ref, f32[8,4,1024]{2,1,0:T(4,128)} %get-tuple-element.92.lse_ref, ...), custom_call_target="tpu_custom_call" | custom-call | flops 60000002048 | tf_op jit(solution)/shard_map/attend_back/pallas_call | solution.py:756
  331.9 10.1 %collective-permute-start.31 = (bf16[4,4,288,256]{3,2,1,0:T(8,128)(2,1)}, bf16[4,4,288,256]{3,2,1,0:T(8,128)(2,1)S(1)}, u32[]{:S(2)}, u32[]{:S(2)}) collective-permute-start(bf16[4,4,288,256]{3,2,1,0:T(8,128)(2,1)} %get-tuple-element.95), channel_id=1, source_target_pairs={{0,1},{1,0},{2,3},{3,2},{4,5},{5,4},{6,7},{7,6},{8,9},{9,8},{10,11... | collective-permute-start | bytes 7077896 | tf_op jit(solution)/shard_map/ppermute | solution.py:362
  342.0 4.4 collective-permute-done.31
  346.4 3.2 fusion.4
  349.6 22.2 %collective-permute-start.32 = (bf16[4,288,256]{2,1,0:T(8,128)(2,1)S(1)}, bf16[4,288,256]{2,1,0:T(8,128)(2,1)S(1)}, u32[]{:S(2)}, u32[]{:S(2)}) collective-permute-start(bf16[4,288,256]{2,1,0:T(8,128)(2,1)S(1)} %get-tuple-element.115), channel_id=1, source_target_pairs={{0,2},{2,4},{4,6},{6,0},{1,3},{3,5},{5,7},{7,1},{8,10},{10,12},{12... | collective-permute-start | bytes 1769480 | tf_op jit(solution)/shard_map/ppermute | solution.py:367
  371.9 38.2 %collective-permute-start.33 = (bf16[4,288,256]{2,1,0:T(8,128)(2,1)S(1)}, bf16[4,288,256]{2,1,0:T(8,128)(2,1)S(1)}, u32[]{:S(2)}, u32[]{:S(2)}) collective-permute-start(bf16[4,288,256]{2,1,0:T(8,128)(2,1)S(1)} %get-tuple-element.114), channel_id=1, source_target_pairs={{0,4},{2,6},{4,0},{6,2},{1,5},{3,7},{5,1},{7,3},{8,12},{10,14},{12... | collective-permute-start | bytes 1769480 | tf_op jit(solution)/shard_map/ppermute | solution.py:367
  410.0 13.1 %attend_back.4 = (bf16[2048,1024]{1,0:T(8,128)(2,1)}, bf16[4,2,288,256]{3,2,1,0:T(8,128)(2,1)}, bf16[4,2,288,256]{3,2,1,0:T(8,128)(2,1)}) custom-call(s32[8,8]{1,0:T(8,128)} %docs_ref.11, bf16[1024,2048]{1,0:T(8,128)(2,1)} %project_queries.1.q_ref, bf16[1024,2048]{1,0:T(8,128)(2,1)} %get-tuple-element.91.do_ref, ...), custom_call_target="tpu_custom_call", output_to_operand_aliasing={{0}: (14, {})} | custom-call | flops 30000001024 | tf_op jit(solution)/shard_map/attend_back/pallas_call | solution.py:756
  423.1 4.6 collective-permute-start.35
  427.7 9.3 %collective-permute-done.33.refs_14_ = bf16[4,288,256]{2,1,0:T(8,128)(2,1)S(1)} collective-permute-done((bf16[4,288,256]{2,1,0:T(8,128)(2,1)S(1)}, bf16[4,288,256]{2,1,0:T(8,128)(2,1)S(1)}, u32[]{:S(2)}, u32[]{:S(2)}) %collective-permute-start.33) | collective-permute-done | bytes 589856 | tf_op jit(solution)/shard_map/ppermute | solution.py:367
  437.0 13.5 %attend_back.5 = (bf16[2048,1024]{1,0:T(8,128)(2,1)}, bf16[4,2,288,256]{3,2,1,0:T(8,128)(2,1)}, bf16[4,2,288,256]{3,2,1,0:T(8,128)(2,1)}) custom-call(s32[8,8]{1,0:T(8,128)} %docs_ref.11, bf16[1024,2048]{1,0:T(8,128)(2,1)} %project_queries.1.q_ref, bf16[1024,2048]{1,0:T(8,128)(2,1)} %get-tuple-element.91.do_ref, ...), custom_call_target="tpu_custom_call", output_to_operand_aliasing={{0}: (14, {})} | custom-call | flops 30000001024 | tf_op jit(solution)/shard_map/attend_back/pallas_call | solution.py:756
  450.5 5.0 collective-permute-start.36
  455.5 8.8 %head_grads.3.refs_10_ = bf16[2,1024,512]{2,1,0:T(8,128)(2,1)} custom-call(s32[1]{0:T(128)} %bitcast.5.core_ref, bf16[1024,2048]{1,0:T(8,128)(2,1)} %get-tuple-element.61.nt_ref.left_ref.refs_3_, bf16[2048,1024]{1,0:T(8,128)(2,1)} %get-tuple-element.100.right_ref.refs_2_), custom_call_target="tpu_custom_call" | custom-call | flops 4294967296 | tf_op jit(solution)/shard_map/head_grads/pallas_call | solution.py:1019
  464.7 1.2 pad_maximum_fusion.3.refs_16_
  466.2 1.2 pad_maximum_fusion.4.refs_17_
  467.4 95.2 %tail.1 = (f32[8,256,1024]{2,1,0:T(8,128)}, f32[64,512]{1,0:T(8,128)}, f32[64,256]{1,0:T(8,128)}, f32[64,4736]{1,0:T(8,128)}) custom-call(bf16[8,256,1024]{2,1,0:T(8,128)(2,1)} %refs_0_.1, f32[8,256,1024]{2,1,0:T(8,128)} %get-tuple-element.77.refs_1_, bf16[2048,1024]{1,0:T(8,128)(2,1)} %get-tuple-element.100.right_ref.refs_2_, ...), custom_call_target="tpu_custom_call" | custom-call | flops 40000000000 | tf_op jit(solution)/shard_map/tail/pallas_call | solution.py:1248
  562.6 2.2 slice_bitcast_fusion.2
  564.8 1.6 slice_bitcast_fusion.3
  568.3 8.5 %copy.44 = f32[8,256,1024]{2,1,0:T(8,128)} copy(f32[8,256,1024]{2,1,0:T(8,128)} %get-tuple-element.157) | data formatting | bytes 16777216
  (147 shorter events, 11.7 us)
Async XLA Ops:
  7.2 7.4 %copy-start.10 = (bf16[1024,32]{0,1:T(8,128)(2,1)S(1)}, bf16[1024,32]{0,1:T(8,128)(2,1)}, u32[]{:S(2)}) copy-start(bf16[1024,32]{0,1:T(8,128)(2,1)} %param.16) | copy-start | bytes 196612
  7.2 460.1 %reduce-scatter.2.cloned.1.call-start = ((), (), s32[]{:S(2)}) async-start(), calls=%async_computation.1 | async-start | bytes 12124160 | tf_op jit(solution)/shard_map/reduce_scatter | solution.py:1368
  7.3 50.5 %collective-permute-start = (bf16[1408,1024]{1,0:T(8,128)(2,1)}, bf16[1408,1024]{1,0:T(8,128)(2,1)}, u32[]{:S(2)}, u32[]{:S(2)}) collective-permute-start(bf16[1408,1024]{1,0:T(8,128)(2,1)} %wdo_ref.3), channel_id=1, source_target_pairs={{0,1},{1,0},{2,3},{3,2},{4,5},{5,4},{6,7},{7,6},{8,9},{9,8},{10,11... | collective-permute-start | bytes 8650760 | tf_op jit(solution)/shard_map/ppermute | solution.py:362
  8.9 4.7 collective-permute-start.1
  10.6 19.6 %collective-permute-start.2 = (bf16[512,1024]{1,0:T(8,128)(2,1)S(1)}, bf16[512,1024]{1,0:T(8,128)(2,1)S(1)}, u32[]{:S(2)}, u32[]{:S(2)}) collective-permute-start(bf16[512,1024]{1,0:T(8,128)(2,1)S(1)} %bitcast.32), channel_id=1, source_target_pairs={{0,1},{1,0},{2,3},{3,2},{4,5},{5,4},{6,7},{7,6},{8,9},{9,8},{10,11... | collective-permute-start | bytes 3145736 | tf_op jit(solution)/shard_map/ppermute | solution.py:362
  11.0 20.7 %collective-permute-start.24 = (bf16[512,1024]{1,0:T(8,128)(2,1)S(1)}, bf16[512,1024]{1,0:T(8,128)(2,1)}, u32[]{:S(2)}, u32[]{:S(2)}) collective-permute-start(bf16[512,1024]{1,0:T(8,128)(2,1)S(1)} %copy-done.5), channel_id=1, source_target_pairs={{0,1},{1,0},{2,3},{3,2},{4,5},{5,4},{6,7},{7,6},{8,9},{9,8},{10,11... | collective-permute-start | bytes 3145736 | tf_op jit(solution)/shard_map/ppermute | solution.py:362
  11.2 12.4 %copy-start.12 = (f32[256]{0:T(256)}, f32[256]{0:T(256)S(1)}, u32[]{:S(2)}) copy-start(f32[256]{0:T(256)S(1)} %add_convert_fusion.12) | copy-start | bytes 3076
  11.2 12.4 %copy-start.14 = (f32[16]{0:T(128)}, f32[16]{0:T(128)S(1)}, u32[]{:S(2)}) copy-start(f32[16]{0:T(128)S(1)} %multiply_power_fusion) | copy-start | bytes 196
  24.6 8.6 %copy-start.7 = (bf16[2,288,256]{2,1,0:T(8,128)(2,1)}, bf16[2,288,256]{2,1,0:T(8,128)(2,1)S(1)}, u32[]{:S(2)}) copy-start(bf16[2,288,256]{2,1,0:T(8,128)(2,1)S(1)} %get-tuple-element.63.refs_0_) | copy-start | bytes 884740
  24.7 32.5 %copy-start.8 = (bf16[2,288,256]{2,1,0:T(8,128)(2,1)}, bf16[2,288,256]{2,1,0:T(8,128)(2,1)S(1)}, u32[]{:S(2)}) copy-start(bf16[2,288,256]{2,1,0:T(8,128)(2,1)S(1)} %get-tuple-element.133.refs_0_) | copy-start | bytes 884740
  24.7 11.7 %collective-permute-start.17 = (bf16[2,288,256]{2,1,0:T(8,128)(2,1)S(1)}, bf16[2,288,256]{2,1,0:T(8,128)(2,1)S(1)}, u32[]{:S(2)}, u32[]{:S(2)}) collective-permute-start(bf16[2,288,256]{2,1,0:T(8,128)(2,1)S(1)} %get-tuple-element.63.refs_0_), channel_id=1, source_target_pairs={{0,2},{2,4},{4,6},{6,0},{1,3},{3,5},{5,7},{7,1},{8,10},{10,12},{12... | collective-permute-start | bytes 884744 | tf_op jit(solution)/shard_map/ppermute | solution.py:367
  27.6 15.0 %collective-permute-start.18 = (bf16[2,288,256]{2,1,0:T(8,128)(2,1)S(1)}, bf16[2,288,256]{2,1,0:T(8,128)(2,1)S(1)}, u32[]{:S(2)}, u32[]{:S(2)}) collective-permute-start(bf16[2,288,256]{2,1,0:T(8,128)(2,1)S(1)} %get-tuple-element.63.refs_0_), channel_id=1, source_target_pairs={{0,4},{2,6},{4,0},{6,2},{1,5},{3,7},{5,1},{7,3},{8,12},{10,14},{12... | collective-permute-start | bytes 884744 | tf_op jit(solution)/shard_map/ppermute | solution.py:367
  30.2 61.9 %copy-start.6 = (bf16[4,288,256]{2,1,0:T(8,128)(2,1)}, bf16[4,288,256]{2,1,0:T(8,128)(2,1)S(1)}, u32[]{:S(2)}) copy-start(bf16[4,288,256]{2,1,0:T(8,128)(2,1)S(1)} %slice.114.refs_0_) | copy-start | bytes 1769476
  30.2 13.0 %collective-permute-start.19 = (bf16[2,288,256]{2,1,0:T(8,128)(2,1)S(1)}, bf16[2,288,256]{2,1,0:T(8,128)(2,1)S(1)}, u32[]{:S(2)}, u32[]{:S(2)}) collective-permute-start(bf16[2,288,256]{2,1,0:T(8,128)(2,1)S(1)} %get-tuple-element.63.refs_0_), channel_id=1, source_target_pairs={{0,6},{2,0},{4,2},{6,4},{1,7},{3,1},{5,3},{7,5},{8,14},{10,8},{12,... | collective-permute-start | bytes 884744 | tf_op jit(solution)/shard_map/ppermute | solution.py:367
  31.7 22.4 %collective-permute-start.20 = (bf16[2,288,256]{2,1,0:T(8,128)(2,1)S(1)}, bf16[2,288,256]{2,1,0:T(8,128)(2,1)}, u32[]{:S(2)}, u32[]{:S(2)}) collective-permute-start(bf16[2,288,256]{2,1,0:T(8,128)(2,1)S(1)} %get-tuple-element.63.refs_0_), channel_id=1, source_target_pairs={{0,1},{1,0},{2,3},{3,2},{4,5},{5,4},{6,7},{7,6},{8,9},{9,8},{10,11... | collective-permute-start | bytes 884744 | tf_op jit(solution)/shard_map/ppermute | solution.py:362
  36.4 17.7 %copy-start.25 = (bf16[2,288,256]{2,1,0:T(8,128)(2,1)}, bf16[2,288,256]{2,1,0:T(8,128)(2,1)S(1)}, u32[]{:S(2)}) copy-start(bf16[2,288,256]{2,1,0:T(8,128)(2,1)S(1)} %collective-permute-done.17.refs_1_) | copy-start | bytes 884740
  36.4 19.7 %collective-permute-start.10 = (bf16[2,288,256]{2,1,0:T(8,128)(2,1)S(1)}, bf16[2,288,256]{2,1,0:T(8,128)(2,1)S(1)}, u32[]{:S(2)}, u32[]{:S(2)}) collective-permute-start(bf16[2,288,256]{2,1,0:T(8,128)(2,1)S(1)} %get-tuple-element.133.refs_0_), channel_id=1, source_target_pairs={{0,2},{2,4},{4,6},{6,0},{1,3},{3,5},{5,7},{7,1},{8,10},{10,12},{12... | collective-permute-start | bytes 884744 | tf_op jit(solution)/shard_map/ppermute | solution.py:367
  42.6 11.5 %copy-start.26 = (bf16[2,288,256]{2,1,0:T(8,128)(2,1)}, bf16[2,288,256]{2,1,0:T(8,128)(2,1)S(1)}, u32[]{:S(2)}) copy-start(bf16[2,288,256]{2,1,0:T(8,128)(2,1)S(1)} %collective-permute-done.18.refs_2_) | copy-start | bytes 884740
  42.6 14.5 %collective-permute-start.21 = (bf16[2,288,256]{2,1,0:T(8,128)(2,1)S(1)}, bf16[2,288,256]{2,1,0:T(8,128)(2,1)S(1)}, u32[]{:S(2)}, u32[]{:S(2)}) collective-permute-start(bf16[2,288,256]{2,1,0:T(8,128)(2,1)S(1)} %collective-permute-done.17.refs_1_), channel_id=1, source_target_pairs={{0,1},{1,0},{2,3},{3,2},{4,5},{5,4},{6,7},{7,6},{8,9},{9,8},{10,11... | collective-permute-start | bytes 884744 | tf_op jit(solution)/shard_map/ppermute | solution.py:362
  44.0 13.2 %collective-permute-start.22 = (bf16[2,288,256]{2,1,0:T(8,128)(2,1)S(1)}, bf16[2,288,256]{2,1,0:T(8,128)(2,1)S(1)}, u32[]{:S(2)}, u32[]{:S(2)}) collective-permute-start(bf16[2,288,256]{2,1,0:T(8,128)(2,1)S(1)} %collective-permute-done.18.refs_2_), channel_id=1, source_target_pairs={{0,1},{1,0},{2,3},{3,2},{4,5},{5,4},{6,7},{7,6},{8,9},{9,8},{10,11... | collective-permute-start | bytes 884744 | tf_op jit(solution)/shard_map/ppermute | solution.py:362
  44.0 13.3 %copy-start.28 = (bf16[2,288,256]{2,1,0:T(8,128)(2,1)S(1)}, bf16[2,288,256]{2,1,0:T(8,128)(2,1)}, u32[]{:S(2)}) copy-start(bf16[2,288,256]{2,1,0:T(8,128)(2,1)} %copy-done.27) | copy-start | bytes 884740
  54.1 23.8 %collective-permute-start.11 = (bf16[2,288,256]{2,1,0:T(8,128)(2,1)S(1)}, bf16[2,288,256]{2,1,0:T(8,128)(2,1)S(1)}, u32[]{:S(2)}, u32[]{:S(2)}) collective-permute-start(bf16[2,288,256]{2,1,0:T(8,128)(2,1)S(1)} %get-tuple-element.133.refs_0_), channel_id=1, source_target_pairs={{0,4},{2,6},{4,0},{6,2},{1,5},{3,7},{5,1},{7,3},{8,12},{10,14},{12... | collective-permute-start | bytes 884744 | tf_op jit(solution)/shard_map/ppermute | solution.py:367
  56.1 20.8 %copy-start.31 = (bf16[2,288,256]{2,1,0:T(8,128)(2,1)}, bf16[2,288,256]{2,1,0:T(8,128)(2,1)S(1)}, u32[]{:S(2)}) copy-start(bf16[2,288,256]{2,1,0:T(8,128)(2,1)S(1)} %collective-permute-done.10.refs_1_) | copy-start | bytes 884740
  56.1 22.1 %collective-permute-start.12 = (bf16[2,288,256]{2,1,0:T(8,128)(2,1)S(1)}, bf16[2,288,256]{2,1,0:T(8,128)(2,1)S(1)}, u32[]{:S(2)}, u32[]{:S(2)}) collective-permute-start(bf16[2,288,256]{2,1,0:T(8,128)(2,1)S(1)} %get-tuple-element.133.refs_0_), channel_id=1, source_target_pairs={{0,6},{2,0},{4,2},{6,4},{1,7},{3,1},{5,3},{7,5},{8,14},{10,8},{12,... | collective-permute-start | bytes 884744 | tf_op jit(solution)/shard_map/ppermute | solution.py:367
  57.2 19.8 %copy-start.29 = (bf16[2,288,256]{2,1,0:T(8,128)(2,1)}, bf16[2,288,256]{2,1,0:T(8,128)(2,1)S(1)}, u32[]{:S(2)}) copy-start(bf16[2,288,256]{2,1,0:T(8,128)(2,1)S(1)} %collective-permute-done.21.refs_5_) | copy-start | bytes 884740
  57.2 23.5 %collective-permute-start.13 = (bf16[2,288,256]{2,1,0:T(8,128)(2,1)S(1)}, bf16[2,288,256]{2,1,0:T(8,128)(2,1)S(1)}, u32[]{:S(2)}, u32[]{:S(2)}) collective-permute-start(bf16[2,288,256]{2,1,0:T(8,128)(2,1)S(1)} %get-tuple-element.133.refs_0_), channel_id=1, source_target_pairs={{0,1},{1,0},{2,3},{3,2},{4,5},{5,4},{6,7},{7,6},{8,9},{9,8},{10,11... | collective-permute-start | bytes 884744 | tf_op jit(solution)/shard_map/ppermute | solution.py:362
  57.3 19.7 %copy-start.30 = (bf16[2,288,256]{2,1,0:T(8,128)(2,1)}, bf16[2,288,256]{2,1,0:T(8,128)(2,1)S(1)}, u32[]{:S(2)}) copy-start(bf16[2,288,256]{2,1,0:T(8,128)(2,1)S(1)} %collective-permute-done.22.refs_6_) | copy-start | bytes 884740
  57.3 19.7 %collective-permute-start.23 = (bf16[2,288,256]{2,1,0:T(8,128)(2,1)S(1)}, bf16[2,288,256]{2,1,0:T(8,128)(2,1)S(1)}, u32[]{:S(2)}, u32[]{:S(2)}) collective-permute-start(bf16[2,288,256]{2,1,0:T(8,128)(2,1)S(1)} %copy-done.28), channel_id=1, source_target_pairs={{0,1},{1,0},{2,3},{3,2},{4,5},{5,4},{6,7},{7,6},{8,9},{9,8},{10,11... | collective-permute-start | bytes 884744 | tf_op jit(solution)/shard_map/ppermute | solution.py:362
  57.8 22.9 %collective-permute-start.14 = (bf16[2,288,256]{2,1,0:T(8,128)(2,1)S(1)}, bf16[2,288,256]{2,1,0:T(8,128)(2,1)S(1)}, u32[]{:S(2)}, u32[]{:S(2)}) collective-permute-start(bf16[2,288,256]{2,1,0:T(8,128)(2,1)S(1)} %collective-permute-done.10.refs_1_), channel_id=1, source_target_pairs={{0,1},{1,0},{2,3},{3,2},{4,5},{5,4},{6,7},{7,6},{8,9},{9,8},{10,11... | collective-permute-start | bytes 884744 | tf_op jit(solution)/shard_map/ppermute | solution.py:362
  76.9 10.7 %copy-start.18 = (bf16[1024,1408]{1,0:T(8,128)(2,1)S(1)}, bf16[1024,1408]{1,0:T(8,128)(2,1)}, u32[]{:S(2)}) copy-start(bf16[1024,1408]{1,0:T(8,128)(2,1)} %wgo_ref.1) | copy-start | bytes 8650756
  77.0 17.1 %collective-permute-start.3 = (bf16[4,288,256]{2,1,0:T(8,128)(2,1)S(1)}, bf16[4,288,256]{2,1,0:T(8,128)(2,1)S(1)}, u32[]{:S(2)}, u32[]{:S(2)}) collective-permute-start(bf16[4,288,256]{2,1,0:T(8,128)(2,1)S(1)} %slice.114.refs_0_), channel_id=1, source_target_pairs={{0,2},{2,4},{4,6},{6,0},{1,3},{3,5},{5,7},{7,1},{8,10},{10,12},{12... | collective-permute-start | bytes 1769480 | tf_op jit(solution)/shard_map/ppermute | solution.py:367
  78.0 9.6 %copy-start.33 = (bf16[2,288,256]{2,1,0:T(8,128)(2,1)}, bf16[2,288,256]{2,1,0:T(8,128)(2,1)S(1)}, u32[]{:S(2)}) copy-start(bf16[2,288,256]{2,1,0:T(8,128)(2,1)S(1)} %collective-permute-done.11.refs_2_) | copy-start | bytes 884740
  78.0 28.0 %collective-permute-start.4 = (bf16[4,288,256]{2,1,0:T(8,128)(2,1)S(1)}, bf16[4,288,256]{2,1,0:T(8,128)(2,1)S(1)}, u32[]{:S(2)}, u32[]{:S(2)}) collective-permute-start(bf16[4,288,256]{2,1,0:T(8,128)(2,1)S(1)} %slice.114.refs_0_), channel_id=1, source_target_pairs={{0,4},{2,6},{4,0},{6,2},{1,5},{3,7},{5,1},{7,3},{8,12},{10,14},{12... | collective-permute-start | bytes 1769480 | tf_op jit(solution)/shard_map/ppermute | solution.py:367
  78.1 9.5 %copy-start.34 = (bf16[2,288,256]{2,1,0:T(8,128)(2,1)}, bf16[2,288,256]{2,1,0:T(8,128)(2,1)S(1)}, u32[]{:S(2)}) copy-start(bf16[2,288,256]{2,1,0:T(8,128)(2,1)S(1)} %collective-permute-done.12.refs_3_) | copy-start | bytes 884740
  78.1 27.9 %collective-permute-start.5 = (bf16[4,288,256]{2,1,0:T(8,128)(2,1)S(1)}, bf16[4,288,256]{2,1,0:T(8,128)(2,1)}, u32[]{:S(2)}, u32[]{:S(2)}) collective-permute-start(bf16[4,288,256]{2,1,0:T(8,128)(2,1)S(1)} %slice.114.refs_0_), channel_id=1, source_target_pairs={{0,6},{2,0},{4,2},{6,4},{1,7},{3,1},{5,3},{7,5},{8,14},{10,8},{12,... | collective-permute-start | bytes 1769480 | tf_op jit(solution)/shard_map/ppermute | solution.py:367
  80.7 6.9 %copy-start.35 = (bf16[2,288,256]{2,1,0:T(8,128)(2,1)}, bf16[2,288,256]{2,1,0:T(8,128)(2,1)S(1)}, u32[]{:S(2)}) copy-start(bf16[2,288,256]{2,1,0:T(8,128)(2,1)S(1)} %collective-permute-done.13.refs_4_) | copy-start | bytes 884740
  80.7 7.0 %collective-permute-start.15 = (bf16[2,288,256]{2,1,0:T(8,128)(2,1)S(1)}, bf16[2,288,256]{2,1,0:T(8,128)(2,1)S(1)}, u32[]{:S(2)}, u32[]{:S(2)}) collective-permute-start(bf16[2,288,256]{2,1,0:T(8,128)(2,1)S(1)} %collective-permute-done.11.refs_2_), channel_id=1, source_target_pairs={{0,1},{1,0},{2,3},{3,2},{4,5},{5,4},{6,7},{7,6},{8,9},{9,8},{10,11... | collective-permute-start | bytes 884744 | tf_op jit(solution)/shard_map/ppermute | solution.py:362
  80.7 6.9 %copy-start.36 = (bf16[2,288,256]{2,1,0:T(8,128)(2,1)}, bf16[2,288,256]{2,1,0:T(8,128)(2,1)S(1)}, u32[]{:S(2)}) copy-start(bf16[2,288,256]{2,1,0:T(8,128)(2,1)S(1)} %collective-permute-done.14.refs_5_) | copy-start | bytes 884740
  80.7 11.4 %collective-permute-start.16 = (bf16[2,288,256]{2,1,0:T(8,128)(2,1)S(1)}, bf16[2,288,256]{2,1,0:T(8,128)(2,1)S(1)}, u32[]{:S(2)}, u32[]{:S(2)}) collective-permute-start(bf16[2,288,256]{2,1,0:T(8,128)(2,1)S(1)} %collective-permute-done.12.refs_3_), channel_id=1, source_target_pairs={{0,1},{1,0},{2,3},{3,2},{4,5},{5,4},{6,7},{7,6},{8,9},{9,8},{10,11... | collective-permute-start | bytes 884744 | tf_op jit(solution)/shard_map/ppermute | solution.py:362
  87.6 18.9 %copy-start.37 = (bf16[2,288,256]{2,1,0:T(8,128)(2,1)}, bf16[2,288,256]{2,1,0:T(8,128)(2,1)S(1)}, u32[]{:S(2)}) copy-start(bf16[2,288,256]{2,1,0:T(8,128)(2,1)S(1)} %collective-permute-done.15.refs_6_) | copy-start | bytes 884740
  87.7 40.3 %collective-permute-start.25 = (bf16[1024,1408]{1,0:T(8,128)(2,1)S(1)}, bf16[1024,1408]{1,0:T(8,128)(2,1)}, u32[]{:S(2)}, u32[]{:S(2)}) collective-permute-start(bf16[1024,1408]{1,0:T(8,128)(2,1)S(1)} %copy-done.18), channel_id=1, source_target_pairs={{0,1},{1,0},{2,3},{3,2},{4,5},{5,4},{6,7},{7,6},{8,9},{9,8},{10,11... | collective-permute-start | bytes 8650760 | tf_op jit(solution)/shard_map/ppermute | solution.py:362
  92.1 14.4 %copy-start.38 = (bf16[2,288,256]{2,1,0:T(8,128)(2,1)}, bf16[2,288,256]{2,1,0:T(8,128)(2,1)S(1)}, u32[]{:S(2)}) copy-start(bf16[2,288,256]{2,1,0:T(8,128)(2,1)S(1)} %collective-permute-done.16.refs_7_) | copy-start | bytes 884740
  92.1 20.9 %collective-permute-start.6 = (bf16[4,288,256]{2,1,0:T(8,128)(2,1)S(1)}, bf16[4,288,256]{2,1,0:T(8,128)(2,1)}, u32[]{:S(2)}, u32[]{:S(2)}) collective-permute-start(bf16[4,288,256]{2,1,0:T(8,128)(2,1)S(1)} %slice.114.refs_0_), channel_id=1, source_target_pairs={{0,1},{1,0},{2,3},{3,2},{4,5},{5,4},{6,7},{7,6},{8,9},{9,8},{10,11... | collective-permute-start | bytes 1769480 | tf_op jit(solution)/shard_map/ppermute | solution.py:362
  94.1 18.9 %copy-start.20 = (bf16[4,288,256]{2,1,0:T(8,128)(2,1)}, bf16[4,288,256]{2,1,0:T(8,128)(2,1)S(1)}, u32[]{:S(2)}) copy-start(bf16[4,288,256]{2,1,0:T(8,128)(2,1)S(1)} %collective-permute-done.3.refs_1_) | copy-start | bytes 1769476
  94.1 23.4 %collective-permute-start.7 = (bf16[4,288,256]{2,1,0:T(8,128)(2,1)S(1)}, bf16[4,288,256]{2,1,0:T(8,128)(2,1)}, u32[]{:S(2)}, u32[]{:S(2)}) collective-permute-start(bf16[4,288,256]{2,1,0:T(8,128)(2,1)S(1)} %collective-permute-done.3.refs_1_), channel_id=1, source_target_pairs={{0,1},{1,0},{2,3},{3,2},{4,5},{5,4},{6,7},{7,6},{8,9},{9,8},{10,11... | collective-permute-start | bytes 1769480 | tf_op jit(solution)/shard_map/ppermute | solution.py:362
  106.0 7.0 %copy-start.21 = (bf16[4,288,256]{2,1,0:T(8,128)(2,1)}, bf16[4,288,256]{2,1,0:T(8,128)(2,1)S(1)}, u32[]{:S(2)}) copy-start(bf16[4,288,256]{2,1,0:T(8,128)(2,1)S(1)} %collective-permute-done.4.refs_2_) | copy-start | bytes 1769476
  106.0 11.5 %collective-permute-start.8 = (bf16[4,288,256]{2,1,0:T(8,128)(2,1)S(1)}, bf16[4,288,256]{2,1,0:T(8,128)(2,1)}, u32[]{:S(2)}, u32[]{:S(2)}) collective-permute-start(bf16[4,288,256]{2,1,0:T(8,128)(2,1)S(1)} %collective-permute-done.4.refs_2_), channel_id=1, source_target_pairs={{0,1},{1,0},{2,3},{3,2},{4,5},{5,4},{6,7},{7,6},{8,9},{9,8},{10,11... | collective-permute-start | bytes 1769480 | tf_op jit(solution)/shard_map/ppermute | solution.py:362
  106.0 11.5 %collective-permute-start.9 = (bf16[4,288,256]{2,1,0:T(8,128)(2,1)}, bf16[4,288,256]{2,1,0:T(8,128)(2,1)}, u32[]{:S(2)}, u32[]{:S(2)}) collective-permute-start(bf16[4,288,256]{2,1,0:T(8,128)(2,1)} %collective-permute-done.5.refs_3_), channel_id=1, source_target_pairs={{0,1},{1,0},{2,3},{3,2},{4,5},{5,4},{6,7},{7,6},{8,9},{9,8},{10,11... | collective-permute-start | bytes 1769480 | tf_op jit(solution)/shard_map/ppermute | solution.py:362
  113.1 14.9 %collective-permute-start.26 = (bf16[1024,1408]{1,0:T(8,128)(2,1)S(1)}, bf16[1024,1408]{1,0:T(8,128)(2,1)}, u32[]{:S(2)}, u32[]{:S(2)}) collective-permute-start(bf16[1024,1408]{1,0:T(8,128)(2,1)S(1)} %copy-done.19), channel_id=1, source_target_pairs={{0,1},{1,0},{2,3},{3,2},{4,5},{5,4},{6,7},{7,6},{8,9},{9,8},{10,11... | collective-permute-start | bytes 8650760 | tf_op jit(solution)/shard_map/ppermute | solution.py:362
  234.6 59.8 %collective-permute-start.27 = (bf16[1024,1408]{1,0:T(8,128)(2,1)}, bf16[1024,1408]{1,0:T(8,128)(2,1)S(1)}, u32[]{:S(2)}, u32[]{:S(2)}) collective-permute-start(bf16[1024,1408]{1,0:T(8,128)(2,1)} %get-tuple-element.81), channel_id=1, source_target_pairs={{0,1},{1,0},{2,3},{3,2},{4,5},{5,4},{6,7},{7,6},{8,9},{9,8},{10,11... | collective-permute-start | bytes 8650760 | tf_op jit(solution)/shard_map/ppermute | solution.py:362
  261.3 33.8 %collective-permute-start.28 = (bf16[1024,1408]{1,0:T(8,128)(2,1)}, bf16[1024,1408]{1,0:T(8,128)(2,1)S(1)}, u32[]{:S(2)}, u32[]{:S(2)}) collective-permute-start(bf16[1024,1408]{1,0:T(8,128)(2,1)} %get-tuple-element.84), channel_id=1, source_target_pairs={{0,1},{1,0},{2,3},{3,2},{4,5},{5,4},{6,7},{7,6},{8,9},{9,8},{10,11... | collective-permute-start | bytes 8650760 | tf_op jit(solution)/shard_map/ppermute | solution.py:362
  279.5 17.5 %collective-permute-start.29 = (bf16[1024,1408]{1,0:T(8,128)(2,1)}, bf16[1024,1408]{1,0:T(8,128)(2,1)}, u32[]{:S(2)}, u32[]{:S(2)}) collective-permute-start(bf16[1024,1408]{1,0:T(8,128)(2,1)} %get-tuple-element.88), channel_id=1, source_target_pairs={{0,1},{1,0},{2,3},{3,2},{4,5},{5,4},{6,7},{7,6},{8,9},{9,8},{10,11... | collective-permute-start | bytes 8650760 | tf_op jit(solution)/shard_map/ppermute | solution.py:362
  290.3 2.7 collective-permute-start.30
  331.9 14.5 %collective-permute-start.31 = (bf16[4,4,288,256]{3,2,1,0:T(8,128)(2,1)}, bf16[4,4,288,256]{3,2,1,0:T(8,128)(2,1)S(1)}, u32[]{:S(2)}, u32[]{:S(2)}) collective-permute-start(bf16[4,4,288,256]{3,2,1,0:T(8,128)(2,1)} %get-tuple-element.95), channel_id=1, source_target_pairs={{0,1},{1,0},{2,3},{3,2},{4,5},{5,4},{6,7},{7,6},{8,9},{9,8},{10,11... | collective-permute-start | bytes 7077896 | tf_op jit(solution)/shard_map/ppermute | solution.py:362
  349.6 78.1 %collective-permute-start.32 = (bf16[4,288,256]{2,1,0:T(8,128)(2,1)S(1)}, bf16[4,288,256]{2,1,0:T(8,128)(2,1)S(1)}, u32[]{:S(2)}, u32[]{:S(2)}) collective-permute-start(bf16[4,288,256]{2,1,0:T(8,128)(2,1)S(1)} %get-tuple-element.115), channel_id=1, source_target_pairs={{0,2},{2,4},{4,6},{6,0},{1,3},{3,5},{5,7},{7,1},{8,10},{10,12},{12... | collective-permute-start | bytes 1769480 | tf_op jit(solution)/shard_map/ppermute | solution.py:367
  371.9 65.2 %collective-permute-start.33 = (bf16[4,288,256]{2,1,0:T(8,128)(2,1)S(1)}, bf16[4,288,256]{2,1,0:T(8,128)(2,1)S(1)}, u32[]{:S(2)}, u32[]{:S(2)}) collective-permute-start(bf16[4,288,256]{2,1,0:T(8,128)(2,1)S(1)} %get-tuple-element.114), channel_id=1, source_target_pairs={{0,4},{2,6},{4,0},{6,2},{1,5},{3,7},{5,1},{7,3},{8,12},{10,14},{12... | collective-permute-start | bytes 1769480 | tf_op jit(solution)/shard_map/ppermute | solution.py:367
  410.0 27.0 %collective-permute-start.34 = (bf16[4,288,256]{2,1,0:T(8,128)(2,1)S(1)}, bf16[4,288,256]{2,1,0:T(8,128)(2,1)S(1)}, u32[]{:S(2)}, u32[]{:S(2)}) collective-permute-start(bf16[4,288,256]{2,1,0:T(8,128)(2,1)S(1)} %get-tuple-element.113), channel_id=1, source_target_pairs={{0,6},{2,0},{4,2},{6,4},{1,7},{3,1},{5,3},{7,5},{8,14},{10,8},{12,... | collective-permute-start | bytes 1769480 | tf_op jit(solution)/shard_map/ppermute | solution.py:367
  423.1 41.2 %collective-permute-start.35 = (bf16[4,2,288,256]{3,2,1,0:T(8,128)(2,1)}, bf16[4,2,288,256]{3,2,1,0:T(8,128)(2,1)S(1)}, u32[]{:S(2)}, u32[]{:S(2)}) collective-permute-start(bf16[4,2,288,256]{3,2,1,0:T(8,128)(2,1)} %get-tuple-element.104), channel_id=1, source_target_pairs={{0,1},{1,0},{2,3},{3,2},{4,5},{5,4},{6,7},{7,6},{8,9},{9,8},{10,11... | collective-permute-start | bytes 3538952 | tf_op jit(solution)/shard_map/ppermute | solution.py:362
  427.7 22.8 %copy-start.22 = (bf16[4,288,256]{2,1,0:T(8,128)(2,1)}, bf16[4,288,256]{2,1,0:T(8,128)(2,1)S(1)}, u32[]{:S(2)}) copy-start(bf16[4,288,256]{2,1,0:T(8,128)(2,1)S(1)} %collective-permute-done.32.refs_13_) | copy-start | bytes 1769476
  437.0 13.5 %copy-start.23 = (bf16[4,288,256]{2,1,0:T(8,128)(2,1)}, bf16[4,288,256]{2,1,0:T(8,128)(2,1)S(1)}, u32[]{:S(2)}) copy-start(bf16[4,288,256]{2,1,0:T(8,128)(2,1)S(1)} %collective-permute-done.33.refs_14_) | copy-start | bytes 1769476
  437.0 13.5 %copy-start.24 = (bf16[4,288,256]{2,1,0:T(8,128)(2,1)}, bf16[4,288,256]{2,1,0:T(8,128)(2,1)S(1)}, u32[]{:S(2)}) copy-start(bf16[4,288,256]{2,1,0:T(8,128)(2,1)S(1)} %collective-permute-done.34.refs_15_) | copy-start | bytes 1769476
  450.5 15.3 %collective-permute-start.36 = (bf16[4,2,288,256]{3,2,1,0:T(8,128)(2,1)}, bf16[4,2,288,256]{3,2,1,0:T(8,128)(2,1)S(1)}, u32[]{:S(2)}, u32[]{:S(2)}) collective-permute-start(bf16[4,2,288,256]{3,2,1,0:T(8,128)(2,1)} %get-tuple-element.106), channel_id=1, source_target_pairs={{0,1},{1,0},{2,3},{3,2},{4,5},{5,4},{6,7},{7,6},{8,9},{9,8},{10,11... | collective-permute-start | bytes 3538952 | tf_op jit(solution)/shard_map/ppermute | solution.py:362
  455.5 8.8 %copy-start.3 = (bf16[4,2,288,256]{3,2,1,0:T(8,128)(2,1)S(1)}, bf16[4,2,288,256]{3,2,1,0:T(8,128)(2,1)}, u32[]{:S(2)}) copy-start(bf16[4,2,288,256]{3,2,1,0:T(8,128)(2,1)} %get-tuple-element.103) | copy-start | bytes 3538948
  568.3 8.5 %copy-start.9 = (f32[64,512]{1,0:T(8,128)S(1)}, f32[64,512]{1,0:T(8,128)}, u32[]{:S(2)}) copy-start(f32[64,512]{1,0:T(8,128)} %get-tuple-element.159) | copy-start | bytes 393220
  (13 other events, 39.8 us)
Sparse Core Ops, SparseCore 0:
  306.3 156.9 reduce-scatter.1

commit v3 on v2

--- a/solution.py
+++ b/solution.py
@@ -367,9 +367,31 @@
     return lax.ppermute(value, axis, [(i, (i + by) % size) for i in range(size)])
 
 
-def gather_keys(kv):
-    near = [kv] + [shift(kv, "seq", k) for k in range(1, lax.axis_size("seq"))]
-    return near + [swap_cores(value) for value in near]
+def send_near(kv):
+    return [kv] + [shift(kv, "seq", k) for k in range(1, lax.axis_size("seq"))]
+
+
+def send_far(near):
+    return [part[None] for part in near + [swap_cores(value) for value in near]]
+
+
+def pick(value, index, axis):
+    return lax.dynamic_index_in_dim(value, index, axis, keepdims=False)
+
+
+def send_steps(value, axis, dim):
+    size, me = lax.axis_size(axis), lax.axis_index(axis)
+    terms = [pick(value, me, dim)]
+    for k in range(1, size):
+        terms.append(shift(pick(value, (me + k) % size, dim), axis, k))
+    return terms
+
+
+def add_up(terms):
+    total = terms[0].astype(F32)
+    for term in terms[1:]:
+        total = total + term.astype(F32)
+    return total
 
 
 def by_core(own, other, axis):
@@ -385,48 +407,68 @@
     return jnp.concatenate([a * cosine - b * sine_table, b * cosine + a * sine_table], axis=0)
 
 
-def keys_kernel(x_ref, gain_ref, w_ref, cos_ref, sin_ref, kv_ref, nt_ref):
+def project_kernel(
+    sent, x_ref, og_ref, gain_ref, wkv_ref, wq_ref, wdo_ref, wdp_ref, cos_ref, sin_ref,
+    kv_ref, nt_ref, q_ref, ga_ref, near_ref, far_ref, kept, wd, load_sems, own_sems, sends, receives,
+):
+    b = pl.program_id(0)
+    count_s = lax.axis_size("seq")
+    me_s, core = lax.axis_index("seq"), lax.axis_index("mp")
+    peers = [{"seq": lax.rem(me_s + k, count_s)} for k in range(1, count_s)]
+    other_core = {"mp": 1 - core}
+    near, forward = [], []
+    slots = iter(range(sends.shape[0]))
+
+    def link(source, target, peer):
+        slot = next(slots)
+        return pltpu.make_async_remote_copy(
+            src_ref=source,
+            dst_ref=target,
+            send_sem=sends.at[slot],
+            recv_sem=receives.at[slot],
+            device_id=peer,
+            device_id_type=pl.DeviceIdType.MESH,
+        )
+
+    for i in range(sent):
+        near.append([link(kept.at[i], near_ref.at[k, i], peers[k - 1]) for k in range(1, count_s)])
+        forward.append(
+            [link(kept.at[i], far_ref.at[0, i], other_core)]
+            + [link(near_ref.at[k, i], far_ref.at[k, i], other_core) for k in range(1, count_s)]
+        )
+    own = [pltpu.make_async_copy(kept.at[i], near_ref.at[0, i], own_sems.at[i]) for i in range(sent)]
+    loads = load_weights([(wdo_ref, 0, 0), (wdp_ref, 1, 0)], [wd, wd], load_sems)
+
+    @pl.when(b == 0)
+    def _():
+        for copy in loads:
+            copy.start()
+        barrier = pltpu.get_barrier_semaphore()
+        for peer in [other_core] + peers:
+            pl.semaphore_signal(barrier, inc=1, device_id=peer, device_id_type=pl.DeviceIdType.MESH)
+        pl.semaphore_wait(barrier, count_s)
+
     x = x_ref[0].astype(F32)
     inverse = lax.rsqrt(jnp.mean(x * x, axis=-1, keepdims=True) + epsilon)
     normed = (x * inverse * gain_ref[...]).astype(BF)
+    lin = mxu(wkv_ref[...], normed, NT)
+    tied = wkv_ref.shape[0] - RD
+    cosine, sine_table = cos_ref[...], sin_ref[...]
+    rope = rotate_rows(lin[tied:], cosine, sine_table)
+    keys = jnp.concatenate([lin[:tied], rope], axis=0).astype(BF)
+    kv_ref[0] = keys
+    for i in range(sent):
+
+        @pl.when(b == i)
+        def _():
+            kept[i] = keys
+            for copy in near[i]:
+                copy.start()
+            forward[i][0].start()
+            own[i].start()
+
     nt_ref[...] = normed.T
-    lin = mxu(w_ref[...], normed, NT)
-    tied = w_ref.shape[0] - RD
-    kv_ref[0, :tied] = lin[:tied].astype(BF)
-    kv_ref[0, tied:] = rotate_rows(lin[tied:], cos_ref[...], sin_ref[...]).astype(BF)
-
-
-def project_keys(x, gain, weights, cosine, sine_table):
-    count, own, width = x.shape
-    rows = weights.shape[0]
-    whole = lambda b: (0, 0)
-    return pl.pallas_call(
-        keys_kernel,
-        grid=(count,),
-        in_specs=[
-            pl.BlockSpec((1, own, width), lambda b: (b, 0, 0)),
-            pl.BlockSpec((1, width), whole),
-            pl.BlockSpec((rows, width), whole),
-            pl.BlockSpec(cosine.shape, whole),
-            pl.BlockSpec(cosine.shape, whole),
-        ],
-        out_specs=[
-            pl.BlockSpec((1, rows, own), lambda b: (b, 0, 0)),
-            pl.BlockSpec((width, own), lambda b: (0, b)),
-        ],
-        out_shape=[
-            jax.ShapeDtypeStruct((count, rows, own), BF),
-            jax.ShapeDtypeStruct((width, count * own), BF),
-        ],
-        compiler_params=params(),
-        cost_estimate=cost(2 * x.size * rows, 4 * x.size),
-        name="project_keys",
-    )(x, gain, weights, cosine, sine_table)
-
-
-def queries_kernel(nt_ref, w_ref, cos_ref, sin_ref, q_ref):
-    lin = mxu(w_ref[...], nt_ref[...], NN)
-    cosine, sine_table = cos_ref[...], sin_ref[...]
+    lin = mxu(wq_ref[...], normed, NT)
     plain = HD - RD
     pieces = []
     for at in range(0, lin.shape[0], HD):
@@ -435,26 +477,79 @@
     queries = jnp.concatenate(pieces, axis=0)
     q_ref[...] = (queries.astype(BF) * HD ** (-0.5)).astype(BF)
 
-
-def project_queries(normed_t, weights, cosine, sine_table):
-    width, tokens = normed_t.shape
-    rows, own = weights.shape[0], cosine.shape[1]
-    whole = lambda b: (0, 0)
+    @pl.when(b == 0)
+    def _():
+        for copy in loads:
+            copy.wait()
+
+    og = og_ref[0]
+    for at in range(0, wd.shape[0], 2 * LANE):
+        to = slice(at, at + 2 * LANE)
+        ga_ref[:, to] = mxu(og, wd[to], NT).astype(BF)
+
+    steps = pl.num_programs(0)
+    for i in range(sent):
+
+        @pl.when(b == steps - 1 - (3 * (sent - 1 - i) + 1) // 2)
+        def _():
+            for copy in near[i]:
+                copy.wait()
+            for copy in forward[i][1:]:
+                copy.start()
+
+    @pl.when(b == steps - 1)
+    def _():
+        for i in range(sent):
+            own[i].wait()
+            for copy in forward[i]:
+                copy.wait()
+
+
+def project(x, og, gain, wkv, wq, wd, cosine, sine_table, sent):
+    count, own, width = x.shape
+    kv_rows, rows, half = wkv.shape[0], wq.shape[0], wd[0].shape[0]
+    count_s = lax.axis_size("seq")
+    whole = lambda array: pl.BlockSpec(array.shape, lambda b: (0, 0))
+    seq = pl.BlockSpec((1, own, width), lambda b: (b, 0, 0))
+    hbm = pl.BlockSpec(memory_space=pl.ANY)
+    gathered = jax.ShapeDtypeStruct((count_s, sent, kv_rows, own), BF)
+    links = sent * (2 * count_s - 1)
     return pl.pallas_call(
-        queries_kernel,
-        grid=(tokens // own,),
+        functools.partial(project_kernel, sent),
+        grid=(count,),
         in_specs=[
+            seq, seq, whole(gain), whole(wkv), whole(wq), hbm, hbm, whole(cosine), whole(cosine),
+        ],
+        out_specs=[
+            pl.BlockSpec((1, kv_rows, own), lambda b: (b, 0, 0)),
             pl.BlockSpec((width, own), lambda b: (0, b)),
-            pl.BlockSpec((rows, width), whole),
-            pl.BlockSpec(cosine.shape, whole),
-            pl.BlockSpec(cosine.shape, whole),
-        ],
-        out_specs=pl.BlockSpec((rows, own), lambda b: (0, b)),
-        out_shape=jax.ShapeDtypeStruct((rows, tokens), BF),
-        compiler_params=params(),
-        cost_estimate=cost(2 * normed_t.size * rows, 4 * normed_t.size),
-        name="project_queries",
-    )(normed_t, weights, cosine, sine_table)
+            pl.BlockSpec((rows, own), lambda b: (0, b)),
+            pl.BlockSpec((own, 2 * half), lambda b: (b, 0)),
+            hbm,
+            hbm,
+        ],
+        out_shape=[
+            jax.ShapeDtypeStruct((count, kv_rows, own), BF),
+            jax.ShapeDtypeStruct((width, count * own), BF),
+            jax.ShapeDtypeStruct((rows, count * own), BF),
+            jax.ShapeDtypeStruct((count * own, 2 * half), BF),
+            gathered,
+            gathered,
+        ],
+        scratch_shapes=[
+            pltpu.VMEM((sent, kv_rows, own), BF),
+            pltpu.VMEM((2 * half, width), BF),
+            pltpu.SemaphoreType.DMA((2 * (half // LANE),)),
+            pltpu.SemaphoreType.DMA((sent,)),
+            pltpu.SemaphoreType.DMA((links,)),
+            pltpu.SemaphoreType.DMA((links,)),
+        ],
+        compiler_params=pltpu.CompilerParams(
+            vmem_limit_bytes=56 * MIB, collective_id=2, has_side_effects=True
+        ),
+        cost_estimate=cost(3 * 10**10),
+        name="project",
+    )(x, og, gain, wkv, wq, *wd, cosine, sine_table)
 
 
 def segment_counts(starts, first, width):
@@ -505,23 +600,38 @@
 
 
 def place_keys(refs, kv, begin, me):
-    steps = len(refs) // 2
+    steps = lax.axis_size("seq")
     seq, core = lax.axis_index("seq"), lax.axis_index("mp")
-    for at, ref in enumerate(refs):
+    places = [(ref, i) for ref in refs for i in range(ref.shape[0])]
+    for at, (ref, i) in enumerate(places):
         of = core if at < steps else 1 - core
         j = lax.rem(seq - at % steps + steps, steps) * 2 + of
 
         @pl.when((j >= begin) & (j <= me))
         def _():
-            kv[j] = ref[0]
-
-
-def stack_heads(value, at, heads):
-    return jnp.concatenate([value[at + h * HD : at + (h + 1) * HD] for h in range(heads)], axis=1)
-
-
-def attend_kernel(groups, heads, first, chunks, docs_ref, q_ref, *refs):
-    kv_refs = refs[:chunks]
+            kv[j] = ref[i, 0]
+
+
+def stack_heads(value, at, heads, rows=HD):
+    half = value.shape[1] // 2
+    return jnp.concatenate(
+        [
+            value[at + h * rows : at + (h + 1) * rows, s * half : (s + 1) * half]
+            for s in range(2)
+            for h in range(heads)
+        ],
+        axis=1,
+    )
+
+
+def stack_queries(starts, first, half, heads):
+    return jnp.concatenate(
+        [query_rows(starts, first + s * half, half) for s in range(2) for _ in range(heads)], axis=1
+    )
+
+
+def attend_kernel(groups, heads, first, inputs, docs_ref, q_ref, *refs):
+    kv_refs = refs[:inputs]
     out_ref, lse_ref, kv_ref, qa, acc, top = refs[-6:]
     b = pl.program_id(0) + first
     own = q_ref.shape[1]
@@ -529,12 +639,14 @@
     starts = [docs_ref[b, k] for k in range(ndoc)]
     me = my_chunk()
     begin = start_chunk(starts, me * own, own)
+    half = own // 2
+    begin_second = start_chunk(starts, me * own + half, own)
     place_keys(kv_refs, kv_ref, begin, me)
     wide = heads * own
+    first_half = wide // 2
     tied = groups * HD
     plain = HD - RD
-    q_doc = query_rows(starts, me * own, own)
-    q_doc = jnp.concatenate([q_doc] * heads, axis=1)
+    q_doc = stack_queries(starts, me * own, half, heads)
     q_all = q_ref[...]
     for g in range(groups):
         qa[g, :HD] = stack_heads(q_all, g * heads * HD, heads)
@@ -543,7 +655,7 @@
     ones = first_rows(1, own)
     zeros = jnp.zeros((LANE - HD - 16, own), BF)
 
-    def scores(j, g):
+    def keys_of(j, g):
         doc = key_rows(starts, j * own, own)
         block = jnp.concatenate(
             [
@@ -554,54 +666,81 @@
             ],
             axis=0,
         )
-        return mxu(block.T, qa[g], NN)
-
-    def weighted(j, g, weights):
-        values = jnp.concatenate([kv_ref[j, g * HD : (g + 1) * HD], ones], axis=0)
-        return mxu(values, weights.astype(BF), NN)
-
-    key_at = lax.broadcasted_iota(jnp.int32, (own, own), 0)
-    query_at = lax.broadcasted_iota(jnp.int32, (own, own), 1)
-    causal = jnp.concatenate([key_at <= query_at] * heads, axis=1)
-    for g in range(groups):
-        logits = jnp.where(causal, scores(me, g), masked_value)
-        peak = jnp.max(logits, axis=0, keepdims=True)
-        acc[g] = weighted(me, g, jnp.exp(logits - peak))
-        top[g] = peak
-
-    def step(i, carry):
-        j = me - 1 - i
+        return block.T
+
+    def values_of(j, g):
+        return jnp.concatenate([kv_ref[j, g * HD : (g + 1) * HD], ones], axis=0)
+
+    key_at = lax.broadcasted_iota(jnp.int32, (own, half), 0)
+    query_at = lax.broadcasted_iota(jnp.int32, (own, half), 1)
+    causal = jnp.concatenate(
+        [key_at <= query_at + s * half for s in range(2) for _ in range(heads)], axis=1
+    )
+
+    def block(j, lanes, diagonal=False):
+        def logits_of(g):
+            return mxu(keys_of(j, g), qa[g, :, lanes], NN)
+
+        following = logits_of(0)
         for g in range(groups):
-            logits = scores(j, g)
-            peak = jnp.maximum(top[g], jnp.max(logits, axis=0, keepdims=True))
-            shrink = jnp.exp(top[g] - peak)
-            acc[g] = acc[g] * shrink + weighted(j, g, jnp.exp(logits - peak))
-            top[g] = peak
+            logits = following
+            if g + 1 < groups:
+                following = logits_of(g + 1)
+            if diagonal:
+                logits = jnp.where(causal, logits, masked_value)
+            peak = jnp.max(logits, axis=0, keepdims=True)
+            if not diagonal:
+                old = top[g, :, lanes]
+                peak = jnp.maximum(old, peak)
+            weights = jnp.exp(logits - peak).astype(BF)
+            added = mxu(values_of(j, g), weights, NN)
+            if not diagonal:
+                added = acc[g, :, lanes] * jnp.exp(old - peak) + added
+            acc[g, :, lanes] = added
+            top[g, :, lanes] = peak
+
+    block(me, slice(0, wide), True)
+
+    def both(i, carry):
+        block(me - 1 - i, slice(0, wide))
         return carry
 
-    lax.fori_loop(0, me - begin, step, 0)
+    def first_only(i, carry):
+        block(begin_second - 1 - i, slice(0, first_half))
+        return carry
+
+    lax.fori_loop(0, me - begin_second, both, 0)
+    lax.fori_loop(0, begin_second - begin, first_only, 0)
     for g in range(groups):
         total = acc[g, HD : HD + 1]
         result = acc[g, :HD] / total
         lse_ref[0, g : g + 1] = top[g] + jnp.log(total)
-        for h in range(heads):
-            at = (g * heads + h) * HD
-            out_ref[at : at + HD] = result[:, h * own : (h + 1) * own].astype(BF)
-
-
-def attend_forward(docs, q, kv, groups, heads, first, into):
-    size, kv_rows, own = kv[0].shape
-    count, chunks = docs.shape[0], len(kv)
+        for s in range(2):
+            for h in range(heads):
+                at, of = (g * heads + h) * HD, (s * heads + h) * half
+                out_ref[at : at + HD, s * half : (s + 1) * half] = result[:, of : of + half].astype(BF)
+
+
+def kv_specs(kv, kv_at):
+    return [
+        pl.BlockSpec((part.shape[0], 1, *part.shape[2:]), lambda b: (0, b + kv_at, 0, 0))
+        for part in kv
+    ]
+
+
+def attend_forward(docs, q, kv, groups, heads, first, size, kv_at, into):
+    kv_rows, own = kv[0].shape[2:]
+    count, chunks, inputs = docs.shape[0], 2 * lax.axis_size("seq"), len(kv)
     wide = heads * own
     hbm = pl.BlockSpec(memory_space=pl.ANY)
     return pl.pallas_call(
-        functools.partial(attend_kernel, groups, heads, first, chunks),
+        functools.partial(attend_kernel, groups, heads, first, inputs),
         grid=(size,),
         in_specs=[
             pl.BlockSpec(memory_space=pltpu.SMEM),
             pl.BlockSpec((q.shape[0], own), lambda b: (0, b + first)),
         ]
-        + [pl.BlockSpec((1, kv_rows, own), lambda b: (b, 0, 0))] * chunks
+        + kv_specs(kv, kv_at)
         + [hbm] * len(into),
         out_specs=[
             pl.BlockSpec((q.shape[0], own), lambda b: (0, b + first)),
@@ -617,7 +756,7 @@
             pltpu.VMEM((groups, HD + 16, wide), F32),
             pltpu.VMEM((groups, 1, wide), F32),
         ],
-        input_output_aliases={2 + chunks + i: i for i in range(len(into))},
+        input_output_aliases={2 + inputs + i: i for i in range(len(into))},
         compiler_params=params(),
         cost_estimate=cost(10**10 * size),
         name="attend",
@@ -625,9 +764,10 @@
 
 
 def attend_back_kernel(
-    groups, heads, first, chunks, docs_ref, q_ref, do_ref, lse_ref, delta_ref, rot_ref, *refs
+    groups, heads, first, inputs, docs_ref, q_ref, do_ref, lse_ref, delta_ref, rot_ref, *refs
 ):
-    kv_refs = refs[:chunks]
+    kv_refs = refs[:inputs]
+    chunks = 2 * lax.axis_size("seq")
     dq_ref, keep_ref, give_ref, kv_ref, stage, qs, qa, ds_, da, dq = refs[-10:]
     b = pl.program_id(0) + first
     own = q_ref.shape[1]
@@ -635,12 +775,13 @@
     starts = [docs_ref[b, k] for k in range(ndoc)]
     me = my_chunk()
     begin = start_chunk(starts, me * own, own)
+    half = own // 2
+    begin_second = start_chunk(starts, me * own + half, own)
     place_keys(kv_refs, kv_ref, begin, me)
     wide = heads * own
     tied = groups * HD
     plain = HD - RD
-    q_doc = query_rows(starts, me * own, own)
-    q_doc = jnp.concatenate([q_doc] * heads, axis=1)
+    q_doc = stack_queries(starts, me * own, half, heads)
     q_all, do_all = q_ref[...], do_ref[...]
     pad_q = jnp.zeros((LANE - HD - 32, wide), BF)
     pad_d = jnp.zeros((LANE - HD - 16, wide), BF)
@@ -661,9 +802,7 @@
         qs[g] = q_rows
         ds_[g] = do_rows
         lse_rows = three_parts(-lse_ref[0, g : g + 1], wide)
-        delta_row = jnp.concatenate(
-            [delta_ref[0, g * heads + h : g * heads + h + 1] for h in range(heads)], axis=1
-        )
+        delta_row = stack_heads(delta_ref[0], g * heads, heads, 1)
         delta_rows = three_parts(-delta_row, wide)
         turn(jnp.concatenate([q_rows, q_doc, lse_rows, pad_q], axis=0), qa.at[g])
         turn(jnp.concatenate([do_rows, delta_rows, pad_d], axis=0), da.at[g])
@@ -692,29 +831,46 @@
     lax.fori_loop(0, begin, clear, 0)
     lax.fori_loop(me + 1, chunks, clear, 0)
 
-    def block(j, diagonal):
+    def block(j, rows, diagonal):
         doc = key_rows(starts, j * own, own)
         rope_rows = kv_ref[j, tied : tied + RD]
         rope_sum = jnp.zeros((RD, own), F32)
+
+        def keys_of(g):
+            return jnp.concatenate(
+                [kv_ref[j, g * HD : g * HD + plain], rope_rows], axis=0
+            )
+
+        def products(g):
+            values = kv_ref[j, g * HD : (g + 1) * HD]
+            return (
+                mxu(qa[g, :rows], jnp.concatenate([keys_of(g), doc, ones, pad_k], axis=0), NN),
+                mxu(da[g, :rows], jnp.concatenate([values, ones, pad_v], axis=0), NN),
+            )
+
+        following = products(0)
         for g in range(groups):
-            values = kv_ref[j, g * HD : (g + 1) * HD]
-            keys = jnp.concatenate([values[:plain], rope_rows], axis=0)
-            logits = mxu(qa[g], jnp.concatenate([keys, doc, ones, pad_k], axis=0), NN)
+            logits, slopes = following
+            if g + 1 < groups:
+                following = products(g + 1)
+            keys = keys_of(g)
             weights = jnp.exp(logits)
             if diagonal:
-                query_at = lax.broadcasted_iota(jnp.int32, (own, own), 0)
-                key_at = lax.broadcasted_iota(jnp.int32, (own, own), 1)
-                causal = jnp.concatenate([key_at <= query_at] * heads, axis=0)
+                query_at = lax.broadcasted_iota(jnp.int32, (half, own), 0)
+                key_at = lax.broadcasted_iota(jnp.int32, (half, own), 1)
+                causal = jnp.concatenate(
+                    [key_at <= query_at + s * half for s in range(2) for _ in range(heads)], axis=0
+                )
                 weights = jnp.where(causal, weights, 0.0)
-            slopes = mxu(da[g], jnp.concatenate([values, ones, pad_v], axis=0), NN)
             grads = (weights * slopes).astype(BF)
-            grad_values = mxu(ds_[g], weights.astype(BF), NN)
-            grad_keys = mxu(qs[g], grads, NN)
-            grad_queries = mxu(grads, keys.T, NN)
+            grad_values = mxu(ds_[g, :, :rows], weights.astype(BF), NN)
+            grad_keys = mxu(qs[g, :, :rows], grads, NN)
+            keys_t = keys.T
+            grad_queries = mxu(grads, jnp.concatenate([keys_t, keys_t], axis=1), NN)
             if diagonal:
                 dq[g] = grad_queries
             else:
-                dq[g] += grad_queries
+                dq[g, :rows] += grad_queries
             stage[g * HD : g * HD + plain] = (
                 grad_values[:plain] + grad_keys[:plain]
             ).astype(BF)
@@ -723,38 +879,45 @@
         stage[tied : tied + RD] = rope_sum.astype(BF)
         deliver(j, lambda: stage[...])
 
-    block(me, True)
-
-    def step(j, carry):
-        block(j, False)
+    block(me, wide, True)
+
+    def both(j, carry):
+        block(j, wide, False)
         return carry
 
-    lax.fori_loop(begin, me, step, 0)
+    def first_only(j, carry):
+        block(j, wide // 2, False)
+        return carry
+
+    lax.fori_loop(begin_second, me, both, 0)
+    lax.fori_loop(begin, begin_second, first_only, 0)
     straight, ahead, behind = rot_ref[0], rot_ref[1], rot_ref[2]
-    half = RD // 2
+    lane = lax.broadcasted_iota(jnp.int32, (half, LANE), 1)
+    quarter = RD // 2
     for g in range(groups):
-        for pair in range(heads // 2):
-            at = 2 * pair * own
-            both = jnp.concatenate([dq[g, at : at + own], dq[g, at + own : at + 2 * own]], axis=1)
-            both = both * HD ** (-0.5)
-            turned = (
-                both * straight
-                + pltpu.roll(both, LANE - half, 1) * ahead
-                + pltpu.roll(both, half, 1) * behind
-            )
-            to = (g * heads + 2 * pair) * HD
-            dq_ref[:, to : to + 2 * HD] = turned.astype(BF)
-
-
-def attend_backward(docs, q, do, lse, delta, turns, kv, groups, heads, first, into):
-    size, kv_rows, own = kv[0].shape
-    count, chunks = docs.shape[0], len(kv)
+        for s in range(2):
+            positions = slice(s * half, (s + 1) * half)
+            for pair in range(heads // 2):
+                at = (s * heads + 2 * pair) * half
+                two = jnp.where(lane < HD, dq[g, at : at + half], dq[g, at + half : at + 2 * half])
+                turned = (
+                    two * straight[positions]
+                    + pltpu.roll(two, LANE - quarter, 1) * ahead[positions]
+                    + pltpu.roll(two, quarter, 1) * behind[positions]
+                )
+                to = (g * heads + 2 * pair) * HD
+                dq_ref[positions, to : to + 2 * HD] = turned.astype(BF)
+
+
+def attend_backward(docs, q, do, lse, delta, turns, kv, groups, heads, first, size, kv_at, into):
+    kv_rows, own = kv[0].shape[2:]
+    count, chunks, inputs = docs.shape[0], 2 * lax.axis_size("seq"), len(kv)
     wide = heads * own
     width = q.shape[0]
     column = pl.BlockSpec((width, own), lambda b: (0, b + first))
     hbm = pl.BlockSpec(memory_space=pl.ANY)
     return pl.pallas_call(
-        functools.partial(attend_back_kernel, groups, heads, first, chunks),
+        functools.partial(attend_back_kernel, groups, heads, first, inputs),
         grid=(size,),
         in_specs=[
             pl.BlockSpec(memory_space=pltpu.SMEM),
@@ -764,7 +927,7 @@
             pl.BlockSpec((1, groups * heads, own), lambda b: (b + first, 0, 0)),
             pl.BlockSpec(turns.shape, lambda b: (0, 0, 0)),
         ]
-        + [pl.BlockSpec((1, kv_rows, own), lambda b: (b, 0, 0))] * chunks
+        + kv_specs(kv, kv_at)
         + [hbm] * len(into),
         out_specs=[
             pl.BlockSpec((own, width), lambda b: (b + first, 0)),
@@ -783,11 +946,11 @@
             pltpu.VMEM((groups, wide, LANE), BF),
             pltpu.VMEM((groups, HD, wide), BF),
             pltpu.VMEM((groups, wide, LANE), BF),
-            pltpu.VMEM((groups, wide, HD), F32),
-        ],
-        input_output_aliases={6 + chunks + i: i for i in range(len(into))},
+            pltpu.VMEM((groups, wide, LANE), F32),
+        ],
+        input_output_aliases={6 + inputs + i: i for i in range(len(into))},
         compiler_params=params(),
-        cost_estimate=cost(15 * 10**9 * size),
+        cost_estimate=cost(10**9 * size),
         name="attend_back",
     )(docs, q, do, lse, delta, turns, *kv, *into)
 
@@ -816,41 +979,6 @@
             copies.append(pltpu.make_async_copy(src, dst, sems.at[slot]))
             slot += 1
     return copies
-
-
-def slopes_kernel(og_ref, wdo_ref, wdp_ref, out_ref, wd, sems):
-    @pl.when(pl.program_id(0) == 0)
-    def _():
-        copies = load_weights([(wdo_ref, 0, 0), (wdp_ref, 1, 0)], [wd, wd], sems)
-        for copy in copies:
-            copy.start()
-        for copy in copies:
-            copy.wait()
-
-    og = og_ref[0]
-    for at in range(0, wd.shape[0], 2 * LANE):
-        to = slice(at, at + 2 * LANE)
-        out_ref[:, to] = mxu(og, wd[to], NT).astype(BF)
-
-
-def unit_slopes(og, wd):
-    count, own, width = og.shape
-    half = wd[0].shape[0]
-    hbm = pl.BlockSpec(memory_space=pl.ANY)
-    return pl.pallas_call(
-        slopes_kernel,
-        grid=(count,),
-        in_specs=[pl.BlockSpec((1, own, width), lambda b: (b, 0, 0)), hbm, hbm],
-        out_specs=pl.BlockSpec((own, 2 * half), lambda b: (b, 0)),
-        out_shape=jax.ShapeDtypeStruct((count * own, 2 * half), BF),
-        scratch_shapes=[
-            pltpu.VMEM((2 * half, width), BF),
-            pltpu.SemaphoreType.DMA((2 * (half // LANE),)),
-        ],
-        compiler_params=params(),
-        cost_estimate=cost(4 * og.size * half),
-        name="unit_slopes",
-    )(og, *wd)
 
 
 def feed_kernel(
@@ -974,76 +1102,186 @@
     )
 
 
-def unit_grads_kernel(split, left_ref, right_ref, own_ref, other_ref):
-    product = regroup_rows(mxu(left_ref[...], right_ref[...], NN), split).astype(BF)
-    own_ref[...] = product[:, :LANE]
-    other_ref[...] = product[:, LANE:]
-
-
-def unit_grads(left, right, split):
-    width, tokens = left.shape
-    units = right.shape[1]
+def early_kernel(
+    split, nt_ref, gg_ref, gu_ref, act_ref, act_next_ref, ogt_ref, gat_ref, o_ref, out_ref,
+    ogt, gat, heads_out, stage, landed, load_sems, sends, receives,
+):
+    t = pl.program_id(0)
+    core = lax.axis_index("mp")
+    tiles = landed.shape[0]
+    width = nt_ref.shape[0]
     tile = 2 * LANE
-    part = pl.BlockSpec((width, LANE), lambda t: (0, t))
+    pairs, head_tiles = gg_tiles(gg_ref, tiles, heads_out)
+    other_core = {"mp": 1 - core}
+    loads = [
+        pltpu.make_async_copy(source, target, load_sems.at[i])
+        for i, (source, target) in enumerate(((gat_ref, gat), (o_ref, heads_out), (ogt_ref, ogt)))
+    ]
+
+    @pl.when(t == 0)
+    def _():
+        for copy in loads:
+            copy.start()
+        barrier = pltpu.get_barrier_semaphore()
+        pl.semaphore_signal(barrier, inc=1, device_id=other_core, device_id_type=pl.DeviceIdType.MESH)
+        pl.semaphore_wait(barrier, 1)
+
+    @pl.when(t == pairs)
+    def _():
+        loads[0].wait()
+        loads[1].wait()
+
+    @pl.when(t == pairs + head_tiles)
+    def _():
+        loads[2].wait()
+
+    def send(i):
+        return pltpu.make_async_remote_copy(
+            src_ref=stage.at[lax.rem(i, 2)],
+            dst_ref=landed.at[i],
+            send_sem=sends.at[i],
+            recv_sem=receives.at[i],
+            device_id=other_core,
+            device_id_type=pl.DeviceIdType.MESH,
+        )
+
+    def deliver(product):
+        product = regroup_rows(product, split)
+
+        @pl.when(t < tiles)
+        def _():
+            @pl.when(t >= 2)
+            def _():
+                send(t - 2).wait_send()
+
+            stage[lax.rem(t, 2)] = product.astype(BF)
+            send(t).start()
+
+        @pl.when(t >= tiles)
+        def _():
+            @pl.when(t < tiles + 2)
+            def _():
+                send(t - 2).wait_send()
+
+            send(t - tiles).wait_recv()
+            out_ref[...] = (product + landed[t - tiles].astype(F32)).astype(BF)
+
+    at = lax.rem(t, tiles)
+
+    @pl.when(at < pairs)
+    def _():
+        deliver(mxu(nt_ref[...], jnp.concatenate([gg_ref[...], gu_ref[...]], axis=1), NN))
+
+    @pl.when((at >= pairs) & (at < pairs + head_tiles))
+    def _():
+        side = jnp.where(t < tiles, 1 - core, core)
+        row = pl.multiple_of((side * head_tiles + at - pairs) * tile, tile)
+        deliver(mxu(gat[...], heads_out[pl.ds(row, tile)], NT))
+
+    @pl.when(at >= pairs + head_tiles)
+    def _():
+        deliver(mxu(ogt[...], jnp.concatenate([act_ref[...], act_next_ref[...]], axis=1), NN))
+
+
+def gg_tiles(gg_ref, tiles, heads_out):
+    head_tiles = heads_out.shape[0] // (4 * LANE)
+    return (2 * (tiles - head_tiles)) // 3, head_tiles
+
+
+def early_grads(nt, gg, gu, act, ogt, gat, heads_out, split):
+    width, tokens = nt.shape
+    units = gg.shape[1]
+    blocks = units // (2 * LANE)
+    tile = 2 * LANE
+    head_tiles = heads_out.shape[0] // (2 * tile)
+    down_tiles = (blocks + 1) // 2
+    tiles = blocks + head_tiles + down_tiles
+    columns = units + units // 2 + heads_out.shape[0] // 2
+    hbm = pl.BlockSpec(memory_space=pl.ANY)
+    side = lambda t: jnp.where(t < tiles, 1, 0)
+
+    def pair(t):
+        return (0, 2 * jnp.minimum(lax.rem(t, tiles), blocks - 1) + side(t))
+
+    def down(t, shift_by):
+        at = jnp.clip(lax.rem(t, tiles) - blocks - head_tiles, 0, down_tiles - 1)
+        return (0, 2 * jnp.minimum(2 * at + shift_by, blocks - 1) + side(t))
+
+    block = lambda index: pl.BlockSpec((tokens, LANE), index)
     return pl.pallas_call(
-        functools.partial(unit_grads_kernel, split),
-        grid=(units // tile,),
+        functools.partial(early_kernel, split),
+        grid=(2 * tiles,),
         in_specs=[
-            pl.BlockSpec((width, tokens), lambda t: (0, 0)),
-            pl.BlockSpec((tokens, tile), lambda t: (0, t)),
-        ],
-        out_specs=[part, part],
-        out_shape=[jax.ShapeDtypeStruct((width, units // 2), BF)] * 2,
-        compiler_params=params(),
-        cost_estimate=cost(2 * left.size * units),
-        name="unit_grads",
-    )(left, right)
-
-
-def head_grads_kernel(dims, split, core_ref, left_ref, right_ref, out_ref):
-    product = regroup_rows(mxu(left_ref[...], right_ref[...], dims), split)
-    out_ref[0] = product.astype(BF)
-
-
-def head_grads(left, right, dims, split):
+            pl.BlockSpec((width, tokens), lambda t: (0, 0), pipeline_mode=pl.Buffered(1)),
+            block(pair),
+            block(pair),
+            block(lambda t: down(t, 0)),
+            block(lambda t: down(t, 1)),
+            hbm,
+            hbm,
+            hbm,
+        ],
+        out_specs=pl.BlockSpec((width, tile), lambda t: (0, jnp.maximum(t - tiles, 0))),
+        out_shape=jax.ShapeDtypeStruct((width, columns), BF),
+        scratch_shapes=[
+            pltpu.VMEM((width, tokens), BF),
+            pltpu.VMEM((width, tokens), BF),
+            pltpu.VMEM(heads_out.shape, BF),
+            pltpu.VMEM((2, width, tile), BF),
+            pltpu.VMEM((tiles, width, tile), BF),
+            pltpu.SemaphoreType.DMA((3,)),
+            pltpu.SemaphoreType.DMA((tiles,)),
+            pltpu.SemaphoreType.DMA((tiles,)),
+        ],
+        compiler_params=pltpu.CompilerParams(
+            vmem_limit_bytes=56 * MIB, collective_id=3, has_side_effects=True
+        ),
+        cost_estimate=cost(6 * 10**10),
+        name="early_grads",
+    )(nt, gg, gu, act, act, ogt, gat, heads_out)
+
+
+def head_grads_kernel(core_ref, left_ref, right_ref, out_ref):
+    out_ref[0] = mxu(left_ref[...], right_ref[...], NN).astype(BF)
+
+
+def head_grads(left, right):
     rows, tokens = left.shape
-    columns = right.shape[1] if dims == NN else right.shape[0]
+    columns = right.shape[1]
     tile = 2 * LANE
     tiles = columns // tile
     part = tiles // 2
-    at = lambda t, core: (t + core[0] * part) % tiles
-    if dims == NN:
-        spec = pl.BlockSpec((tokens, tile), lambda t, core: (0, at(t, core)))
-    else:
-        spec = pl.BlockSpec((tile, tokens), lambda t, core: (at(t, core), 0))
     return pl.pallas_call(
-        functools.partial(head_grads_kernel, dims, split),
+        head_grads_kernel,
         grid_spec=pltpu.PrefetchScalarGridSpec(
             num_scalar_prefetch=1,
             grid=(tiles,),
-            in_specs=[pl.BlockSpec((rows, tokens), lambda t, core: (0, 0)), spec],
+            in_specs=[
+                pl.BlockSpec((rows, tokens), lambda t, core: (0, 0)),
+                pl.BlockSpec((tokens, tile), lambda t, core: (0, (t + core[0] * part) % tiles)),
+            ],
             out_specs=pl.BlockSpec((1, rows, tile), lambda t, core: (t // part, 0, t % part)),
         ),
         out_shape=jax.ShapeDtypeStruct((2, rows, columns // 2), BF),
         compiler_params=params(),
-        cost_estimate=cost(2 * left.size * columns),
+        cost_estimate=cost(10**8),
         name="head_grads",
     )(lax.axis_index("mp").astype(jnp.int32)[None], left, right)
 
 
 def tail_kernel(
     order, x_ref, gh_ref, dq_ref, nt_ref, gain_ref, wq_ref, wkv_ref, cos_ref, sin_ref, gg2_ref,
-    query_ref, early_ref, near_refs, *refs,
+    query_ref, near_refs, *refs,
 ):
     count_d, count_s = lax.axis_size("dp"), lax.axis_size("seq")
     me_d, me_s, core = lax.axis_index("dp"), lax.axis_index("seq"), lax.axis_index("mp")
-    late = len(order) - 1
+    late = len(order) - len(near_refs)
     far_refs, refs = refs[:late], refs[late:]
-    gi_ref, query_out, small_out, early_out = refs[:4]
+    gi_ref, query_out, small_out = refs[:3]
     (
-        key_in, query_in, query_sum, query_seq, query_part, query_dp, early_in, dw, gg1,
+        key_in, query_in, query_sum, query_seq, query_part, query_dp, dw, gg1,
         small_other, small_in, small_sum, small_seq, small_part, small_dp, sends, receives,
-    ) = refs[4:]
+    ) = refs[3:]
     rows = query_out.shape[0]
     step = pl.program_id(0)
     other_core = {"mp": 1 - core}
@@ -1065,9 +1303,6 @@
 
     to_seq = [lax.rem(me_s + k, count_s) for k in range(1, count_s)]
     to_dp = [lax.rem(me_d + k, count_d) for k in range(1, count_d)]
-    early_copies = [
-        link(early_ref.at[to_dp[k]], early_in.at[k], dp_peers[k]) for k in range(count_d - 1)
-    ]
     key_copies, at = [], 0
     for far in far_refs:
         size = far.shape[1]
@@ -1123,7 +1358,6 @@
         start([query_core])
         for copies in key_copies:
             start(copies)
-        start(early_copies)
         dw[...] = jnp.zeros(dw.shape, F32)
         gg1[...] = jnp.zeros(gg1.shape, F32)
 
@@ -1147,14 +1381,17 @@
         mean = jnp.mean(scaled * x, axis=-1, keepdims=True)
         gi_ref[0] = gh_ref[0] + inverse * scaled - x * (inverse * inverse * inverse * mean)
 
-    begin = order[0][1]
-
-    @pl.when(step < begin)
-    def _():
-        summed = near_refs[0][0].astype(F32)
-        for ref in near_refs[1:]:
-            summed = summed + ref[0].astype(F32)
-        finish(summed)
+    begin = 0
+    for (_, size), terms in zip(order, near_refs):
+
+        @pl.when((step >= begin) & (step < begin + size))
+        def _():
+            summed = terms[0][0].astype(F32)
+            for ref in terms[1:]:
+                summed = summed + ref[0].astype(F32)
+            finish(summed)
+
+        begin += size
 
     base = begin
     for part, far in enumerate(far_refs):
@@ -1202,14 +1439,13 @@
         start(small_seqs)
         by_dp(gather(small_sum[me_s], small_seqs, small_seq), small_part)
         start(small_dps)
-        early_out[...] = gather(early_ref[me_d], early_copies, early_in)
         query_out[...] = gather(query_part[me_d], query_dps, query_dp)
         small_out[...] = gather(small_part[me_d], small_dps, small_dp)
 
 
 def tail(
     order, x, grad_hidden, dq, nt, gain, wq, wkv, cosine, sine_table, grad_gain_two, grad_query,
-    early, near, far,
+    near, far,
 ):
     count, own, width = x.shape
     count_d, count_s = lax.axis_size("dp"), lax.axis_size("seq")
@@ -1229,22 +1465,25 @@
 
     seq = pl.BlockSpec((1, own, width), lambda i: (place(i), 0, 0))
     whole = lambda array: pl.BlockSpec(array.shape, lambda i: (0,) * array.ndim)
-    last = order[0][1] - 1
-    near_spec = pl.BlockSpec((1, kv_rows, own), lambda i: (jnp.minimum(i, last), 0, 0))
-    fixed = [gain, wq, wkv, cosine, sine_table, grad_gain_two, grad_query, early]
+    near_specs, done = [], 0
+    for (_, size), terms in zip(order, near):
+        index = lambda i, done=done, size=size: (jnp.clip(i - done, 0, size - 1), 0, 0)
+        near_specs += [pl.BlockSpec((1, kv_rows, own), index)] * len(terms)
+        done += size
+    fixed = [gain, wq, wkv, cosine, sine_table, grad_gain_two, grad_query]
     outs = [
         jax.ShapeDtypeStruct(x.shape, F32),
         jax.ShapeDtypeStruct((rows, wide), F32),
         jax.ShapeDtypeStruct((rows, narrow), F32),
-        jax.ShapeDtypeStruct((rows, early.shape[2]), F32),
     ]
-    terms = len(near)
+    near_all = [term for terms in near for term in terms]
 
     def kernel(*refs):
-        head, nears, rest = refs[:12], refs[12 : 12 + terms], refs[12 + terms :]
+        head, rest = refs[:11], refs[11 + len(near_all) :]
+        nears = [refs[11 + i * count_s : 11 + (i + 1) * count_s] for i in range(len(near))]
         tail_kernel(order, *head, nears, *rest)
 
-    slots = 3 * (count_d - 1) + (2 + len(far)) * (count_s - 1) + 2
+    slots = 2 * (count_d - 1) + (2 + len(far)) * (count_s - 1) + 2
     return pl.pallas_call(
         kernel,
         grid=(count,),
@@ -1254,7 +1493,7 @@
             pl.BlockSpec((width, own), lambda i: (0, place(i))),
         ]
         + [whole(array) for array in fixed]
-        + [near_spec] * terms
+        + near_specs
         + [whole(array) for array in far],
         out_specs=[seq] + [whole(out) for out in outs[1:]],
         out_shape=outs,
@@ -1265,7 +1504,6 @@
             pltpu.VMEM((count_s - 1, count_d * rows, wide), BF),
             pltpu.VMEM((count_d, rows, wide), BF),
             pltpu.VMEM((count_d - 1, rows, wide), BF),
-            pltpu.VMEM((count_d - 1, rows, early.shape[2]), BF),
             pltpu.VMEM((width, kv_rows), F32),
             pltpu.VMEM((1, width), F32),
             pltpu.VMEM((width, narrow), BF),
@@ -1282,7 +1520,7 @@
         ),
         cost_estimate=cost(4 * 10**10),
         name="tail",
-    )(x, grad_hidden, dq, nt, *fixed, *near, *far)
+    )(x, grad_hidden, dq, nt, *fixed, *near_all, *far)
 
 
 def turn_tables(cosine, sine_table):
@@ -1293,22 +1531,12 @@
     straight = jnp.concatenate([one, cosine, cosine], axis=1)
     ahead = jnp.concatenate([none, sine_table, quiet], axis=1)
     behind = jnp.concatenate([none, quiet, -sine_table], axis=1)
-    return jnp.stack([jnp.concatenate([t, t], axis=1) for t in (straight, ahead, behind)])
+    tables = jnp.stack([jnp.concatenate([t, t], axis=1) for t in (straight, ahead, behind)])
+    return tables * HD ** (-0.5)
 
 
 def after(value, *others):
     return lax.optimization_barrier((value, *others))[0]
-
-
-def spans(count, shares):
-    if count % 4:
-        return [(0, count)]
-    cuts, at = [], 0
-    for share in shares:
-        size = share * count // 4
-        cuts.append((at, size))
-        at += size
-    return cuts
 
 
 def on_device_fast(
@@ -1332,18 +1560,21 @@
     gain_two_float = gain_two.astype(F32)[None]
     cosine, sine_table = rope_tables(my_chunk() * own, own, RD)
     cosine_t, sine_t = cosine.T, sine_table.T
-    kv, normed_t = project_keys(inputs, gain_one_float, keys_weights, cosine_t, sine_t)
-    forward = spans(count, (1, 1, 2))
-    gathered = [gather_keys(kv[at : at + size]) for at, size in forward]
-    q = project_queries(normed_t, queries_weights, cosine_t, sine_t)
-    slopes = unit_slopes(out_grad, (w_down, down_other))
+    half = count // 2
+    kv, normed_t, q, slopes, kv_near, kv_far = project(
+        inputs, out_grad, gain_one_float, keys_weights, queries_weights, (w_down, down_other),
+        cosine_t, sine_t, half,
+    )
+    kv_late = send_near(kv[half:])
     out_other = swap_cores(w_out)
     gate_other, up_other = swap_cores(w_gate), swap_cores(w_up)
-    gathered[0] = list(after(tuple(gathered[0]), slopes))
-    made = ()
-    for (at, _), kv_part in zip(forward, gathered):
-        made = attend_forward(doc_starts, q, kv_part, groups, heads, at, made)
-    heads_out, lse = made
+    span = half - half // 4
+    made = attend_forward(doc_starts, q, [kv_near, kv_far], groups, heads, 0, span, 0, ())
+    kv_late = send_far([after(part, *made) for part in kv_late])
+    made = attend_forward(
+        doc_starts, q, [kv_near, kv_far], groups, heads, span, half - span, span, made
+    )
+    heads_out, lse = attend_forward(doc_starts, q, kv_late, groups, heads, half, half, 0, made)
     out_both = by_core(w_out, out_other, 0)
     (
         outputs, normed_two_t, out_grad_t, active, grad_gate, grad_up, grad_hidden, grad_attended_t,
@@ -1352,51 +1583,54 @@
         inputs, out_grad, slopes, heads_out, gain_two_float, out_both, (w_gate, gate_other),
         (w_up, up_other), (w_down, down_other),
     )
-    def unit_part(left, right, parts):
-        own_part, other_part = unit_grads(left, right, parts)
-        return own_part, swap_cores(other_part)
-
-    parts = [
-        unit_part(normed_two_t, grad_gate, split),
-        unit_part(normed_two_t, grad_up, split),
-        unit_part(out_grad_t, active, split),
-    ]
-    out = head_grads(grad_attended_t, heads_out, NT, split)
-    parts.append((out[0], swap_cores(out[1])))
-    first_sum = jnp.concatenate([mine + other for mine, other in parts], axis=1)
+    units, head_half = w_gate.shape[1], w_out.shape[0]
+    first_sum = early_grads(
+        normed_two_t, grad_gate, grad_up, active, out_grad_t, grad_attended_t, heads_out, split
+    )
     first_sum, grad_heads = lax.optimization_barrier((first_sum, grad_heads))
     first_sum = lax.psum_scatter(first_sum, "seq", scatter_dimension=0, tiled=True)
 
     turns = turn_tables(cosine, sine_table)
-    backward = list(zip(forward, gathered))[::-1]
-    dq, summed = (), []
-    for part, ((at, _), kv_part) in enumerate(backward):
-        first_q = q
-        if part == 1:
-            near = send_keys(summed[0])
-            first_q = after(q, near[0])
+    quarter = half // 2
+    backward = [
+        (half, half, kv_late, 0),
+        (quarter, half - quarter, [kv_near, kv_far], quarter),
+        (0, quarter, [kv_near, kv_far], 0),
+    ]
+    dq, near, summed = (), [], None
+    for part, (at, size, kv_part, kv_at) in enumerate(backward):
+        need = []
+        if part > 0:
+            near.append(send_keys(summed))
+            need = near[-1][:1]
         if part == 2:
-            first_q = after(q, *near)
+            need = [first_sum, *near[0], near[1][0]]
         made_dq, keep, give = attend_backward(
-            doc_starts, first_q, grad_heads, lse, delta, turns, kv_part, groups, heads, at, dq
+            doc_starts, after(q, *need), grad_heads, lse, delta, turns, kv_part, groups, heads, at,
+            size, kv_at, dq,
         )
         dq = (made_dq,)
-        summed.append(join_cores(keep, give))
-    if len(backward) == 1:
-        near = send_keys(summed[0])
-    early = first_sum.reshape(split[0], -1, first_sum.shape[1])
-    grad_query = head_grads(normed_t, dq[0], NN, None)
-    order = [span for span, _ in backward]
-    grad_inputs, query_sum, small_sum, first_sum = tail(
+        if part > 0:
+            give = after(give, *near[-1])
+        summed = join_cores(keep, give)
+    first_sum = first_sum.reshape(split[0], -1, first_sum.shape[1])
+    first_sum = add_up(send_steps(first_sum, "dp", 0))
+    grad_query = head_grads(normed_t, dq[0])
+    order = [span[:2] for span in backward]
+    grad_inputs, query_sum, small_sum = tail(
         order, inputs, grad_hidden, dq[0], normed_t, gain_one_float, queries_weights, keys_weights,
-        cosine_t, sine_t, grad_gain_two, grad_query, early, near,
-        [jnp.stack(terms) for terms in summed[1:]],
+        cosine_t, sine_t, grad_gain_two, grad_query, near,
+        [jnp.stack(summed)],
     )
     half_tied = groups * HD // cores
     late_sum, small_sum = small_sum[:, :half_tied], small_sum[:, half_tied:]
     rows = small_sum.shape[0] // cores
     small_sum = lax.dynamic_slice_in_dim(small_sum, mp_index * rows, rows, 0)
-    units = w_gate.shape[1]
+    pairs = first_sum[:, : 2 * units].reshape(first_sum.shape[0], units // LANE, 2, LANE)
+    gate_sum = pairs[:, :, 0].reshape(-1, units)
+    up_sum = pairs[:, :, 1].reshape(-1, units)
+    out_sum = first_sum[:, 2 * units : 2 * units + head_half]
+    down_sum = first_sum[:, 2 * units + head_half :]
     return (
         outputs,
         grad_inputs,
@@ -1404,11 +1638,11 @@
         query_sum,
         late_sum,
         small_sum[:, :RD],
-        first_sum[:, 3 * units :].T,
+        out_sum.T,
         small_sum[:, RD + 1],
-        first_sum[:, :units],
-        first_sum[:, units : 2 * units],
-        first_sum[:, 2 * units : 3 * units].T,
+        gate_sum,
+        up_sum,
+        down_sum.T,
     )
 
 

time: 587 us -> 563 us (0.959); the launches traced: 585 us -> 554 us
  waiting for transfers between devices: 36.6 us -> 78.9 us
  starting transfers between devices: 115 us -> 79.5 us
  Pallas kernels: 366 us -> 335 us
  other arithmetic: 26.7 us -> 18.4 us
    reduce_scatter x1, waiting for transfers between devices: 0.01 us -> 30.5 us  [on_device_fast(): lax.psum_scatter(first_sum, 'seq', scatter_dimension=0, tiled=True)]
    pallas_call x1, Pallas kernels: 95.2 us -> 65.8 us  [tail(): pl.pallas_call(kernel, grid=(count,), in_specs=[seq, seq, pl.BlockSpec((o...]
    ppermute x25 -> x13, starting transfers between devices: 40.9 us -> 22 us  [swap_cores(): return lax.ppermute(value, 'mp', [(0, 1), (1, 0)])]
    ppermute x12, starting transfers between devices: 74.1 us -> 57.5 us  [shift(): lax.ppermute(value, axis, [(i, (i + by) % size) for i in range(size)])]
    ppermute x12, waiting for transfers between devices: 29.1 us -> 39.4 us  [shift(): lax.ppermute(value, axis, [(i, (i + by) % size) for i in range(size)])]
    pallas_call x3, Pallas kernels: 49.6 us -> 43.5 us  [attend_backward(): pl.pallas_call(functools.partial(attend_back_kernel, groups, heads, first...]
    pallas_call x11 -> x6, Pallas kernels: 133 us -> 137 us  [the longest x1 65 us: early_grads(): pl.pallas_call(functools.partial(early_kernel, split), grid=(2 * tiles,),...]
    unnamed x82 -> x52, local copies, waits for them, and re-layouts: 15.4 us -> 17.4 us
  transfers between devices with their start and end apart: 38 -> 26, of which waited for: 9 -> 9; matrix products, arithmetic and copies ran while one was open for 4% -> 5% of each run, Pallas kernels for 28% -> 21%
where the time goes in v3:
time: 563 us; the launch traced here: 554 us
  Pallas kernels  335 us (60%)
  starting transfers between devices  79.5 us (14%)
  waiting for transfers between devices  78.9 us (14%)
  local copies, waits for them, and re-layouts  28.3 us (5%)
  other arithmetic  18.4 us (3%)
  between operations  14.6 us (3%)
    pallas_call x1, Pallas kernels, feed(): pl.pallas_call(feed_kernel, grid=(count,), in_specs=[seq, seq, row, colum...  88.1 us
    pallas_call x1, Pallas kernels, tail(): pl.pallas_call(kernel, grid=(count,), in_specs=[seq, seq, pl.BlockSpec((o...  65.8 us
    pallas_call x1, Pallas kernels, early_grads(): pl.pallas_call(functools.partial(early_kernel, split), grid=(2 * tiles,),...  65 us
    ppermute x12, starting transfers between devices, shift(): lax.ppermute(value, axis, [(i, (i + by) % size) for i in range(size)])  57.5 us
    pallas_call x3, Pallas kernels, attend_backward(): pl.pallas_call(functools.partial(attend_back_kernel, groups, heads, first...  43.5 us
    pallas_call x1, Pallas kernels, project(): pl.pallas_call(functools.partial(project_kernel, sent), grid=(count,), in...  43.1 us
    ppermute x12, waiting for transfers between devices, shift(): lax.ppermute(value, axis, [(i, (i + by) % size) for i in range(size)])  39.4 us
    reduce_scatter x1, waiting for transfers between devices, on_device_fast(): lax.psum_scatter(first_sum, 'seq', scatter_dimension=0, tiled=True)  30.5 us
  transfers between devices with their start and end apart: 26, of which 9 were waited for; matrix products, arithmetic and copies ran while one was open for 5% of the time, Pallas kernels for 21%

profile of v3, /device:TPU:0, one launch (start us, length us, event | category | flops | bytes accessed | tf_op | source)
XLA Modules:
  0.0 554.3 jit_solution(11050353475557492699)
XLA Ops:
  7.8 1.5 copy.34
  9.9 1.1 copy.33
  12.2 0.6 broadcast_in_dim.65
  12.8 0.8 multiply_sine_fusion.1
  13.5 4.6 collective-permute-done
  18.1 1.0 broadcast_select_fusion.5
  19.1 0.8 pad_maximum_fusion.3.wkv_ref.refs_6_
  19.9 1.5 broadcast_select_fusion.1
  21.5 1.5 pad_maximum_fusion.wq_ref.refs_5_
  22.9 1.5 pad_maximum_fusion.1.wo_ref
  24.5 43.1 %project.1 = (bf16[8,288,256]{2,1,0:T(8,128)(2,1)}, bf16[1024,2048]{1,0:T(8,128)(2,1)}, bf16[1024,2048]{1,0:T(8,128)(2,1)}, bf16[2048,2816]{1,0:T(8,128)(2,1)}, ...) custom-call(bf16[8,256,1024]{2,1,0:T(8,128)(2,1)} %refs_0_.1, bf16[8,256,1024]{2,1,0:T(8,128)(2,1)} %og_ref.3, ...), custom_call_target="tpu_custom_call" | custom-call | flops 30000001024 | tf_op jit(solution)/shard_map/project/pallas_call | solution.py:517
  67.6 1.1 slice.105
  68.7 0.8 collective-permute-start.5
  69.5 1.3 collective-permute-start.4
  71.4 7.1 %attend.3 = (bf16[1024,2048]{1,0:T(8,128)(2,1)}, f32[8,4,1024]{2,1,0:T(4,128)}) custom-call(s32[8,8]{1,0:T(8,128)} %docs_ref.11, bf16[1024,2048]{1,0:T(8,128)(2,1)} %get-tuple-element.90.q_ref, bf16[4,4,288,256]{3,2,1,0:T(8,128)(2,1)} %get-tuple-element.59.refs_0_, bf16[4,4,288,256]{3,2,1,0:T(8,128)(2,1)} %get-tuple-element.60.refs_1_), custom_call_target="tpu_custom_call" | custom-call | flops 30000001024 | tf_op jit(solution)/shard_map/attend/pallas_call | solution.py:736
  78.5 4.8 collective-permute-start.6
  83.3 1.7 collective-permute-done.5
  84.9 12.5 %collective-permute-done.4 = bf16[4,288,256]{2,1,0:T(8,128)(2,1)S(1)} collective-permute-done((bf16[4,288,256]{2,1,0:T(8,128)(2,1)S(1)}, bf16[4,288,256]{2,1,0:T(8,128)(2,1)S(1)}, u32[]{:S(2)}, u32[]{:S(2)}) %collective-permute-start.4) | collective-permute-done | bytes 589856 | tf_op jit(solution)/shard_map/ppermute | solution.py:367
  98.1 4.3 attend.4
  102.4 2.2 collective-permute-start.12
  104.7 8.9 %attend.5 = (bf16[1024,2048]{1,0:T(8,128)(2,1)}, f32[8,4,1024]{2,1,0:T(4,128)}) custom-call(s32[8,8]{1,0:T(8,128)} %docs_ref.11, bf16[1024,2048]{1,0:T(8,128)(2,1)} %get-tuple-element.90.q_ref, bf16[1,4,288,256]{3,2,1,0:T(8,128)(2,1)} %bitcast.65, bf16[1,4,288,256]{3,2,1,0:T(8,128)(2,1)} %bitcast.80, ...), custom_call_target="tpu_custom_call", output_to_operand_aliasing={{0}: (10, {}), {1}: (11, {})} | custom-call | flops 40000000000 | tf_op jit(solution)/shard_map/attend/pallas_call | solution.py:736
  113.6 1.5 copy-done.13
  115.2 88.1 %feed.1 = (bf16[8,256,1024]{2,1,0:T(8,128)(2,1)}, bf16[1024,2048]{1,0:T(8,128)(2,1)}, bf16[1024,2048]{1,0:T(8,128)(2,1)}, bf16[2048,2816]{1,0:T(8,128)(2,1)}, bf...) custom-call(bf16[8,256,1024]{2,1,0:T(8,128)(2,1)} %refs_0_.1, ...), custom_call_target="tpu_custom_call" | custom-call | flops 67645734912 | tf_op jit(solution)/shard_map/feed/pallas_call | solution.py:1055
  203.3 65.0 %early_grads.1 = bf16[1024,4736]{1,0:T(8,128)(2,1)} custom-call(bf16[1024,2048]{1,0:T(8,128)(2,1)} %get-tuple-element.72.nt_ref, bf16[2048,2816]{1,0:T(8,128)(2,1)} %get-tuple-element.73.gg_ref, bf16[2048,2816]{1,0:T(8,128)(2,1)} %get-tuple-element.74.gu_ref, bf16[2048,2816]{1,0:T(8,128)(2,1)} %get-tuple-element.75.act_ref.act_next_ref, ...), custom_call_target="tpu_custom_call" | custom-call | flops 60000002048 | tf_op jit(solution)/shard_map/early_grads/pallas_call | solution.py:1211
  268.4 0.6 copy-done.7
  270.4 0.8 maximum_multiply_fusion.rot_ref
  271.2 20.4 %attend_back.3 = (bf16[2048,1024]{1,0:T(8,128)(2,1)}, bf16[4,4,288,256]{3,2,1,0:T(8,128)(2,1)}, bf16[4,4,288,256]{3,2,1,0:T(8,128)(2,1)}) custom-call(s32[8,8]{1,0:T(8,128)} %docs_ref.11, bf16[1024,2048]{1,0:T(8,128)(2,1)} %get-tuple-element.90.q_ref, bf16[1024,2048]{1,0:T(8,128)(2,1)} %get-tuple-element.80.do_ref, f32[8,4,1024]{2,1,0:T(4,128)} %get-tuple-element.81.lse_ref, ...), custom_call_target="tpu_custom_call" | custom-call | flops 4000000000 | tf_op jit(solution)/shard_map/attend_back/pallas_call | solution.py:919
  291.6 9.8 %collective-permute-start.13 = (bf16[4,4,288,256]{3,2,1,0:T(8,128)(2,1)}, bf16[4,4,288,256]{3,2,1,0:T(8,128)(2,1)S(1)}, u32[]{:S(2)}, u32[]{:S(2)}) collective-permute-start(bf16[4,4,288,256]{3,2,1,0:T(8,128)(2,1)} %get-tuple-element.84), channel_id=1, source_target_pairs={{0,1},{1,0},{2,3},{3,2},{4,5},{5,4},{6,7},{7,6},{8,9},{9,8},{10,11... | collective-permute-start | bytes 7077896 | tf_op jit(solution)/shard_map/ppermute | solution.py:362
  301.4 4.4 collective-permute-done.13
  305.8 3.2 fusion.5
  309.0 23.6 %collective-permute-start.14 = (bf16[4,288,256]{2,1,0:T(8,128)(2,1)S(1)}, bf16[4,288,256]{2,1,0:T(8,128)(2,1)S(1)}, u32[]{:S(2)}, u32[]{:S(2)}) collective-permute-start(bf16[4,288,256]{2,1,0:T(8,128)(2,1)S(1)} %get-tuple-element.107), channel_id=1, source_target_pairs={{0,2},{2,4},{4,6},{6,0},{1,3},{3,5},{5,7},{7,1},{8,10},{10,12},{12... | collective-permute-start | bytes 1769480 | tf_op jit(solution)/shard_map/ppermute | solution.py:367
  332.6 23.5 %collective-permute-start.15 = (bf16[4,288,256]{2,1,0:T(8,128)(2,1)S(1)}, bf16[4,288,256]{2,1,0:T(8,128)(2,1)S(1)}, u32[]{:S(2)}, u32[]{:S(2)}) collective-permute-start(bf16[4,288,256]{2,1,0:T(8,128)(2,1)S(1)} %get-tuple-element.106), channel_id=1, source_target_pairs={{0,4},{2,6},{4,0},{6,2},{1,5},{3,7},{5,1},{7,3},{8,12},{10,14},{12... | collective-permute-start | bytes 1769480 | tf_op jit(solution)/shard_map/ppermute | solution.py:367
  356.1 11.3 %attend_back.4 = (bf16[2048,1024]{1,0:T(8,128)(2,1)}, bf16[4,2,288,256]{3,2,1,0:T(8,128)(2,1)}, bf16[4,2,288,256]{3,2,1,0:T(8,128)(2,1)}) custom-call(s32[8,8]{1,0:T(8,128)} %docs_ref.11, bf16[1024,2048]{1,0:T(8,128)(2,1)} %get-tuple-element.90.q_ref, bf16[1024,2048]{1,0:T(8,128)(2,1)} %get-tuple-element.80.do_ref, ...), custom_call_target="tpu_custom_call", output_to_operand_aliasing={{0}: (8, {})} | custom-call | flops 2000000000 | tf_op jit(solution)/shard_map/attend_back/pallas_call | solution.py:919
  367.4 2.3 collective-permute-done.14.refs_12_
  369.6 12.1 %collective-permute-done.15.refs_13_ = bf16[4,288,256]{2,1,0:T(8,128)(2,1)S(1)} collective-permute-done((bf16[4,288,256]{2,1,0:T(8,128)(2,1)S(1)}, bf16[4,288,256]{2,1,0:T(8,128)(2,1)S(1)}, u32[]{:S(2)}, u32[]{:S(2)}) %collective-permute-start.15) | collective-permute-done | bytes 589856 | tf_op jit(solution)/shard_map/ppermute | solution.py:367
  381.8 0.8 copy-done.15
  382.8 30.5 %reduce-scatter.2.cloned.1.call-done = bf16[256,4736]{1,0:T(8,128)(2,1)} async-done(((bf16[1024,4736]{1,0:T(8,128)(2,1)}), bf16[256,4736]{1,0:T(8,128)(2,1)}) %reduce-scatter.2.cloned.1.call-update) | async-done | bytes 2424848 | tf_op jit(solution)/shard_map/reduce_scatter | solution.py:1591
  413.3 2.6 dynamic-slice_bitcast_fusion.2
  415.9 1.5 collective-permute-start.22
  417.4 2.4 collective-permute-start.23
  419.8 1.4 collective-permute-start.24
  421.2 1.0 fusion.9
  422.2 1.4 collective-permute-start.18
  423.6 0.6 collective-permute-start.19
  424.3 6.9 %collective-permute-done.18.refs_16_ = bf16[2,288,256]{2,1,0:T(8,128)(2,1)S(1)} collective-permute-done((bf16[2,288,256]{2,1,0:T(8,128)(2,1)S(1)}, bf16[2,288,256]{2,1,0:T(8,128)(2,1)S(1)}, u32[]{:S(2)}, u32[]{:S(2)}) %collective-permute-start.18) | collective-permute-done | bytes 294944 | tf_op jit(solution)/shard_map/ppermute | solution.py:367
  431.1 0.7 copy-done.20
  432.3 11.7 %attend_back.5 = (bf16[2048,1024]{1,0:T(8,128)(2,1)}, bf16[4,2,288,256]{3,2,1,0:T(8,128)(2,1)}, bf16[4,2,288,256]{3,2,1,0:T(8,128)(2,1)}) custom-call(s32[8,8]{1,0:T(8,128)} %docs_ref.11, bf16[1024,2048]{1,0:T(8,128)(2,1)} %get-tuple-element.90.q_ref, bf16[1024,2048]{1,0:T(8,128)(2,1)} %get-tuple-element.80.do_ref, ...), custom_call_target="tpu_custom_call", output_to_operand_aliasing={{0}: (8, {})} | custom-call | flops 2000000000 | tf_op jit(solution)/shard_map/attend_back/pallas_call | solution.py:919
  444.0 2.8 collective-permute-start.21
  446.9 8.6 %head_grads.1.refs_10_ = bf16[2,1024,512]{2,1,0:T(8,128)(2,1)} custom-call(s32[1]{0:T(128)} %bitcast.21.core_ref, bf16[1024,2048]{1,0:T(8,128)(2,1)} %get-tuple-element.93.left_ref.refs_3_, bf16[2048,1024]{1,0:T(8,128)(2,1)} %get-tuple-element.92.right_ref.refs_2_), custom_call_target="tpu_custom_call" | custom-call | flops 100000000 | tf_op jit(solution)/shard_map/head_grads/pallas_call | solution.py:1254
  455.5 4.0 collective-permute-done.23
  459.5 1.9 fusion.1
  461.9 1.9 slice_reduce_fusion
  463.8 0.8 copy.40
  464.7 0.8 copy.41
  465.5 0.7 slice_bitcast_fusion.1
  466.2 0.8 slice_bitcast_fusion
  466.9 1.6 add_convert_fusion.7
  468.5 1.2 pad_maximum_fusion.2.refs_19_
  469.7 65.8 %tail.1 = (f32[8,256,1024]{2,1,0:T(8,128)}, f32[64,512]{1,0:T(8,128)}, f32[64,256]{1,0:T(8,128)}) custom-call(bf16[8,256,1024]{2,1,0:T(8,128)(2,1)} %refs_0_.1, f32[8,256,1024]{2,1,0:T(8,128)} %get-tuple-element.71.refs_1_, bf16[2048,1024]{1,0:T(8,128)(2,1)} %get-tuple-element.92.right_ref.refs_2_, bf16[1024,2048]{1,0:T(8,128)(2,1)} %get-tuple-element.93.left_ref.refs_3_, ...), custom_call_target="tpu_custom_call" | custom-call | flops 40000000000 | tf_op jit(solution)/shard_map/tail/pallas_call | solution.py:1487
  535.4 1.4 fusion.11
  536.8 0.6 constant_dynamic-slice_fusion
  537.4 0.7 dynamic-slice_reduce_fusion
  538.1 8.5 %copy.50 = f32[8,256,1024]{2,1,0:T(8,128)} copy(f32[8,256,1024]{2,1,0:T(8,128)} %get-tuple-element.147) | data formatting | bytes 16777216
  546.6 0.7 copy.51
  (85 shorter events, 6.1 us)
Async XLA Ops:
  7.2 2.3 copy-start.2
  7.2 4.4 copy-start.10
  7.2 5.0 copy-start.11
  7.2 11.9 %copy-start.5 = (bf16[1024,32]{0,1:T(8,128)(2,1)S(1)}, bf16[1024,32]{0,1:T(8,128)(2,1)}, u32[]{:S(2)}) copy-start(bf16[1024,32]{0,1:T(8,128)(2,1)} %param.16) | copy-start | bytes 196612
  7.2 406.1 %reduce-scatter.2.cloned.1.call-start = ((), (), s32[]{:S(2)}) async-start(), calls=%async_computation.1 | async-start | bytes 12124160 | tf_op jit(solution)/shard_map/reduce_scatter | solution.py:1591
  7.3 17.2 %collective-permute-start.2 = (bf16[1408,1024]{1,0:T(8,128)(2,1)}, bf16[1408,1024]{1,0:T(8,128)(2,1)}, u32[]{:S(2)}, u32[]{:S(2)}) collective-permute-start(bf16[1408,1024]{1,0:T(8,128)(2,1)} %wdo_ref.3), channel_id=1, source_target_pairs={{0,1},{1,0},{2,3},{3,2},{4,5},{5,4},{6,7},{7,6},{8,9},{9,8},{10,11... | collective-permute-start | bytes 8650760 | tf_op jit(solution)/shard_map/ppermute | solution.py:362
  9.3 10.7 %collective-permute-start.1 = (bf16[512,1024]{1,0:T(8,128)(2,1)S(1)}, bf16[512,1024]{1,0:T(8,128)(2,1)S(1)}, u32[]{:S(2)}, u32[]{:S(2)}) collective-permute-start(bf16[512,1024]{1,0:T(8,128)(2,1)S(1)} %bitcast.59), channel_id=1, source_target_pairs={{0,1},{1,0},{2,3},{3,2},{4,5},{5,4},{6,7},{7,6},{8,9},{9,8},{10,11... | collective-permute-start | bytes 3145736 | tf_op jit(solution)/shard_map/ppermute | solution.py:362
  9.5 10.4 %collective-permute-start.10 = (bf16[512,1024]{1,0:T(8,128)(2,1)S(1)}, bf16[512,1024]{1,0:T(8,128)(2,1)}, u32[]{:S(2)}, u32[]{:S(2)}) collective-permute-start(bf16[512,1024]{1,0:T(8,128)(2,1)S(1)} %copy-done.2), channel_id=1, source_target_pairs={{0,1},{1,0},{2,3},{3,2},{4,5},{5,4},{6,7},{7,6},{8,9},{9,8},{10,11... | collective-permute-start | bytes 3145736 | tf_op jit(solution)/shard_map/ppermute | solution.py:362
  10.9 7.1 %collective-permute-start = (bf16[128,1024]{1,0:T(8,128)(2,1)S(1)}, bf16[128,1024]{1,0:T(8,128)(2,1)}, u32[]{:S(2)}, u32[]{:S(2)}) collective-permute-start(bf16[128,1024]{1,0:T(8,128)(2,1)S(1)} %bitcast.64), channel_id=1, source_target_pairs={{0,1},{1,0},{2,3},{3,2},{4,5},{5,4},{6,7},{7,6},{8,9},{9,8},{10,11... | collective-permute-start | bytes 786440 | tf_op jit(solution)/shard_map/ppermute | solution.py:362
  11.2 102.4 %collective-permute-start.11 = (bf16[1024,1408]{1,0:T(8,128)(2,1)}, bf16[1024,1408]{1,0:T(8,128)(2,1)}, u32[]{:S(2)}, u32[]{:S(2)}) collective-permute-start(bf16[1024,1408]{1,0:T(8,128)(2,1)} %wgo_ref.1), channel_id=1, source_target_pairs={{0,1},{1,0},{2,3},{3,2},{4,5},{5,4},{6,7},{7,6},{8,9},{9,8},{10,11... | collective-permute-start | bytes 8650760 | tf_op jit(solution)/shard_map/ppermute | solution.py:362
  11.5 9.9 %copy-start.6 = (f32[256]{0:T(256)}, f32[256]{0:T(256)S(1)}, u32[]{:S(2)}) copy-start(f32[256]{0:T(256)S(1)} %add_convert_fusion.12) | copy-start | bytes 3076
  11.5 9.9 %copy-start.8 = (f32[16]{0:T(128)}, f32[16]{0:T(128)S(1)}, u32[]{:S(2)}) copy-start(f32[16]{0:T(128)S(1)} %multiply_power_fusion) | copy-start | bytes 196
  68.7 9.8 %copy-start.3 = (bf16[4,288,256]{2,1,0:T(8,128)(2,1)}, bf16[4,288,256]{2,1,0:T(8,128)(2,1)S(1)}, u32[]{:S(2)}) copy-start(bf16[4,288,256]{2,1,0:T(8,128)(2,1)S(1)} %slice.105) | copy-start | bytes 1769476
  68.7 16.2 %collective-permute-start.5 = (bf16[4,288,256]{2,1,0:T(8,128)(2,1)S(1)}, bf16[4,288,256]{2,1,0:T(8,128)(2,1)S(1)}, u32[]{:S(2)}, u32[]{:S(2)}) collective-permute-start(bf16[4,288,256]{2,1,0:T(8,128)(2,1)S(1)} %slice.105), channel_id=1, source_target_pairs={{0,6},{2,0},{4,2},{6,4},{1,7},{3,1},{5,3},{7,5},{8,14},{10,8},{12,... | collective-permute-start | bytes 1769480 | tf_op jit(solution)/shard_map/ppermute | solution.py:367
  69.5 27.9 %collective-permute-start.4 = (bf16[4,288,256]{2,1,0:T(8,128)(2,1)S(1)}, bf16[4,288,256]{2,1,0:T(8,128)(2,1)S(1)}, u32[]{:S(2)}, u32[]{:S(2)}) collective-permute-start(bf16[4,288,256]{2,1,0:T(8,128)(2,1)S(1)} %slice.105), channel_id=1, source_target_pairs={{0,4},{2,6},{4,0},{6,2},{1,5},{3,7},{5,1},{7,3},{8,12},{10,14},{12... | collective-permute-start | bytes 1769480 | tf_op jit(solution)/shard_map/ppermute | solution.py:367
  70.8 26.6 %collective-permute-start.3 = (bf16[4,288,256]{2,1,0:T(8,128)(2,1)S(1)}, bf16[4,288,256]{2,1,0:T(8,128)(2,1)S(1)}, u32[]{:S(2)}, u32[]{:S(2)}) collective-permute-start(bf16[4,288,256]{2,1,0:T(8,128)(2,1)S(1)} %slice.105), channel_id=1, source_target_pairs={{0,2},{2,4},{4,6},{6,0},{1,3},{3,5},{5,7},{7,1},{8,10},{10,12},{12... | collective-permute-start | bytes 1769480 | tf_op jit(solution)/shard_map/ppermute | solution.py:367
  78.5 23.9 %copy-start.12 = (bf16[1024,1408]{1,0:T(8,128)(2,1)S(1)}, bf16[1024,1408]{1,0:T(8,128)(2,1)}, u32[]{:S(2)}) copy-start(bf16[1024,1408]{1,0:T(8,128)(2,1)} %wuo_ref.1) | copy-start | bytes 8650756
  78.5 23.9 %collective-permute-start.6 = (bf16[4,288,256]{2,1,0:T(8,128)(2,1)S(1)}, bf16[4,288,256]{2,1,0:T(8,128)(2,1)}, u32[]{:S(2)}, u32[]{:S(2)}) collective-permute-start(bf16[4,288,256]{2,1,0:T(8,128)(2,1)S(1)} %slice.105), channel_id=1, source_target_pairs={{0,1},{1,0},{2,3},{3,2},{4,5},{5,4},{6,7},{7,6},{8,9},{9,8},{10,11... | collective-permute-start | bytes 1769480 | tf_op jit(solution)/shard_map/ppermute | solution.py:362
  84.9 17.5 %copy-start.17 = (bf16[4,288,256]{2,1,0:T(8,128)(2,1)}, bf16[4,288,256]{2,1,0:T(8,128)(2,1)S(1)}, u32[]{:S(2)}) copy-start(bf16[4,288,256]{2,1,0:T(8,128)(2,1)S(1)} %collective-permute-done.5) | copy-start | bytes 1769476
  97.4 5.0 copy-start.18
  97.4 5.0 copy-start.19
  97.5 7.2 %collective-permute-start.9 = (bf16[4,288,256]{2,1,0:T(8,128)(2,1)S(1)}, bf16[4,288,256]{2,1,0:T(8,128)(2,1)}, u32[]{:S(2)}, u32[]{:S(2)}) collective-permute-start(bf16[4,288,256]{2,1,0:T(8,128)(2,1)S(1)} %collective-permute-done.5), channel_id=1, source_target_pairs={{0,1},{1,0},{2,3},{3,2},{4,5},{5,4},{6,7},{7,6},{8,9},{9,8},{10,11... | collective-permute-start | bytes 1769480 | tf_op jit(solution)/shard_map/ppermute | solution.py:362
  97.5 7.1 %collective-permute-start.8 = (bf16[4,288,256]{2,1,0:T(8,128)(2,1)S(1)}, bf16[4,288,256]{2,1,0:T(8,128)(2,1)}, u32[]{:S(2)}, u32[]{:S(2)}) collective-permute-start(bf16[4,288,256]{2,1,0:T(8,128)(2,1)S(1)} %collective-permute-done.4), channel_id=1, source_target_pairs={{0,1},{1,0},{2,3},{3,2},{4,5},{5,4},{6,7},{7,6},{8,9},{9,8},{10,11... | collective-permute-start | bytes 1769480 | tf_op jit(solution)/shard_map/ppermute | solution.py:362
  98.0 6.6 %collective-permute-start.7 = (bf16[4,288,256]{2,1,0:T(8,128)(2,1)S(1)}, bf16[4,288,256]{2,1,0:T(8,128)(2,1)}, u32[]{:S(2)}, u32[]{:S(2)}) collective-permute-start(bf16[4,288,256]{2,1,0:T(8,128)(2,1)S(1)} %collective-permute-done.3), channel_id=1, source_target_pairs={{0,1},{1,0},{2,3},{3,2},{4,5},{5,4},{6,7},{7,6},{8,9},{9,8},{10,11... | collective-permute-start | bytes 1769480 | tf_op jit(solution)/shard_map/ppermute | solution.py:362
  102.4 11.2 %collective-permute-start.12 = (bf16[1024,1408]{1,0:T(8,128)(2,1)S(1)}, bf16[1024,1408]{1,0:T(8,128)(2,1)S(1)}, u32[]{:S(2)}, u32[]{:S(2)}) collective-permute-start(bf16[1024,1408]{1,0:T(8,128)(2,1)S(1)} %copy-done.12), channel_id=1, source_target_pairs={{0,1},{1,0},{2,3},{3,2},{4,5},{5,4},{6,7},{7,6},{8,9},{9,8},{10,11... | collective-permute-start | bytes 8650760 | tf_op jit(solution)/shard_map/ppermute | solution.py:362
  113.6 1.6 copy-start.13
  268.4 0.7 copy-start.7
  268.4 0.7 copy-start.9
  291.6 14.2 %collective-permute-start.13 = (bf16[4,4,288,256]{3,2,1,0:T(8,128)(2,1)}, bf16[4,4,288,256]{3,2,1,0:T(8,128)(2,1)S(1)}, u32[]{:S(2)}, u32[]{:S(2)}) collective-permute-start(bf16[4,4,288,256]{3,2,1,0:T(8,128)(2,1)} %get-tuple-element.84), channel_id=1, source_target_pairs={{0,1},{1,0},{2,3},{3,2},{4,5},{5,4},{6,7},{7,6},{8,9},{9,8},{10,11... | collective-permute-start | bytes 7077896 | tf_op jit(solution)/shard_map/ppermute | solution.py:362
  309.0 60.7 %collective-permute-start.14 = (bf16[4,288,256]{2,1,0:T(8,128)(2,1)S(1)}, bf16[4,288,256]{2,1,0:T(8,128)(2,1)S(1)}, u32[]{:S(2)}, u32[]{:S(2)}) collective-permute-start(bf16[4,288,256]{2,1,0:T(8,128)(2,1)S(1)} %get-tuple-element.107), channel_id=1, source_target_pairs={{0,2},{2,4},{4,6},{6,0},{1,3},{3,5},{5,7},{7,1},{8,10},{10,12},{12... | collective-permute-start | bytes 1769480 | tf_op jit(solution)/shard_map/ppermute | solution.py:367
  332.6 49.2 %collective-permute-start.15 = (bf16[4,288,256]{2,1,0:T(8,128)(2,1)S(1)}, bf16[4,288,256]{2,1,0:T(8,128)(2,1)S(1)}, u32[]{:S(2)}, u32[]{:S(2)}) collective-permute-start(bf16[4,288,256]{2,1,0:T(8,128)(2,1)S(1)} %get-tuple-element.106), channel_id=1, source_target_pairs={{0,4},{2,6},{4,0},{6,2},{1,5},{3,7},{5,1},{7,3},{8,12},{10,14},{12... | collective-permute-start | bytes 1769480 | tf_op jit(solution)/shard_map/ppermute | solution.py:367
  356.1 25.7 %collective-permute-start.16 = (bf16[4,288,256]{2,1,0:T(8,128)(2,1)S(1)}, bf16[4,288,256]{2,1,0:T(8,128)(2,1)S(1)}, u32[]{:S(2)}, u32[]{:S(2)}) collective-permute-start(bf16[4,288,256]{2,1,0:T(8,128)(2,1)S(1)} %get-tuple-element.105), channel_id=1, source_target_pairs={{0,6},{2,0},{4,2},{6,4},{1,7},{3,1},{5,3},{7,5},{8,14},{10,8},{12,... | collective-permute-start | bytes 1769480 | tf_op jit(solution)/shard_map/ppermute | solution.py:367
  367.4 53.9 %copy-start = (bf16[4,2,288,256]{3,2,1,0:T(8,128)(2,1)S(1)}, bf16[4,2,288,256]{3,2,1,0:T(8,128)(2,1)}, u32[]{:S(2)}) copy-start(bf16[4,2,288,256]{3,2,1,0:T(8,128)(2,1)} %get-tuple-element.87) | copy-start | bytes 3538948
  369.6 12.1 %copy-start.14 = (bf16[4,288,256]{2,1,0:T(8,128)(2,1)}, bf16[4,288,256]{2,1,0:T(8,128)(2,1)S(1)}, u32[]{:S(2)}) copy-start(bf16[4,288,256]{2,1,0:T(8,128)(2,1)S(1)} %collective-permute-done.14.refs_12_) | copy-start | bytes 1769476
  381.8 0.8 copy-start.15
  381.8 1.0 copy-start.16
  382.8 38.4 %collective-permute-start.17 = (bf16[4,2,288,256]{3,2,1,0:T(8,128)(2,1)}, bf16[4,2,288,256]{3,2,1,0:T(8,128)(2,1)S(1)}, u32[]{:S(2)}, u32[]{:S(2)}) collective-permute-start(bf16[4,2,288,256]{3,2,1,0:T(8,128)(2,1)} %get-tuple-element.89), channel_id=1, source_target_pairs={{0,1},{1,0},{2,3},{3,2},{4,5},{5,4},{6,7},{7,6},{8,9},{9,8},{10,11... | collective-permute-start | bytes 3538952 | tf_op jit(solution)/shard_map/ppermute | solution.py:362
  415.9 39.6 %collective-permute-start.22 = (bf16[64,4736]{1,0:T(8,128)(2,1)}, bf16[64,4736]{1,0:T(8,128)(2,1)}, u32[]{:S(2)}, u32[]{:S(2)}) collective-permute-start(bf16[64,4736]{1,0:T(8,128)(2,1)} %get-tuple-element.109), channel_id=1, source_target_pairs={{0,8},{8,16},{16,24},{24,0},{1,9},{9,17},{17,25},{25,1},{2,10},{10... | collective-permute-start | bytes 1818632 | tf_op jit(solution)/shard_map/ppermute | solution.py:367
  417.4 42.1 %collective-permute-start.23 = (bf16[64,4736]{1,0:T(8,128)(2,1)}, bf16[64,4736]{1,0:T(8,128)(2,1)}, u32[]{:S(2)}, u32[]{:S(2)}) collective-permute-start(bf16[64,4736]{1,0:T(8,128)(2,1)} %get-tuple-element.111), channel_id=1, source_target_pairs={{0,16},{8,24},{16,0},{24,8},{1,17},{9,25},{17,1},{25,9},{2,18},{10... | collective-permute-start | bytes 1818632 | tf_op jit(solution)/shard_map/ppermute | solution.py:367
  419.8 39.7 %collective-permute-start.24 = (bf16[64,4736]{1,0:T(8,128)(2,1)S(1)}, bf16[64,4736]{1,0:T(8,128)(2,1)}, u32[]{:S(2)}, u32[]{:S(2)}) collective-permute-start(bf16[64,4736]{1,0:T(8,128)(2,1)S(1)} %get-tuple-element.110), channel_id=1, source_target_pairs={{0,24},{8,0},{16,8},{24,16},{1,25},{9,1},{17,9},{25,17},{2,26},{10... | collective-permute-start | bytes 1818632 | tf_op jit(solution)/shard_map/ppermute | solution.py:367
  422.2 8.9 %collective-permute-start.18 = (bf16[2,288,256]{2,1,0:T(8,128)(2,1)S(1)}, bf16[2,288,256]{2,1,0:T(8,128)(2,1)S(1)}, u32[]{:S(2)}, u32[]{:S(2)}) collective-permute-start(bf16[2,288,256]{2,1,0:T(8,128)(2,1)S(1)} %get-tuple-element.118), channel_id=1, source_target_pairs={{0,2},{2,4},{4,6},{6,0},{1,3},{3,5},{5,7},{7,1},{8,10},{10,12},{12... | collective-permute-start | bytes 884744 | tf_op jit(solution)/shard_map/ppermute | solution.py:367
  423.6 20.4 %collective-permute-start.19 = (bf16[2,288,256]{2,1,0:T(8,128)(2,1)S(1)}, bf16[2,288,256]{2,1,0:T(8,128)(2,1)S(1)}, u32[]{:S(2)}, u32[]{:S(2)}) collective-permute-start(bf16[2,288,256]{2,1,0:T(8,128)(2,1)S(1)} %get-tuple-element.117), channel_id=1, source_target_pairs={{0,4},{2,6},{4,0},{6,2},{1,5},{3,7},{5,1},{7,3},{8,12},{10,14},{12... | collective-permute-start | bytes 884744 | tf_op jit(solution)/shard_map/ppermute | solution.py:367
  431.1 0.7 copy-start.20
  431.8 12.2 %collective-permute-start.20 = (bf16[2,288,256]{2,1,0:T(8,128)(2,1)S(1)}, bf16[2,288,256]{2,1,0:T(8,128)(2,1)S(1)}, u32[]{:S(2)}, u32[]{:S(2)}) collective-permute-start(bf16[2,288,256]{2,1,0:T(8,128)(2,1)S(1)} %get-tuple-element.116), channel_id=1, source_target_pairs={{0,6},{2,0},{4,2},{6,4},{1,7},{3,1},{5,3},{7,5},{8,14},{10,8},{12,... | collective-permute-start | bytes 884744 | tf_op jit(solution)/shard_map/ppermute | solution.py:367
  444.0 11.5 %copy-start.21 = (bf16[2,288,256]{2,1,0:T(8,128)(2,1)}, bf16[2,288,256]{2,1,0:T(8,128)(2,1)S(1)}, u32[]{:S(2)}) copy-start(bf16[2,288,256]{2,1,0:T(8,128)(2,1)S(1)} %collective-permute-done.19.refs_17_) | copy-start | bytes 884740
  444.0 11.5 %copy-start.22 = (bf16[2,288,256]{2,1,0:T(8,128)(2,1)}, bf16[2,288,256]{2,1,0:T(8,128)(2,1)S(1)}, u32[]{:S(2)}) copy-start(bf16[2,288,256]{2,1,0:T(8,128)(2,1)S(1)} %collective-permute-done.20.refs_18_) | copy-start | bytes 884740
  444.0 22.9 %collective-permute-start.21 = (bf16[4,2,288,256]{3,2,1,0:T(8,128)(2,1)}, bf16[4,2,288,256]{3,2,1,0:T(8,128)(2,1)}, u32[]{:S(2)}, u32[]{:S(2)}) collective-permute-start(bf16[4,2,288,256]{3,2,1,0:T(8,128)(2,1)} %get-tuple-element.97), channel_id=1, source_target_pairs={{0,1},{1,0},{2,3},{3,2},{4,5},{5,4},{6,7},{7,6},{8,9},{9,8},{10,11... | collective-permute-start | bytes 3538952 | tf_op jit(solution)/shard_map/ppermute | solution.py:362
  461.9 5.1 copy-start.1
  538.1 8.5 %copy-start.4 = (f32[64,512]{1,0:T(8,128)S(1)}, f32[64,512]{1,0:T(8,128)}, u32[]{:S(2)}) copy-start(f32[64,512]{1,0:T(8,128)} %get-tuple-element.149) | copy-start | bytes 393220
Sparse Core Ops, SparseCore 0:
  268.5 144.7 reduce-scatter.1
